TPU v7x, 32 devices: a whole 2x2x4 slice. The times are simulated.
32 devices in a mesh: mem: 8 (over z, y), reg: 4 (over x, core).
Axes of the slice: x: 2, y: 2, z: 4, core: 2. Of those that a mesh axis runs over, the one named last changes fastest.
Arguments:
- prior_members_field: bfloat16 [1024, 4, 8, 2048], P('mem', 'reg'), may hold values from -6 to 6
- measure_space_deviations: bfloat16 [1024, 4, 8, 1024], P('mem', 'reg'), may hold values from -12 to 12
- measured_minus_predicted: bfloat16 [4, 8, 1024], P('reg'), may hold values from -12 to 12
- measure_pool_indices: int32 [4, 8, 1024], P('reg'), may hold values from 0 to 5119
- active_measure_tally: int32 [4, 8], P('reg', 'mem'), may hold values from 256 to 1024, as said below
- tapered_error_weight: float32 [4, 8, 1024], P('reg', 'mem'), may hold values from 0.02 to 0.5
Outputs:
- analysis: bfloat16 [1024, 4, 8, 2048], P('mem', 'reg')
Inputs may be any that keep to these rules, and one draw needn't show every extreme that they name: `active_measure_tally`: some block has exactly 1024 live entries.
All inputs are finite; a program needn't handle non-finite values.
Results may differ from a plain program's by a relative error of at most 0.0089.
Values may be sent and summed in bfloat16 or wider, within the bound.
No kernel may reach another device: no remote copies, remote signals or barrier semaphores. Data moves between devices by JAX's collectives and lax.ppermute only.
A program may use at most 128 MiB of HBM per device.

v0:
```python
import jax
import jax.numpy as jnp
from jax import lax
from jax.sharding import PartitionSpec as P

ITERS = 2


def padded(cells, sides, width):
    for axis, dim in sides:
        count = lax.axis_size(axis)
        ends = count - 1
        head = lax.slice_in_dim(cells, 0, width, axis=dim)
        tail = lax.slice_in_dim(cells, cells.shape[dim] - width, cells.shape[dim], axis=dim)
        cells = jnp.concatenate(
            [
                lax.ppermute(tail, axis, [(i, (i + 1) % count) for i in range(ends)]),
                cells,
                lax.ppermute(head, axis, [((i + 1) % count, i) for i in range(ends)]),
            ],
            axis=dim,
        )
    return cells


def ensemble_transform(obs_rows, innov_row, obs_weight):
    count_k = obs_rows.shape[0]
    identity = jnp.eye(count_k, dtype=jnp.float32)
    weighted = (obs_rows.astype(jnp.float32) * obs_weight[None, :]).astype(jnp.bfloat16)
    precision_mat = lax.dot_general(
        weighted, obs_rows, (((1,), (1,)), ((), ())), preferred_element_type=jnp.float32
    )
    precision_mat = precision_mat + (count_k - 1.0) * identity
    trace_mean = jnp.trace(precision_mat) / count_k
    root_iter = (precision_mat / trace_mean).astype(jnp.bfloat16)
    inverse_iter = identity.astype(jnp.bfloat16)
    for repeat in range(ITERS):
        product = jnp.dot(inverse_iter, root_iter, preferred_element_type=jnp.float32)
        newton_step = (1.5 * identity - 0.5 * product).astype(jnp.bfloat16)
        if repeat + 1 < ITERS:
            root_iter = jnp.dot(root_iter, newton_step, preferred_element_type=jnp.float32).astype(
                jnp.bfloat16
            )
        inverse_iter = jnp.dot(
            newton_step, inverse_iter, preferred_element_type=jnp.float32
        ).astype(jnp.bfloat16)
    gain_vector = jnp.dot(weighted, innov_row, preferred_element_type=jnp.float32)
    inv_root = inverse_iter.astype(jnp.float32)
    inner = jnp.dot(inv_root, gain_vector, precision=lax.Precision.HIGHEST)
    mean_weight = jnp.dot(inv_root, inner, precision=lax.Precision.HIGHEST) / trace_mean
    spread_factor = jnp.sqrt((count_k - 1.0) / trace_mean)
    return (spread_factor * inv_root + mean_weight[:, None]).astype(jnp.bfloat16)


def body(
    prior_members_field,
    measure_space_deviations,
    measured_minus_predicted,
    measure_pool_indices,
    active_measure_tally,
    tapered_error_weight,
):
    meridian_coordinate = lax.axis_index("mem")
    use_count = measure_pool_indices.shape[2]
    blocks = lax.all_to_all(
        measure_space_deviations, "mem", split_axis=2, concat_axis=0, tiled=True
    )
    innov_own = lax.dynamic_slice_in_dim(measured_minus_predicted, meridian_coordinate, 1, 1)
    obs_pool = jnp.concatenate([blocks, innov_own[None]], axis=0)
    extended = padded(obs_pool, (("reg", 1), ("mem", 2)), 1)
    neighbours = jnp.concatenate(
        [
            extended[:, 1, 1],
            extended[:, 0, 1],
            extended[:, 2, 1],
            extended[:, 1, 0],
            extended[:, 1, 2],
        ],
        axis=1,
    )
    use_list = lax.dynamic_slice_in_dim(measure_pool_indices[0], meridian_coordinate, 1, 0)[0]
    chosen = jnp.take(neighbours, use_list, axis=1)
    slots = jnp.arange(use_count, dtype=jnp.int32)
    obs_weight = jnp.where(slots < active_measure_tally[0, 0], tapered_error_weight[0, 0], 0.0)
    transform = ensemble_transform(chosen[:-1], chosen[-1], obs_weight)
    tile_model_entries = lax.all_to_all(
        prior_members_field, "mem", split_axis=2, concat_axis=0, tiled=True
    )[:, 0, 0]
    state_mean = jnp.mean(tile_model_entries.astype(jnp.float32), axis=0)
    perturb = (tile_model_entries.astype(jnp.float32) - state_mean[None, :]).astype(jnp.bfloat16)
    increment = lax.dot_general(
        transform, perturb, (((0,), (0,)), ((), ())), preferred_element_type=jnp.float32
    )
    analysis_block = (state_mean[None, :] + increment).astype(jnp.bfloat16)
    return lax.all_to_all(
        analysis_block[:, None, None], "mem", split_axis=0, concat_axis=2, tiled=True
    )


def solution(mesh):
    in_specs = (
        P("mem", "reg", None, None),
        P("mem", "reg", None, None),
        P("reg", None, None),
        P("reg", None, None),
        P("reg", "mem"),
        P("reg", "mem", None),
    )
    out_specs = P("mem", "reg", None, None)
    return jax.shard_map(body, mesh=mesh, in_specs=in_specs, out_specs=out_specs, check_vma=False)
```

profile of v0, /device:TPU:9, one launch (start us, length us, event | category | flops | bytes accessed | tf_op | source)
XLA Modules:
  0.0 616.0 jit_solution(17020815709286022246)
XLA Ops:
  0.0 0.0 copy-start
  0.0 4.1 copy.51
  4.1 5.7 all-to-all-start.1
  9.8 0.2 copy.54
  10.0 46.3 %all-to-all-done.1 = bf16[128,1,8,1024]{3,0,1,2:T(8,128)(2,1)S(1)} async-done(((bf16[128,1,8,1024]{3,0,1,2:T(8,128)(2,1)}), bf16[128,1,8,1024]{3,0,1,2:T(8,128)(2,1)S(1)}, u32[]{:S(2)}, u32[]{:S(2)}) %all-to-all-start.1) | async-done | bytes 2097184 | tf_op jit(solution)/shard_map/all_to_all | solution.py:65
  56.3 2.5 copy.74
  58.8 4.5 copy.53
  63.3 2.8 all_to_all.37
  66.1 1.6 pad_maximum_fusion.1
  67.7 4.2 copy.55
  71.9 3.5 collective-permute-start
  75.4 2.1 collective-permute-start.1
  77.6 6.5 %copy.49 = bf16[128,1,8,2048]{3,0,1,2:T(8,128)(2,1)} copy(bf16[128,1,8,2048]{3,2,1,0:T(8,128)(2,1)} %param.6) | data formatting | bytes 8388608 | tf_op args[0]
  84.1 6.4 %all-to-all-start = ((bf16[128,1,8,2048]{3,0,1,2:T(8,128)(2,1)}), bf16[128,1,8,2048]{3,0,1,2:T(8,128)(2,1)}, u32[]{:S(2)}, u32[]{:S(2)}) async-start(bf16[128,1,8,2048]{3,0,1,2:T(8,128)(2,1)} %copy.49), calls=%async_computation | async-start | bytes 8388608 | tf_op jit(solution)/shard_map/all_to_all | solution.py:86
  90.4 8.4 %collective-permute-done = bf16[1025,1,1,1024]{3,0,2,1:T(8,128)(2,1)} collective-permute-done((bf16[1025,1,1,1024]{3,0,2,1:T(8,128)(2,1)}, bf16[1025,1,1,1024]{3,0,2,1:T(8,128)(2,1)}, u32[]{:S(2)}, u32[]{:S(2)}) %collective-permute-start) | collective-permute-done | bytes 2099232 | tf_op jit(solution)/shard_map/ppermute | solution.py:17
  98.8 4.0 copy.56
  102.9 0.7 collective-permute-done.1
  103.5 4.1 copy.58
  107.6 5.7 pad_maximum_fusion
  113.3 9.7 %copy.61 = bf16[1025,3,1,1024]{3,0,2,1:T(8,128)(2,1)} copy(bf16[1025,3,1,1024]{0,3,2,1:T(8,128)(2,1)} %pad_maximum_fusion) | data formatting | bytes 12595200 | tf_op jit(solution)/shard_map/concatenate | solution.py:15
  123.0 2.4 collective-permute-start.2
  125.5 5.1 collective-permute-start.3
  131.2 0.8 compare_select_fusion
  132.0 0.0 copy-done.7
  132.0 1.6 bitcast_dynamic-update-slice_fusion.4
  133.7 1.6 bitcast_dynamic-update-slice_fusion.3
  135.2 0.0 copy-done.3
  135.2 1.6 bitcast_dynamic-update-slice_fusion.2
  136.9 45.3 %all-to-all-done = bf16[128,1,8,2048]{3,0,1,2:T(8,128)(2,1)} async-done(((bf16[128,1,8,2048]{3,0,1,2:T(8,128)(2,1)}), bf16[128,1,8,2048]{3,0,1,2:T(8,128)(2,1)}, u32[]{:S(2)}, u32[]{:S(2)}) %all-to-all-start) | async-done | bytes 4194336 | tf_op jit(solution)/shard_map/all_to_all | solution.py:86
  182.2 4.6 convert_bitcast_fusion
  186.8 4.9 copy.65
  191.7 4.4 convert_reduce_fusion
  196.0 3.3 fusion
  199.3 208.1 %collective-permute-done.2 = bf16[1025,3,1,1024]{3,0,2,1:T(8,128)(2,1)} collective-permute-done((bf16[1025,3,1,1024]{3,0,2,1:T(8,128)(2,1)}, bf16[1025,3,1,1024]{3,0,2,1:T(8,128)(2,1)}, u32[]{:S(2)}, u32[]{:S(2)}) %collective-permute-start.2) | collective-permute-done | bytes 6297632 | tf_op jit(solution)/shard_map/ppermute | solution.py:17
  407.4 3.1 slice.18
  410.5 2.9 copy.69
  413.4 2.6 collective-permute-done.3
  416.1 3.1 slice.19
  419.2 4.0 copy.70
  423.2 1.6 bitcast_dynamic-update-slice_fusion.1
  424.9 0.9 copy-done.4
  425.7 1.6 bitcast_dynamic-update-slice_fusion
  427.3 11.5 %gather_fusion = bf16[1024,1025]{1,0:T(8,128)(2,1)S(1)} fusion(bf16[1025,5120]{0,1:T(8,128)(2,1)} %bitcast_dynamic-update-slice_fusion, s32[1024]{0:T(1024)S(1)} %broadcast_clamp_fusion), kind=kCustom, calls=%fused_computation | custom fusion | bytes 4202496 | tf_op jit(solution)/shard_map/jit(_take)/gather | solution.py:82
  438.9 0.3 select_bitcast_fusion
  439.2 0.2 slice_reduce_fusion
  439.4 5.2 select_reduce_fusion
  445.2 2.8 divide_convert_fusion
  448.0 2.3 fusion.1
  450.4 1.3 copy-done.8
  451.7 3.7 fusion.13
  455.3 8.1 %fusion.2 = bf16[1024,1024]{1,0:T(8,128)(2,1)} fusion(bf16[1024,1024]{1,0:T(8,128)(2,1)} %fusion.13, bf16[1024,1024]{1,0:T(8,128)(2,1)S(1)} %divide_convert_fusion, bf16[1024,1024]{1,0:T(8,128)(2,1)} %copy-done.8), kind=kOutput, calls=%fused_computation.10 | convolution fusion | flops 4301258752 | bytes 8388608 | tf_op jit(solution)/shard_map/dot_general | solution.py:38
  463.4 4.7 convolution_convert_fusion
  468.1 0.5 fusion.16
  468.7 1.9 convolution_bitcast_fusion
  470.6 1.7 fusion.20
  472.5 8.6 %fusion.3 = bf16[1024,1,1,2048]{3,0,2,1:T(8,128)(2,1)} fusion(f32[2048]{0:T(1024)S(1)} %broadcast_multiply_fusion, bf16[1024,2048]{1,0:T(8,128)(2,1)} %fusion, bf16[1024,1024]{1,0:T(8,128)(2,1)S(1)} %convolution_convert_fusion, f32[1024]{0:T(1024)S(1)} %broadcast_divide_fusion, f32[]{:T(128)S(6)} %sqrt.3), kind=kOutput, calls=%fused_computation.11 | convolution fusion | flops 4303355904 | bytes 10498052 | tf_op jit(solution)/shard_map/dot_general | solution.py:91
  481.1 0.5 broadcast.69
  481.6 6.8 %reduce.5 = bf16[1024,2048]{1,0:T(8,128)(2,1)} reduce(bf16[1024,1,1,2048]{3,0,2,1:T(8,128)(2,1)} %fusion.3, bf16[]{:T(256)} %broadcast.69), dimensions={1,2}, to_apply=%copy.66.reduce_sub_computation | reduce | bytes 8388610 | tf_op jit(solution)/shard_map/broadcast_in_dim | solution.py:96
  488.4 7.8 %reshape.73 = bf16[8,2,131072]{2,1,0:T(2,128)(2,1)} reshape(bf16[1024,2048]{1,0:T(8,128)(2,1)} %reduce.5) | data formatting | bytes 8388608
  496.2 100.5 %all_to_all.45 = bf16[8,2,131072]{2,1,0:T(2,128)(2,1)} all-to-all(bf16[8,2,131072]{2,1,0:T(2,128)(2,1)} %reshape.73), channel_id=1, replica_groups=mesh['mem'=8,'reg'=4] {'mem'}, dimensions={0} | all-to-all | bytes 8388608 | tf_op jit(solution)/shard_map/all_to_all | solution.py:95
  596.7 8.8 %reshape.74 = bf16[1024,1,1,2048]{3,2,1,0:T(2,128)(2,1)} reshape(bf16[8,2,131072]{2,1,0:T(2,128)(2,1)} %all_to_all.45) | data formatting | bytes 8388608
  605.4 6.0 copy.68
  611.5 0.0 copy-start.1
  611.5 4.3 copy.67
  (19 shorter events, 0.1 us)
Async XLA Ops:
  0.0 9.8 %copy-start = (bf16[1,8,1024]{2,1,0:T(8,128)(2,1)S(1)}, bf16[1,8,1024]{2,1,0:T(8,128)(2,1)}, u32[]{:S(2)}) copy-start(bf16[1,8,1024]{2,1,0:T(8,128)(2,1)} %param.8) | copy-start | bytes 49156
  4.1 52.2 %all-to-all-start.1 = ((bf16[128,1,8,1024]{3,0,1,2:T(8,128)(2,1)}), bf16[128,1,8,1024]{3,0,1,2:T(8,128)(2,1)S(1)}, u32[]{:S(2)}, u32[]{:S(2)}) async-start(bf16[128,1,8,1024]{3,0,1,2:T(8,128)(2,1)} %copy.51), calls=%async_computation.1 | async-start | bytes 4194304 | tf_op jit(solution)/shard_map/all_to_all | solution.py:65
  71.9 26.9 %collective-permute-start = (bf16[1025,1,1,1024]{3,0,2,1:T(8,128)(2,1)}, bf16[1025,1,1,1024]{3,0,2,1:T(8,128)(2,1)}, u32[]{:S(2)}, u32[]{:S(2)}) collective-permute-start(bf16[1025,1,1,1024]{3,0,2,1:T(8,128)(2,1)} %copy.55), channel_id=1, source_target_pairs={{0,1},{1,2},{2,3},{4,5},{5,6},{6,7},{8,9},{9,10},{10,11},{12,13},{... | collective-permute-start | bytes 6297608 | tf_op jit(solution)/shard_map/ppermute | solution.py:17
  75.4 28.1 %collective-permute-start.1 = (bf16[1025,1,1,1024]{3,0,2,1:T(8,128)(2,1)}, bf16[1025,1,1,1024]{3,0,2,1:T(8,128)(2,1)}, u32[]{:S(2)}, u32[]{:S(2)}) collective-permute-start(bf16[1025,1,1,1024]{3,0,2,1:T(8,128)(2,1)} %copy.55), channel_id=1, source_target_pairs={{1,0},{2,1},{3,2},{5,4},{6,5},{7,6},{9,8},{10,9},{11,10},{13,12},{... | collective-permute-start | bytes 6297608 | tf_op jit(solution)/shard_map/ppermute | solution.py:19
  84.1 98.1 %all-to-all-start = ((bf16[128,1,8,2048]{3,0,1,2:T(8,128)(2,1)}), bf16[128,1,8,2048]{3,0,1,2:T(8,128)(2,1)}, u32[]{:S(2)}, u32[]{:S(2)}) async-start(bf16[128,1,8,2048]{3,0,1,2:T(8,128)(2,1)} %copy.49), calls=%async_computation | async-start | bytes 8388608 | tf_op jit(solution)/shard_map/all_to_all | solution.py:86
  113.3 18.7 %copy-start.7 = (f32[1,1,1024]{2,1,0:T(1,128)S(1)}, f32[1,1,1024]{2,1,0:T(1,128)}, u32[]{:S(2)}) copy-start(f32[1,1,1024]{2,1,0:T(1,128)} %param.11) | copy-start | bytes 12292
  123.0 10.6 %copy-start.2 = (bf16[1025,1,1,1024]{0,3,2,1:T(8,128)(2,1)S(1)}, bf16[1025,1,1,1024]{0,3,2,1:T(8,128)(2,1)}, u32[]{:S(2)}) copy-start(bf16[1025,1,1,1024]{0,3,2,1:T(8,128)(2,1)} %copy.56) | copy-start | bytes 6297604
  123.0 284.4 %collective-permute-start.2 = (bf16[1025,3,1,1024]{3,0,2,1:T(8,128)(2,1)}, bf16[1025,3,1,1024]{3,0,2,1:T(8,128)(2,1)}, u32[]{:S(2)}, u32[]{:S(2)}) collective-permute-start(bf16[1025,3,1,1024]{3,0,2,1:T(8,128)(2,1)} %copy.61), channel_id=1, source_target_pairs={{0,4},{4,8},{8,12},{12,16},{16,20},{20,24},{24,28},{1,5},{5,9},{9,... | collective-permute-start | bytes 18892808 | tf_op jit(solution)/shard_map/ppermute | solution.py:17
  125.5 290.6 %collective-permute-start.3 = (bf16[1025,3,1,1024]{3,0,2,1:T(8,128)(2,1)}, bf16[1025,3,1,1024]{3,0,2,1:T(8,128)(2,1)}, u32[]{:S(2)}, u32[]{:S(2)}) collective-permute-start(bf16[1025,3,1,1024]{3,0,2,1:T(8,128)(2,1)} %copy.61), channel_id=1, source_target_pairs={{4,0},{8,4},{12,8},{16,12},{20,16},{24,20},{28,24},{5,1},{9,5},{13... | collective-permute-start | bytes 18892808 | tf_op jit(solution)/shard_map/ppermute | solution.py:19
  132.0 3.2 copy-start.3
  423.2 2.5 copy-start.4
  439.2 5.3 copy-start.5
  450.3 1.3 copy-start.8
  463.4 4.7 copy-start.6
  611.5 4.3 copy-start.1
where the time goes:
time: 627 us; the launch traced here: 616 us
  waiting for transfers between devices  311 us (50%)
  local copies, waits for them, and re-layouts  108 us (17%)
  blocking collectives  100 us (16%)
  matrix products  36.8 us (6%)
  other arithmetic  31.9 us (5%)
  starting transfers between devices  25.2 us (4%)
    ppermute x2, waiting for transfers between devices, padded(): lax.ppermute(tail, axis, [(i, (i + 1) % count) for i in range(ends)])  217 us
    all_to_all x1, blocking collectives, body(): lax.all_to_all(analysis_block[:, None, None], 'mem', split_axis=0, concat...  100 us
    unnamed x28, local copies, waits for them, and re-layouts  47.2 us
    all_to_all x1, waiting for transfers between devices, body(): lax.all_to_all(measure_space_deviations, 'mem', split_axis=2, concat_axis...  46.3 us
    all_to_all x1, waiting for transfers between devices, body(): lax.all_to_all(prior_members_field, 'mem', split_axis=2, concat_axis=0, t...  45.3 us
  transfers between devices with their start and end apart: 6, of which 6 were waited for; matrix products, arithmetic and copies ran while one was open for 10% of the time, Pallas kernels for 0%

commit v1 on v0

v1 whole, which is shorter than its diff:
```python
import functools

import jax
import jax.numpy as jnp
from jax import lax
from jax.experimental import pallas as pl
from jax.experimental.pallas import tpu as pltpu
from jax.sharding import PartitionSpec as P

ITERS = 2
INNOV_ROWS = 16
SLOT_CHUNK = 256
MIB = 1024 * 1024


def gather_kernel(own_ref, up_ref, down_ref, inn_own, inn_up, inn_down, idx_ref, out_ref, inn_ref):
    block = pl.program_id(0)
    blocks = own_ref.shape[0]
    depth = own_ref.shape[2]
    members = own_ref.shape[1]
    west = jnp.maximum(block - 1, 0)
    east = jnp.minimum(block + 1, blocks - 1)
    slots = out_ref.shape[2]
    sources = (
        (own_ref, inn_own, block, None),
        (up_ref, inn_up, block, None),
        (down_ref, inn_down, block, None),
        (own_ref, inn_own, west, block > 0),
        (own_ref, inn_own, east, block < blocks - 1),
    )
    rows = lax.broadcasted_iota(jnp.int32, (depth, SLOT_CHUNK), 0)

    @pl.loop(0, slots // SLOT_CHUNK)
    def _(chunk):
        where = pl.ds(pl.multiple_of(chunk * SLOT_CHUNK, SLOT_CHUNK), SLOT_CHUNK)
        picks = idx_ref[pl.ds(block, 1), where]
        acc = jnp.zeros((members + INNOV_ROWS, SLOT_CHUNK), jnp.float32)
        for number, (ref, inn, at, live) in enumerate(sources):
            local = picks - number * depth
            if live is not None:
                local = jnp.where(live, local, -1)
            one_hot = jnp.where(rows == local, 1.0, 0.0).astype(jnp.bfloat16)
            lhs = jnp.concatenate([ref[at], inn[at]], axis=0)
            acc += jnp.dot(lhs, one_hot, preferred_element_type=jnp.float32)
        out_ref[0, :, where] = acc[:members].astype(jnp.bfloat16)
        inn_ref[0, :, where] = acc[members:].astype(jnp.bfloat16)


def gather_chosen(own, up, down, inn_own, inn_up, inn_down, picks):
    blocks, members, depth = own.shape
    slots = picks.shape[1]
    vmem = pl.BlockSpec(memory_space=pltpu.VMEM)
    return pl.pallas_call(
        gather_kernel,
        grid=(blocks,),
        in_specs=[vmem] * 7,
        out_specs=[
            pl.BlockSpec((1, members, slots), lambda b: (b, 0, 0)),
            pl.BlockSpec((1, INNOV_ROWS, slots), lambda b: (b, 0, 0)),
        ],
        out_shape=[
            jax.ShapeDtypeStruct((blocks, members, slots), jnp.bfloat16),
            jax.ShapeDtypeStruct((blocks, INNOV_ROWS, slots), jnp.bfloat16),
        ],
        compiler_params=pltpu.CompilerParams(vmem_limit_bytes=40 * MIB),
        cost_estimate=pl.CostEstimate(
            flops=2 * blocks * members * depth * 5 * slots,
            bytes_accessed=2 * blocks * members * (3 * depth + slots),
            transcendentals=0,
        ),
        name="gather_chosen",
    )(own, up, down, inn_own, inn_up, inn_down, picks)


def ensemble_transform(obs_rows, innov_row, obs_weight):
    count_k = obs_rows.shape[0]
    identity = jnp.eye(count_k, dtype=jnp.float32)
    weighted = (obs_rows.astype(jnp.float32) * obs_weight[None, :]).astype(jnp.bfloat16)
    precision_mat = lax.dot_general(
        weighted, obs_rows, (((1,), (1,)), ((), ())), preferred_element_type=jnp.float32
    )
    precision_mat = precision_mat + (count_k - 1.0) * identity
    trace_mean = jnp.trace(precision_mat) / count_k
    root_iter = (precision_mat / trace_mean).astype(jnp.bfloat16)
    inverse_iter = identity.astype(jnp.bfloat16)
    for repeat in range(ITERS):
        product = jnp.dot(inverse_iter, root_iter, preferred_element_type=jnp.float32)
        newton_step = (1.5 * identity - 0.5 * product).astype(jnp.bfloat16)
        if repeat + 1 < ITERS:
            root_iter = jnp.dot(root_iter, newton_step, preferred_element_type=jnp.float32).astype(
                jnp.bfloat16
            )
        inverse_iter = jnp.dot(
            newton_step, inverse_iter, preferred_element_type=jnp.float32
        ).astype(jnp.bfloat16)
    gain_vector = jnp.dot(weighted, innov_row, preferred_element_type=jnp.float32)
    inv_root = inverse_iter.astype(jnp.float32)
    inner = jnp.dot(inv_root, gain_vector, precision=lax.Precision.HIGHEST)
    mean_weight = jnp.dot(inv_root, inner, precision=lax.Precision.HIGHEST) / trace_mean
    spread_factor = jnp.sqrt((count_k - 1.0) / trace_mean)
    return (spread_factor * inv_root + mean_weight[:, None]).astype(jnp.bfloat16)


def body(
    prior_members_field,
    measure_space_deviations,
    measured_minus_predicted,
    measure_pool_indices,
    active_measure_tally,
    tapered_error_weight,
):
    place = lax.axis_index("mem")
    strips = lax.axis_size("reg")
    blocks = prior_members_field.shape[2]
    entries = prior_members_field.shape[3]
    use_count = measure_pool_indices.shape[2]
    to_next = [(i, i + 1) for i in range(strips - 1)]
    to_last = [(i + 1, i) for i in range(strips - 1)]

    def exchange(x):
        return lax.all_to_all(x, "mem", split_axis=0, concat_axis=0, tiled=True)

    obs = jnp.swapaxes(measure_space_deviations[:, 0], 0, 1)
    up = lax.ppermute(obs, "reg", to_next)
    down = lax.ppermute(obs, "reg", to_last)
    innov = measured_minus_predicted[0]
    innov_up = lax.ppermute(innov, "reg", to_next)
    innov_down = lax.ppermute(innov, "reg", to_last)

    def spread(row):
        return jnp.broadcast_to(row[:, None, :], (blocks, INNOV_ROWS, row.shape[1]))

    first = entries * 5 // 8
    state = prior_members_field[:, 0]
    state_a = exchange(jnp.swapaxes(state[:, :, :first], 0, 1))
    chosen, chosen_innov = gather_chosen(
        obs, up, down, spread(innov), spread(innov_up), spread(innov_down), measure_pool_indices[0]
    )
    state_b = jnp.swapaxes(state[:, :, first:], 0, 1)
    obs_rows = exchange(chosen)
    obs_rows, state_b = lax.optimization_barrier((obs_rows, state_b))
    state_b = exchange(state_b)
    innov_row = lax.dynamic_index_in_dim(chosen_innov[:, 0], place, 0, keepdims=False)
    obs_rows = obs_rows.reshape(-1, use_count)
    slots = jnp.arange(use_count, dtype=jnp.int32)
    obs_weight = jnp.where(slots < active_measure_tally[0, 0], tapered_error_weight[0, 0], 0.0)
    transform = ensemble_transform(obs_rows, innov_row, obs_weight)

    def analysed(part):
        shape = part.shape
        part = part.reshape(-1, shape[2]).astype(jnp.float32)
        state_mean = jnp.mean(part, axis=0)
        perturb = (part - state_mean[None, :]).astype(jnp.bfloat16)
        increment = lax.dot_general(
            transform, perturb, (((0,), (0,)), ((), ())), preferred_element_type=jnp.float32
        )
        return (state_mean[None, :] + increment).astype(jnp.bfloat16).reshape(shape)

    half = first // 2
    rest = entries - first
    parts = [
        exchange(analysed(state_a[:, :, :half])),
        exchange(analysed(state_a[:, :, half:])),
        exchange(analysed(state_b)),
    ]
    parts = [jnp.swapaxes(part, 0, 1) for part in parts]
    return jnp.concatenate(parts, axis=2)[:, None]


def solution(mesh):
    in_specs = (
        P("mem", "reg", None, None),
        P("mem", "reg", None, None),
        P("reg", None, None),
        P("reg", None, None),
        P("reg", "mem"),
        P("reg", "mem", None),
    )
    out_specs = P("mem", "reg", None, None)
    return jax.shard_map(body, mesh=mesh, in_specs=in_specs, out_specs=out_specs, check_vma=False)
```

time: 627 us -> 324 us (0.52); the launches traced: 616 us -> 320 us
  waiting for transfers between devices: 311 us -> 118 us
  local copies, waits for them, and re-layouts: 108 us -> 20.4 us
  blocking collectives: 100 us -> 76.9 us
  other arithmetic: 31.9 us -> 9.85 us
  Pallas kernels: 0 us -> 20.3 us
  starting transfers between devices: 25.2 us -> 34.4 us
    ppermute x4, waiting for transfers between devices: 220 us -> 17.5 us  [the longest x1 16.7 us: body(): innov_down = lax.ppermute(innov, 'reg', to_last)]
    unnamed x28 -> x18, local copies, waits for them, and re-layouts: 47.2 us -> 11.6 us
    all_to_all x1 -> x2, blocking collectives: 100 us -> 76.9 us  [exchange(): return lax.all_to_all(x, 'mem', split_axis=0, concat_axis=0, tiled=True)]
    pallas_call x0 -> x1, Pallas kernels: none -> 20.3 us  [gather_chosen(): pl.pallas_call(gather_kernel, grid=(blocks,), in_specs=[vmem] * 7, out_sp...]
    concatenate x3 -> x0, local copies, waits for them, and re-layouts: 15.5 us -> none  [the longest x1 9.73 us: padded(): jnp.concatenate([lax.ppermute(tail, axis, [(i, (i + 1) % count) for i in...]
    all_to_all x4 -> x0, local copies, waits for them, and re-layouts: 14.1 us -> none  [the longest x3 9.78 us: body(): lax.all_to_all(measure_space_deviations, 'mem', split_axis=2, concat_axis...]
    gather x1 -> x0, local copies, waits for them, and re-layouts: 11.5 us -> none  [body(): chosen = jnp.take(neighbours, use_list, axis=1)]
    all_to_all x2 -> x4, starting transfers between devices: 12.1 us -> 22.7 us  [exchange(): return lax.all_to_all(x, 'mem', split_axis=0, concat_axis=0, tiled=True)]
  transfers between devices with their start and end apart: 6 -> 8, of which waited for: 6 -> 6; matrix products, arithmetic and copies ran while one was open for 10% -> 5% of each run, Pallas kernels for 0% -> 6%
where the time goes in v1:
time: 324 us; the launch traced here: 320 us
  waiting for transfers between devices  118 us (36%)
  blocking collectives  76.9 us (24%)
  matrix products  39.2 us (12%)
  starting transfers between devices  34.4 us (11%)
  local copies, waits for them, and re-layouts  20.4 us (6%)
  Pallas kernels  20.3 us (6%)
  other arithmetic  9.85 us (3%)
    all_to_all x4, waiting for transfers between devices, exchange(): return lax.all_to_all(x, 'mem', split_axis=0, concat_axis=0, tiled=True)  100 us
    all_to_all x2, blocking collectives, exchange(): return lax.all_to_all(x, 'mem', split_axis=0, concat_axis=0, tiled=True)  76.9 us
    all_to_all x4, starting transfers between devices, exchange(): return lax.all_to_all(x, 'mem', split_axis=0, concat_axis=0, tiled=True)  22.7 us
    pallas_call x1, Pallas kernels, gather_chosen(): pl.pallas_call(gather_kernel, grid=(blocks,), in_specs=[vmem] * 7, out_sp...  20.3 us
    ppermute x1, waiting for transfers between devices, body(): innov_down = lax.ppermute(innov, 'reg', to_last)  16.7 us
    unnamed x18, local copies, waits for them, and re-layouts  11.6 us
    dot_general x2, matrix products, ensemble_transform(): jnp.dot(inverse_iter, root_iter, preferred_element_type=jnp.float32)  11 us
    dot_general x3, matrix products, analysed(): lax.dot_general(transform, perturb, (((0,), (0,)), ((), ())), preferred_e...  9.05 us
  transfers between devices with their start and end apart: 8, of which 6 were waited for; matrix products, arithmetic and copies ran while one was open for 5% of the time, Pallas kernels for 6%

profile of v1, /device:TPU:9, one launch (start us, length us, event | category | flops | bytes accessed | tf_op | source)
XLA Modules:
  0.0 320.3 jit_solution(9095348751244858096)
XLA Ops:
  0.0 4.5 %copy.19 = bf16[128,1,8,2048]{3,0,2,1:T(8,128)(2,1)S(1)} copy(bf16[128,1,8,2048]{3,2,1,0:T(8,128)(2,1)} %param.6) | data formatting | bytes 8388608 | tf_op args[0]
  4.5 0.0 copy-start.1
  4.5 2.0 copy-done.1
  6.5 1.8 slice_bitcast_fusion
  8.3 5.7 %all-to-all-start = ((bf16[8,128,1280]{2,1,0:T(8,128)(2,1)}), bf16[8,128,1280]{2,1,0:T(8,128)(2,1)S(1)}, u32[]{:S(2)}, u32[]{:S(2)}) async-start(bf16[8,128,1280]{2,1,0:T(8,128)(2,1)} %slice_bitcast_fusion), calls=%async_computation | async-start | bytes 5242880 | tf_op jit(solution)/shard_map/all_to_all | solution.py:121
  14.0 0.0 copy-start.5
  14.0 0.0 copy-start
  14.0 2.8 copy.20
  16.8 3.1 collective-permute-start.1
  19.9 3.0 collective-permute-start
  22.9 0.0 copy-done.5
  22.9 1.9 collective-permute-start.3
  24.9 3.6 %collective-permute-start.2 = (bf16[8,1024]{1,0:T(8,128)(2,1)S(1)}, bf16[8,1024]{1,0:T(8,128)(2,1)S(1)}, u32[]{:S(2)}, u32[]{:S(2)}) collective-permute-start(bf16[8,1024]{1,0:T(8,128)(2,1)S(1)} %bitcast.81), channel_id=1, source_target_pairs={{0,1},{1,2},{2,3},{4,5},{5,6},{6,7},{8,9},{9,10},{10,11},{12,13},{... | collective-permute-start | bytes 49160 | tf_op jit(solution)/shard_map/ppermute | solution.py:127
  28.5 16.7 %collective-permute-done.3 = bf16[8,1024]{1,0:T(8,128)(2,1)S(1)} collective-permute-done((bf16[8,1024]{1,0:T(8,128)(2,1)S(1)}, bf16[8,1024]{1,0:T(8,128)(2,1)S(1)}, u32[]{:S(2)}, u32[]{:S(2)}) %collective-permute-start.3) | collective-permute-done | bytes 16416 | tf_op jit(solution)/shard_map/ppermute | solution.py:128
  45.2 0.9 collective-permute-done.2
  46.1 0.0 collective-permute-done.1.down_ref
  46.1 0.0 collective-permute-done.up_ref
  46.2 0.0 copy-done
  46.2 20.3 %gather_chosen.1 = (bf16[8,128,1024]{2,1,0:T(8,128)(2,1)}, bf16[8,16,1024]{2,1,0:T(8,128)(2,1)S(1)}) custom-call(bf16[8,128,1024]{2,1,0:T(8,128)(2,1)S(1)} %bitcast.68, bf16[8,128,1024]{2,1,0:T(8,128)(2,1)S(1)} %collective-permute-done.up_ref, bf16[8,128,1024]{2,1,0:T(8,128)(2,1)S(1)} %collective-permute-done.1.down_ref, ...), custom_call_target="tpu_custom_call" | custom-call | flops 10737418240 | bytes 8388608 | tf_op jit(solution)/shard_map/gather_chosen/pallas_call | solution.py:53
  66.4 5.3 %all-to-all-done = bf16[8,128,1280]{2,1,0:T(8,128)(2,1)S(1)} async-done(((bf16[8,128,1280]{2,1,0:T(8,128)(2,1)}), bf16[8,128,1280]{2,1,0:T(8,128)(2,1)S(1)}, u32[]{:S(2)}, u32[]{:S(2)}) %all-to-all-start) | async-done | bytes 2621472 | tf_op jit(solution)/shard_map/all_to_all | solution.py:121
  71.8 0.0 copy-start.6
  71.8 5.7 %all-to-all-start.1 = ((bf16[8,128,1024]{2,1,0:T(8,128)(2,1)}), bf16[8,128,1024]{2,1,0:T(8,128)(2,1)}, u32[]{:S(2)}, u32[]{:S(2)}) async-start(bf16[8,128,1024]{2,1,0:T(8,128)(2,1)} %get-tuple-element.9), calls=%async_computation.1 | async-start | bytes 4194304 | tf_op jit(solution)/shard_map/all_to_all | solution.py:121
  78.1 0.0 copy-done.6
  78.1 2.7 slice_bitcast_fusion.1
  80.8 0.4 fusion.11
  81.2 0.6 slice_convert_fusion.1
  81.8 1.6 fusion.5
  83.4 40.5 %all-to-all-done.1 = bf16[8,128,1024]{2,1,0:T(8,128)(2,1)} async-done(((bf16[8,128,1024]{2,1,0:T(8,128)(2,1)}), bf16[8,128,1024]{2,1,0:T(8,128)(2,1)}, u32[]{:S(2)}, u32[]{:S(2)}) %all-to-all-start.1) | async-done | bytes 2097184 | tf_op jit(solution)/shard_map/all_to_all | solution.py:121
  123.8 2.2 multiply_convert_fusion
  126.0 6.6 %select_reduce_fusion = (f32[]{:T(128)}, f32[1024,1024]{1,0:T(8,128)}) fusion(bf16[1024,1024]{1,0:T(8,128)(2,1)S(1)} %bitcast.72, bf16[1024,1024]{1,0:T(8,128)(2,1)} %bitcast.11), kind=kOutput, calls=%fused_computation.9 | convolution fusion | flops 2152726528 | bytes 8388612 | tf_op jit(solution)/shard_map/dot_general | solution.py:79
  133.3 2.8 divide_convert_fusion
  136.1 0.0 copy-start.4
  136.1 2.3 fusion
  138.5 0.0 copy-done.4
  138.5 0.0 copy-start.7
  138.5 1.3 copy-done.7
  139.8 3.6 %fusion.8 = bf16[1024,1024]{1,0:T(8,128)(2,1)} fusion(bf16[1024,1024]{1,0:T(8,128)(2,1)S(1)} %fusion), kind=kOutput, calls=%fused_computation.27 | convolution fusion | flops 2151677952 | bytes 4194304 | tf_op jit(solution)/shard_map/dot_general | solution.py:93
  143.4 8.7 %fusion.1 = bf16[1024,1024]{1,0:T(8,128)(2,1)} fusion(bf16[1024,1024]{1,0:T(8,128)(2,1)} %fusion.8, bf16[1024,1024]{1,0:T(8,128)(2,1)} %copy-done.4, bf16[1024,1024]{1,0:T(8,128)(2,1)} %copy-done.7), kind=kOutput, calls=%fused_computation.3 | convolution fusion | flops 4301258752 | bytes 8388608 | tf_op jit(solution)/shard_map/dot_general | solution.py:87
  152.1 4.8 %convolution_convert_fusion = bf16[1024,1024]{1,0:T(8,128)(2,1)S(1)} fusion(bf16[1024,1024]{1,0:T(8,128)(2,1)} %fusion.1, bf16[1024,1024]{1,0:T(8,128)(2,1)} %fusion.8), kind=kOutput, calls=%fused_computation.28 | convolution fusion | flops 2148532224 | bytes 6291456 | tf_op jit(solution)/shard_map/dot_general | solution.py:93
  156.9 0.0 copy-start.2
  156.9 0.6 convolution_bitcast_fusion.1
  157.5 1.7 convolution_bitcast_fusion
  159.3 1.7 fusion.17
  161.0 0.0 copy-done.2
  161.0 2.0 add_convert_fusion.2
  163.0 35.1 %all_to_all.30 = bf16[8,128,640]{2,1,0:T(8,128)(2,1)S(1)} all-to-all(bf16[8,128,640]{2,1,0:T(8,128)(2,1)S(1)} %bitcast.78), channel_id=1, replica_groups=mesh['mem'=8,'reg'=4] {'mem'}, dimensions={0} | all-to-all | bytes 2621440 | tf_op jit(solution)/shard_map/all_to_all | solution.py:121
  198.1 5.0 %all-to-all-start.4 = ((bf16[8,128,768]{2,1,0:T(8,128)(2,1)}), bf16[8,128,768]{2,1,0:T(8,128)(2,1)S(1)}, u32[]{:S(2)}, u32[]{:S(2)}) async-start(bf16[8,128,768]{2,1,0:T(8,128)(2,1)} %slice_bitcast_fusion.1), calls=%async_computation.4 | async-start | bytes 3145728 | tf_op jit(solution)/shard_map/all_to_all | solution.py:121
  203.2 5.0 %add_convert_fusion.3 = bf16[1024,640]{1,0:T(8,128)(2,1)} fusion(bf16[1024,640]{1,0:T(8,128)(2,1)} %get-tuple-element.20, f32[640]{0:T(1024)S(1)} %broadcast_multiply_fusion.2, bf16[1024,1024]{1,0:T(8,128)(2,1)} %copy-done.2, f32[1024]{0:T(1024)S(1)} %broadcast_divide_fusion, f32[]{:T(128)S(6)} %sqrt.3), kind=kOutput, calls=%fused_computation.24 | convolution fusion | flops 1347682304 | bytes 4725252 | tf_op jit(solution)/shard_map/dot_general | solution.py:154
  208.1 29.6 %all-to-all-done.4 = bf16[8,128,768]{2,1,0:T(8,128)(2,1)S(1)} async-done(((bf16[8,128,768]{2,1,0:T(8,128)(2,1)}), bf16[8,128,768]{2,1,0:T(8,128)(2,1)S(1)}, u32[]{:S(2)}, u32[]{:S(2)}) %all-to-all-start.4) | async-done | bytes 1572896 | tf_op jit(solution)/shard_map/all_to_all | solution.py:121
  237.7 6.3 %all-to-all-start.2 = ((bf16[8,128,640]{2,1,0:T(8,128)(2,1)}), bf16[8,128,640]{2,1,0:T(8,128)(2,1)}, u32[]{:S(2)}, u32[]{:S(2)}) async-start(bf16[8,128,640]{2,1,0:T(8,128)(2,1)} %bitcast.77), calls=%async_computation.2 | async-start | bytes 2621440 | tf_op jit(solution)/shard_map/all_to_all | solution.py:121
  244.0 0.0 copy-start.3
  244.0 0.3 convert_reduce_fusion
  244.3 0.3 fusion.2
  244.6 1.0 copy-done.3
  245.6 2.1 add_convert_fusion.1
  247.7 24.8 %all-to-all-done.2 = bf16[8,128,640]{2,1,0:T(8,128)(2,1)} async-done(((bf16[8,128,640]{2,1,0:T(8,128)(2,1)}), bf16[8,128,640]{2,1,0:T(8,128)(2,1)}, u32[]{:S(2)}, u32[]{:S(2)}) %all-to-all-start.2) | async-done | bytes 1310752 | tf_op jit(solution)/shard_map/all_to_all | solution.py:121
  272.5 41.7 %all_to_all.31 = bf16[8,128,768]{2,1,0:T(8,128)(2,1)S(1)} all-to-all(bf16[8,128,768]{2,1,0:T(8,128)(2,1)S(1)} %bitcast.76), channel_id=1, replica_groups=mesh['mem'=8,'reg'=4] {'mem'}, dimensions={0} | all-to-all | bytes 3145728 | tf_op jit(solution)/shard_map/all_to_all | solution.py:121
  314.2 1.7 maximum_bitcast_fusion
  316.0 4.3 %copy.16 = bf16[128,1,8,2048]{3,2,1,0:T(8,128)(2,1)} copy(bf16[128,1,8,2048]{3,0,2,1:T(8,128)(2,1)S(1)} %maximum_bitcast_fusion) | data formatting | bytes 8388608 | tf_op jit(solution)/shard_map/broadcast_in_dim | solution.py:167
  (9 shorter events, 0.1 us)
Async XLA Ops:
  4.5 2.0 copy-start.1
  8.3 63.5 %all-to-all-start = ((bf16[8,128,1280]{2,1,0:T(8,128)(2,1)}), bf16[8,128,1280]{2,1,0:T(8,128)(2,1)S(1)}, u32[]{:S(2)}, u32[]{:S(2)}) async-start(bf16[8,128,1280]{2,1,0:T(8,128)(2,1)} %slice_bitcast_fusion), calls=%async_computation | async-start | bytes 5242880 | tf_op jit(solution)/shard_map/all_to_all | solution.py:121
  14.0 8.9 %copy-start.5 = (bf16[1,8,1024]{2,1,0:T(8,128)(2,1)S(1)}, bf16[1,8,1024]{2,1,0:T(8,128)(2,1)}, u32[]{:S(2)}) copy-start(bf16[1,8,1024]{2,1,0:T(8,128)(2,1)} %param.8) | copy-start | bytes 49156
  14.0 32.2 %copy-start = (s32[1,8,1024]{2,1,0:T(8,128)S(1)}, s32[1,8,1024]{2,1,0:T(8,128)}, u32[]{:S(2)}) copy-start(s32[1,8,1024]{2,1,0:T(8,128)} %param.9) | copy-start | bytes 98308
  16.8 29.3 %collective-permute-start.1 = (bf16[8,128,1024]{2,1,0:T(8,128)(2,1)S(1)}, bf16[8,128,1024]{2,1,0:T(8,128)(2,1)S(1)}, u32[]{:S(2)}, u32[]{:S(2)}) collective-permute-start(bf16[8,128,1024]{2,1,0:T(8,128)(2,1)S(1)} %bitcast.66), channel_id=1, source_target_pairs={{1,0},{2,1},{3,2},{5,4},{6,5},{7,6},{9,8},{10,9},{11,10},{13,12},{... | collective-permute-start | bytes 6291464 | tf_op jit(solution)/shard_map/ppermute | solution.py:125
  19.9 26.2 %collective-permute-start = (bf16[8,128,1024]{2,1,0:T(8,128)(2,1)S(1)}, bf16[8,128,1024]{2,1,0:T(8,128)(2,1)S(1)}, u32[]{:S(2)}, u32[]{:S(2)}) collective-permute-start(bf16[8,128,1024]{2,1,0:T(8,128)(2,1)S(1)} %bitcast.67), channel_id=1, source_target_pairs={{0,1},{1,2},{2,3},{4,5},{5,6},{6,7},{8,9},{9,10},{10,11},{12,13},{... | collective-permute-start | bytes 6291464 | tf_op jit(solution)/shard_map/ppermute | solution.py:124
  22.9 22.2 %collective-permute-start.3 = (bf16[8,1024]{1,0:T(8,128)(2,1)S(1)}, bf16[8,1024]{1,0:T(8,128)(2,1)S(1)}, u32[]{:S(2)}, u32[]{:S(2)}) collective-permute-start(bf16[8,1024]{1,0:T(8,128)(2,1)S(1)} %bitcast.80), channel_id=1, source_target_pairs={{1,0},{2,1},{3,2},{5,4},{6,5},{7,6},{9,8},{10,9},{11,10},{13,12},{... | collective-permute-start | bytes 49160 | tf_op jit(solution)/shard_map/ppermute | solution.py:128
  24.9 21.2 %collective-permute-start.2 = (bf16[8,1024]{1,0:T(8,128)(2,1)S(1)}, bf16[8,1024]{1,0:T(8,128)(2,1)S(1)}, u32[]{:S(2)}, u32[]{:S(2)}) collective-permute-start(bf16[8,1024]{1,0:T(8,128)(2,1)S(1)} %bitcast.81), channel_id=1, source_target_pairs={{0,1},{1,2},{2,3},{4,5},{5,6},{6,7},{8,9},{9,10},{10,11},{12,13},{... | collective-permute-start | bytes 49160 | tf_op jit(solution)/shard_map/ppermute | solution.py:127
  71.8 6.3 %copy-start.6 = (f32[1,1,1024]{2,1,0:T(1,128)S(1)}, f32[1,1,1024]{2,1,0:T(1,128)}, u32[]{:S(2)}) copy-start(f32[1,1,1024]{2,1,0:T(1,128)} %param.11) | copy-start | bytes 12292
  71.8 52.1 %all-to-all-start.1 = ((bf16[8,128,1024]{2,1,0:T(8,128)(2,1)}), bf16[8,128,1024]{2,1,0:T(8,128)(2,1)}, u32[]{:S(2)}, u32[]{:S(2)}) async-start(bf16[8,128,1024]{2,1,0:T(8,128)(2,1)} %get-tuple-element.9), calls=%async_computation.1 | async-start | bytes 4194304 | tf_op jit(solution)/shard_map/all_to_all | solution.py:121
  136.1 2.4 copy-start.4
  138.5 1.3 copy-start.7
  156.9 4.1 %copy-start.2 = (bf16[1024,1024]{1,0:T(8,128)(2,1)}, bf16[1024,1024]{1,0:T(8,128)(2,1)S(1)}, u32[]{:S(2)}) copy-start(bf16[1024,1024]{1,0:T(8,128)(2,1)S(1)} %convolution_convert_fusion) | copy-start | bytes 6291460
  198.1 39.6 %all-to-all-start.4 = ((bf16[8,128,768]{2,1,0:T(8,128)(2,1)}), bf16[8,128,768]{2,1,0:T(8,128)(2,1)S(1)}, u32[]{:S(2)}, u32[]{:S(2)}) async-start(bf16[8,128,768]{2,1,0:T(8,128)(2,1)} %slice_bitcast_fusion.1), calls=%async_computation.4 | async-start | bytes 3145728 | tf_op jit(solution)/shard_map/all_to_all | solution.py:121
  237.7 34.8 %all-to-all-start.2 = ((bf16[8,128,640]{2,1,0:T(8,128)(2,1)}), bf16[8,128,640]{2,1,0:T(8,128)(2,1)}, u32[]{:S(2)}, u32[]{:S(2)}) async-start(bf16[8,128,640]{2,1,0:T(8,128)(2,1)} %bitcast.77), calls=%async_computation.2 | async-start | bytes 2621440 | tf_op jit(solution)/shard_map/all_to_all | solution.py:121
  244.0 1.6 copy-start.3

commit v2 on v1

--- a/solution.py
+++ b/solution.py
@@ -10,6 +10,7 @@
 ITERS = 2
 INNOV_ROWS = 16
 SLOT_CHUNK = 256
+MEMBER_TILE = 32
 MIB = 1024 * 1024
 
 
@@ -72,6 +73,53 @@
     )(own, up, down, inn_own, inn_up, inn_down, picks)
 
 
+def to_blocks_kernel(in_ref, out_ref):
+    out_ref[...] = jnp.swapaxes(in_ref[...], 0, 1)
+
+
+def to_blocks(state, start, width, name):
+    members, blocks, _ = state.shape
+    return pl.pallas_call(
+        to_blocks_kernel,
+        grid=(members // MEMBER_TILE,),
+        in_specs=[
+            pl.BlockSpec((MEMBER_TILE, blocks, pl.Element(width)), lambda i: (i, 0, start))
+            if start % width
+            else pl.BlockSpec((MEMBER_TILE, blocks, width), lambda i: (i, 0, start // width))
+        ],
+        out_specs=pl.BlockSpec((blocks, MEMBER_TILE, width), lambda i: (0, i, 0)),
+        out_shape=jax.ShapeDtypeStruct((blocks, members, width), state.dtype),
+        compiler_params=pltpu.CompilerParams(vmem_limit_bytes=32 * MIB),
+        cost_estimate=pl.CostEstimate(
+            flops=0, bytes_accessed=4 * members * blocks * width, transcendentals=0
+        ),
+        name=name,
+    )(state)
+
+
+def to_members_kernel(part_ref, *refs):
+    refs[-1][...] = jnp.swapaxes(part_ref[...], 0, 1)
+
+
+def to_members(part, start, entries, whole, name):
+    blocks, members, width = part.shape
+    before = [] if whole is None else [whole]
+    return pl.pallas_call(
+        to_members_kernel,
+        grid=(members // MEMBER_TILE,),
+        in_specs=[pl.BlockSpec((blocks, MEMBER_TILE, width), lambda i: (0, i, 0))]
+        + [pl.BlockSpec(memory_space=pl.ANY)] * len(before),
+        out_specs=pl.BlockSpec((MEMBER_TILE, blocks, width), lambda i: (i, 0, start // width)),
+        out_shape=jax.ShapeDtypeStruct((members, blocks, entries), part.dtype),
+        input_output_aliases={1: 0} if before else {},
+        compiler_params=pltpu.CompilerParams(vmem_limit_bytes=32 * MIB),
+        cost_estimate=pl.CostEstimate(
+            flops=0, bytes_accessed=4 * members * blocks * width, transcendentals=0
+        ),
+        name=name,
+    )(part, *before)
+
+
 def ensemble_transform(obs_rows, innov_row, obs_weight):
     count_k = obs_rows.shape[0]
     identity = jnp.eye(count_k, dtype=jnp.float32)
@@ -130,13 +178,13 @@
     def spread(row):
         return jnp.broadcast_to(row[:, None, :], (blocks, INNOV_ROWS, row.shape[1]))
 
-    first = entries * 5 // 8
+    width = entries // 4
     state = prior_members_field[:, 0]
-    state_a = exchange(jnp.swapaxes(state[:, :, :first], 0, 1))
+    state_a = exchange(to_blocks(state, 0, 2 * width, "state_a"))
     chosen, chosen_innov = gather_chosen(
         obs, up, down, spread(innov), spread(innov_up), spread(innov_down), measure_pool_indices[0]
     )
-    state_b = jnp.swapaxes(state[:, :, first:], 0, 1)
+    state_b = to_blocks(state, 2 * width, 2 * width, "state_b")
     obs_rows = exchange(chosen)
     obs_rows, state_b = lax.optimization_barrier((obs_rows, state_b))
     state_b = exchange(state_b)
@@ -156,15 +204,13 @@
         )
         return (state_mean[None, :] + increment).astype(jnp.bfloat16).reshape(shape)
 
-    half = first // 2
-    rest = entries - first
-    parts = [
-        exchange(analysed(state_a[:, :, :half])),
-        exchange(analysed(state_a[:, :, half:])),
-        exchange(analysed(state_b)),
-    ]
-    parts = [jnp.swapaxes(part, 0, 1) for part in parts]
-    return jnp.concatenate(parts, axis=2)[:, None]
+    done_a = analysed(state_a)
+    done_a, state_b = lax.optimization_barrier((done_a, state_b))
+    done_a = exchange(done_a)
+    done_b = exchange(analysed(state_b))
+    whole = to_members(done_a, 0, entries, None, "analysis_a")
+    whole = to_members(done_b, 2 * width, entries, whole, "analysis_b")
+    return whole[:, None]
 
 
 def solution(mesh):

time: 324 us -> 296 us (0.914)
  blocking collectives: 76.9 us -> 0 us
  waiting for transfers between devices: 118 us -> 154 us
  Pallas kernels: 20.3 us -> 30.8 us
  local copies, waits for them, and re-layouts: 20.4 us -> 11 us
  starting transfers between devices: 34.4 us -> 40.3 us
  matrix products: 39.2 us -> 43.2 us
    all_to_all x2 -> x0, blocking collectives: 76.9 us -> none  [exchange(): return lax.all_to_all(x, 'mem', split_axis=0, concat_axis=0, tiled=True)]
    all_to_all x4 -> x5, waiting for transfers between devices: 100 us -> 134 us  [exchange(): return lax.all_to_all(x, 'mem', split_axis=0, concat_axis=0, tiled=True)]
    ppermute x1, waiting for transfers between devices: 0.89 us -> 15.6 us  [body(): innov_up = lax.ppermute(innov, 'reg', to_next)]
    ppermute x1, waiting for transfers between devices: 16.7 us -> 4.69 us  [body(): innov_down = lax.ppermute(innov, 'reg', to_last)]
    pallas_call x0 -> x4, Pallas kernels: none -> 10.5 us  [the longest x2 6.1 us: to_members(): pl.pallas_call(to_members_kernel, grid=(members // MEMBER_TILE,), in_spec...]
    all_to_all x4 -> x5, starting transfers between devices: 22.7 us -> 28.5 us  [exchange(): return lax.all_to_all(x, 'mem', split_axis=0, concat_axis=0, tiled=True)]
    transpose x2 -> x0, local copies, waits for them, and re-layouts: 4.43 us -> none  [the longest x1 2.66 us: body(): state_b = jnp.swapaxes(state[:, :, first:], 0, 1)]
    broadcast_in_dim x1 -> x0, local copies, waits for them, and re-layouts: 4.31 us -> none  [body(): return jnp.concatenate(parts, axis=2)[:, None]]
  transfers between devices with their start and end apart: 8 -> 9, of which waited for: 6 -> 6; matrix products, arithmetic and copies ran while one was open for 5% -> 14% of each run, Pallas kernels for 6% -> 8%
where the time goes in v2:
time: 296 us; the launch traced here: 291 us
  waiting for transfers between devices  154 us (52%)
  matrix products  43.2 us (15%)
  starting transfers between devices  40.3 us (14%)
  Pallas kernels  30.8 us (10%)
  local copies, waits for them, and re-layouts  11 us (4%)
  other arithmetic  9.9 us (3%)
    all_to_all x5, waiting for transfers between devices, exchange(): return lax.all_to_all(x, 'mem', split_axis=0, concat_axis=0, tiled=True)  134 us
    all_to_all x5, starting transfers between devices, exchange(): return lax.all_to_all(x, 'mem', split_axis=0, concat_axis=0, tiled=True)  28.5 us
    pallas_call x1, Pallas kernels, gather_chosen(): pl.pallas_call(gather_kernel, grid=(blocks,), in_specs=[vmem] * 7, out_sp...  20.3 us
    ppermute x1, waiting for transfers between devices, body(): innov_up = lax.ppermute(innov, 'reg', to_next)  15.6 us
    dot_general x2, matrix products, ensemble_transform(): jnp.dot(inverse_iter, root_iter, preferred_element_type=jnp.float32)  12.4 us
    unnamed x25, local copies, waits for them, and re-layouts  10.9 us
    dot_general x2, matrix products, ensemble_transform(): jnp.dot(newton_step, inverse_iter, preferred_element_type=jnp.float32)  9.81 us
    dot_general x2, matrix products, analysed(): lax.dot_general(transform, perturb, (((0,), (0,)), ((), ())), preferred_e...  7.94 us
  transfers between devices with their start and end apart: 9, of which 6 were waited for; matrix products, arithmetic and copies ran while one was open for 14% of the time, Pallas kernels for 8%

profile of v2, /device:TPU:9, one launch (start us, length us, event | category | flops | bytes accessed | tf_op | source)
XLA Modules:
  0.0 291.2 jit_solution(7690804261100056906)
XLA Ops:
  0.0 0.0 copy-start
  0.0 2.2 copy-done
  2.2 2.2 state_a.1
  4.4 5.7 %all-to-all-start = ((bf16[8,128,1024]{2,1,0:T(8,128)(2,1)}), bf16[8,128,1024]{2,1,0:T(8,128)(2,1)S(1)}, u32[]{:S(2)}, u32[]{:S(2)}) async-start(bf16[8,128,1024]{2,1,0:T(8,128)(2,1)} %state_a.1), calls=%async_computation | async-start | bytes 4194304 | tf_op jit(solution)/shard_map/all_to_all | solution.py:169
  10.1 0.0 copy-start.10
  10.1 0.0 copy-start.2
  10.1 2.8 copy.11
  12.9 4.2 %collective-permute-start = (bf16[8,128,1024]{2,1,0:T(8,128)(2,1)S(1)}, bf16[8,128,1024]{2,1,0:T(8,128)(2,1)S(1)}, u32[]{:S(2)}, u32[]{:S(2)}) collective-permute-start(bf16[8,128,1024]{2,1,0:T(8,128)(2,1)S(1)} %bitcast.54), channel_id=1, source_target_pairs={{0,1},{1,2},{2,3},{4,5},{5,6},{6,7},{8,9},{9,10},{10,11},{12,13},{... | collective-permute-start | bytes 6291464 | tf_op jit(solution)/shard_map/ppermute | solution.py:172
  17.1 1.9 collective-permute-start.1
  19.1 0.0 copy-done.10
  19.1 3.6 %collective-permute-start.2 = (bf16[8,1024]{1,0:T(8,128)(2,1)S(1)}, bf16[8,1024]{1,0:T(8,128)(2,1)S(1)}, u32[]{:S(2)}, u32[]{:S(2)}) collective-permute-start(bf16[8,1024]{1,0:T(8,128)(2,1)S(1)} %bitcast.63), channel_id=1, source_target_pairs={{0,1},{1,2},{2,3},{4,5},{5,6},{6,7},{8,9},{9,10},{10,11},{12,13},{... | collective-permute-start | bytes 49160 | tf_op jit(solution)/shard_map/ppermute | solution.py:175
  22.7 1.9 collective-permute-start.3
  24.6 15.6 %collective-permute-done.2 = bf16[8,1024]{1,0:T(8,128)(2,1)S(1)} collective-permute-done((bf16[8,1024]{1,0:T(8,128)(2,1)S(1)}, bf16[8,1024]{1,0:T(8,128)(2,1)S(1)}, u32[]{:S(2)}, u32[]{:S(2)}) %collective-permute-start.2) | collective-permute-done | bytes 16416 | tf_op jit(solution)/shard_map/ppermute | solution.py:175
  40.3 4.7 %collective-permute-done.3 = bf16[8,1024]{1,0:T(8,128)(2,1)S(1)} collective-permute-done((bf16[8,1024]{1,0:T(8,128)(2,1)S(1)}, bf16[8,1024]{1,0:T(8,128)(2,1)S(1)}, u32[]{:S(2)}, u32[]{:S(2)}) %collective-permute-start.3) | collective-permute-done | bytes 16416 | tf_op jit(solution)/shard_map/ppermute | solution.py:176
  44.9 0.0 collective-permute-done.up_ref
  45.0 0.0 collective-permute-done.1.down_ref
  45.0 0.0 copy-done.2
  45.1 20.3 %gather_chosen.1 = (bf16[8,128,1024]{2,1,0:T(8,128)(2,1)}, bf16[8,16,1024]{2,1,0:T(8,128)(2,1)S(1)}) custom-call(bf16[8,128,1024]{2,1,0:T(8,128)(2,1)S(1)} %bitcast.56, bf16[8,128,1024]{2,1,0:T(8,128)(2,1)S(1)} %collective-permute-done.up_ref, bf16[8,128,1024]{2,1,0:T(8,128)(2,1)S(1)} %collective-permute-done.1.down_ref, ...), custom_call_target="tpu_custom_call" | custom-call | flops 10737418240 | bytes 8388608 | tf_op jit(solution)/shard_map/gather_chosen/pallas_call | solution.py:54
  65.3 0.0 all-to-all-done
  65.3 5.1 %all-to-all-start.1 = ((bf16[8,128,1024]{2,1,0:T(8,128)(2,1)}), bf16[8,128,1024]{2,1,0:T(8,128)(2,1)}, u32[]{:S(2)}, u32[]{:S(2)}) async-start(bf16[8,128,1024]{2,1,0:T(8,128)(2,1)} %get-tuple-element.11), calls=%async_computation.1 | async-start | bytes 4194304 | tf_op jit(solution)/shard_map/all_to_all | solution.py:169
  70.5 0.0 copy-start.1
  70.5 2.2 copy-done.1
  72.7 0.0 copy-start.11
  72.7 2.2 state_b.1
  75.5 0.0 copy-done.11
  75.6 0.4 convert_reduce_fusion.1
  75.9 1.9 fusion.3
  77.8 32.8 %all-to-all-done.1 = bf16[8,128,1024]{2,1,0:T(8,128)(2,1)} async-done(((bf16[8,128,1024]{2,1,0:T(8,128)(2,1)}), bf16[8,128,1024]{2,1,0:T(8,128)(2,1)}, u32[]{:S(2)}, u32[]{:S(2)}) %all-to-all-start.1) | async-done | bytes 2097184 | tf_op jit(solution)/shard_map/all_to_all | solution.py:169
  110.7 2.2 multiply_convert_fusion
  112.8 0.0 copy-start.5
  112.8 7.3 %select_reduce_fusion = (f32[]{:T(128)}, f32[1024,1024]{1,0:T(8,128)}) fusion(bf16[1024,1024]{1,0:T(8,128)(2,1)S(1)} %bitcast.58, bf16[1024,1024]{1,0:T(8,128)(2,1)} %bitcast.9), kind=kOutput, calls=%fused_computation.13 | convolution fusion | flops 2152726528 | bytes 8388612 | tf_op jit(solution)/shard_map/dot_general | solution.py:127
  120.2 0.0 copy-done.5
  120.8 2.8 divide_convert_fusion
  123.6 0.0 copy-start.8
  123.6 1.3 copy-done.8
  125.0 3.7 %fusion = bf16[1024,1024]{1,0:T(8,128)(2,1)} fusion(bf16[1024,1024]{1,0:T(8,128)(2,1)S(1)} %divide_convert_fusion), kind=kOutput, calls=%fused_computation.2 | convolution fusion | flops 2155872256 | bytes 4194304 | tf_op jit(solution)/shard_map/dot_general | solution.py:135
  128.6 6.0 %all-to-all-start.2 = ((bf16[8,128,1024]{2,1,0:T(8,128)(2,1)}), bf16[8,128,1024]{2,1,0:T(8,128)(2,1)S(1)}, u32[]{:S(2)}, u32[]{:S(2)}) async-start(bf16[8,128,1024]{2,1,0:T(8,128)(2,1)} %state_b.1), calls=%async_computation.2 | async-start | bytes 4194304 | tf_op jit(solution)/shard_map/all_to_all | solution.py:169
  134.6 2.2 convolution_bitcast_fusion.1
  136.9 5.3 %fusion.7 = bf16[1024,1024]{1,0:T(8,128)(2,1)} fusion(bf16[1024,1024]{1,0:T(8,128)(2,1)} %fusion), kind=kOutput, calls=%fused_computation.21 | convolution fusion | flops 2151677952 | bytes 4194304 | tf_op jit(solution)/shard_map/dot_general | solution.py:141
  142.2 8.7 %fusion.1 = bf16[1024,1024]{1,0:T(8,128)(2,1)} fusion(bf16[1024,1024]{1,0:T(8,128)(2,1)} %fusion.7, bf16[1024,1024]{1,0:T(8,128)(2,1)} %copy-done.8, bf16[1024,1024]{1,0:T(8,128)(2,1)} %fusion), kind=kOutput, calls=%fused_computation.3 | convolution fusion | flops 4301258752 | bytes 8388608 | tf_op jit(solution)/shard_map/dot_general | solution.py:135
  150.9 4.5 %convolution_convert_fusion = bf16[1024,1024]{1,0:T(8,128)(2,1)S(1)} fusion(bf16[1024,1024]{1,0:T(8,128)(2,1)} %fusion.1, bf16[1024,1024]{1,0:T(8,128)(2,1)} %fusion.7), kind=kOutput, calls=%fused_computation.22 | convolution fusion | flops 2148532224 | bytes 6291456 | tf_op jit(solution)/shard_map/dot_general | solution.py:141
  155.5 0.0 copy-start.6
  155.5 0.0 copy-start.9
  155.5 1.7 convolution_bitcast_fusion
  157.2 1.7 fusion.14
  159.0 0.0 copy-done.6
  159.0 0.0 copy-done.9
  159.0 4.0 %add_convert_fusion.1 = bf16[1024,1024]{1,0:T(8,128)(2,1)} fusion(f32[1024]{0:T(1024)S(1)} %broadcast_multiply_fusion.1, bf16[1024,1024]{1,0:T(8,128)(2,1)S(1)} %copy-done.9, bf16[1024,1024]{1,0:T(8,128)(2,1)S(1)} %convolution_convert_fusion, f32[1024]{0:T(1024)S(1)} %broadcast_divide_fusion, f32[]{:T(128)S(6)} %sqrt.3), kind=kOutput, calls=%fused_computation.9 | convolution fusion | flops 2153775104 | bytes 6299652 | tf_op jit(solution)/shard_map/dot_general | solution.py:202
  163.0 18.2 %all-to-all-done.2 = bf16[8,128,1024]{2,1,0:T(8,128)(2,1)S(1)} async-done(((bf16[8,128,1024]{2,1,0:T(8,128)(2,1)}), bf16[8,128,1024]{2,1,0:T(8,128)(2,1)S(1)}, u32[]{:S(2)}, u32[]{:S(2)}) %all-to-all-start.2) | async-done | bytes 2097184 | tf_op jit(solution)/shard_map/all_to_all | solution.py:169
  181.1 0.0 copy-start.3
  181.1 1.3 copy-done.3
  182.4 6.1 %all-to-all-start.4 = ((bf16[8,128,1024]{2,1,0:T(8,128)(2,1)}), bf16[8,128,1024]{2,1,0:T(8,128)(2,1)S(1)}, u32[]{:S(2)}, u32[]{:S(2)}) async-start(bf16[8,128,1024]{2,1,0:T(8,128)(2,1)} %bitcast.60), calls=%async_computation.4 | async-start | bytes 4194304 | tf_op jit(solution)/shard_map/all_to_all | solution.py:169
  188.5 0.0 copy-start.4
  188.5 2.1 convert_reduce_fusion
  190.6 0.1 copy-done.4
  190.7 0.0 copy-start.7
  190.7 0.6 fusion.2
  191.3 1.0 copy-done.7
  192.3 4.0 %add_convert_fusion = bf16[1024,1024]{1,0:T(8,128)(2,1)} fusion(f32[1024]{0:T(1024)S(1)} %broadcast_multiply_fusion, bf16[1024,1024]{1,0:T(8,128)(2,1)S(1)} %fusion.2, bf16[1024,1024]{1,0:T(8,128)(2,1)S(1)} %copy-done.7, f32[1024]{0:T(1024)S(1)} %broadcast_divide_fusion, f32[]{:T(128)S(6)} %sqrt.3), kind=kOutput, calls=%fused_computation.8 | convolution fusion | flops 2153775104 | bytes 6299652 | tf_op jit(solution)/shard_map/dot_general | solution.py:202
  196.3 38.8 %all-to-all-done.4.part_ref = bf16[8,128,1024]{2,1,0:T(8,128)(2,1)S(1)} async-done(((bf16[8,128,1024]{2,1,0:T(8,128)(2,1)}), bf16[8,128,1024]{2,1,0:T(8,128)(2,1)S(1)}, u32[]{:S(2)}, u32[]{:S(2)}) %all-to-all-start.4) | async-done | bytes 2097184 | tf_op jit(solution)/shard_map/all_to_all | solution.py:169
  235.1 5.6 %all-to-all-start.3 = ((bf16[8,128,1024]{2,1,0:T(8,128)(2,1)}), bf16[8,128,1024]{2,1,0:T(8,128)(2,1)}, u32[]{:S(2)}, u32[]{:S(2)}) async-start(bf16[8,128,1024]{2,1,0:T(8,128)(2,1)} %bitcast.61), calls=%async_computation.3 | async-start | bytes 4194304 | tf_op jit(solution)/shard_map/all_to_all | solution.py:169
  240.7 2.1 analysis_a.1.refs_0_
  242.8 44.4 %all-to-all-done.3.part_ref = bf16[8,128,1024]{2,1,0:T(8,128)(2,1)} async-done(((bf16[8,128,1024]{2,1,0:T(8,128)(2,1)}), bf16[8,128,1024]{2,1,0:T(8,128)(2,1)}, u32[]{:S(2)}, u32[]{:S(2)}) %all-to-all-start.3) | async-done | bytes 2097184 | tf_op jit(solution)/shard_map/all_to_all | solution.py:169
  287.3 4.0 %analysis_b.1 = bf16[128,8,2048]{2,1,0:T(8,128)(2,1)} custom-call(bf16[8,128,1024]{2,1,0:T(8,128)(2,1)} %all-to-all-done.3.part_ref, bf16[128,8,2048]{2,1,0:T(8,128)(2,1)} %analysis_a.1.refs_0_), custom_call_target="tpu_custom_call", output_to_operand_aliasing={{}: (1, {})} | custom-call | bytes 4194304 | tf_op jit(solution)/shard_map/analysis_b/pallas_call | solution.py:107
  (8 shorter events, 0.1 us)
Async XLA Ops:
  0.0 2.2 copy-start
  4.4 60.9 %all-to-all-start = ((bf16[8,128,1024]{2,1,0:T(8,128)(2,1)}), bf16[8,128,1024]{2,1,0:T(8,128)(2,1)S(1)}, u32[]{:S(2)}, u32[]{:S(2)}) async-start(bf16[8,128,1024]{2,1,0:T(8,128)(2,1)} %state_a.1), calls=%async_computation | async-start | bytes 4194304 | tf_op jit(solution)/shard_map/all_to_all | solution.py:169
  10.1 8.9 %copy-start.10 = (bf16[1,8,1024]{2,1,0:T(8,128)(2,1)S(1)}, bf16[1,8,1024]{2,1,0:T(8,128)(2,1)}, u32[]{:S(2)}) copy-start(bf16[1,8,1024]{2,1,0:T(8,128)(2,1)} %param.8) | copy-start | bytes 49156
  10.1 34.9 %copy-start.2 = (s32[1,8,1024]{2,1,0:T(8,128)S(1)}, s32[1,8,1024]{2,1,0:T(8,128)}, u32[]{:S(2)}) copy-start(s32[1,8,1024]{2,1,0:T(8,128)} %param.9) | copy-start | bytes 98308
  12.9 32.1 %collective-permute-start = (bf16[8,128,1024]{2,1,0:T(8,128)(2,1)S(1)}, bf16[8,128,1024]{2,1,0:T(8,128)(2,1)S(1)}, u32[]{:S(2)}, u32[]{:S(2)}) collective-permute-start(bf16[8,128,1024]{2,1,0:T(8,128)(2,1)S(1)} %bitcast.54), channel_id=1, source_target_pairs={{0,1},{1,2},{2,3},{4,5},{5,6},{6,7},{8,9},{9,10},{10,11},{12,13},{... | collective-permute-start | bytes 6291464 | tf_op jit(solution)/shard_map/ppermute | solution.py:172
  17.1 27.8 %collective-permute-start.1 = (bf16[8,128,1024]{2,1,0:T(8,128)(2,1)S(1)}, bf16[8,128,1024]{2,1,0:T(8,128)(2,1)S(1)}, u32[]{:S(2)}, u32[]{:S(2)}) collective-permute-start(bf16[8,128,1024]{2,1,0:T(8,128)(2,1)S(1)} %bitcast.55), channel_id=1, source_target_pairs={{1,0},{2,1},{3,2},{5,4},{6,5},{7,6},{9,8},{10,9},{11,10},{13,12},{... | collective-permute-start | bytes 6291464 | tf_op jit(solution)/shard_map/ppermute | solution.py:173
  19.1 21.2 %collective-permute-start.2 = (bf16[8,1024]{1,0:T(8,128)(2,1)S(1)}, bf16[8,1024]{1,0:T(8,128)(2,1)S(1)}, u32[]{:S(2)}, u32[]{:S(2)}) collective-permute-start(bf16[8,1024]{1,0:T(8,128)(2,1)S(1)} %bitcast.63), channel_id=1, source_target_pairs={{0,1},{1,2},{2,3},{4,5},{5,6},{6,7},{8,9},{9,10},{10,11},{12,13},{... | collective-permute-start | bytes 49160 | tf_op jit(solution)/shard_map/ppermute | solution.py:175
  22.7 22.2 %collective-permute-start.3 = (bf16[8,1024]{1,0:T(8,128)(2,1)S(1)}, bf16[8,1024]{1,0:T(8,128)(2,1)S(1)}, u32[]{:S(2)}, u32[]{:S(2)}) collective-permute-start(bf16[8,1024]{1,0:T(8,128)(2,1)S(1)} %bitcast.64), channel_id=1, source_target_pairs={{1,0},{2,1},{3,2},{5,4},{6,5},{7,6},{9,8},{10,9},{11,10},{13,12},{... | collective-permute-start | bytes 49160 | tf_op jit(solution)/shard_map/ppermute | solution.py:176
  65.3 45.3 %all-to-all-start.1 = ((bf16[8,128,1024]{2,1,0:T(8,128)(2,1)}), bf16[8,128,1024]{2,1,0:T(8,128)(2,1)}, u32[]{:S(2)}, u32[]{:S(2)}) async-start(bf16[8,128,1024]{2,1,0:T(8,128)(2,1)} %get-tuple-element.11), calls=%async_computation.1 | async-start | bytes 4194304 | tf_op jit(solution)/shard_map/all_to_all | solution.py:169
  70.5 2.2 copy-start.1
  72.7 2.9 copy-start.11
  112.8 7.4 %copy-start.5 = (bf16[8,128,1024]{2,1,0:T(8,128)(2,1)}, bf16[8,128,1024]{2,1,0:T(8,128)(2,1)S(1)}, u32[]{:S(2)}) copy-start(bf16[8,128,1024]{2,1,0:T(8,128)(2,1)S(1)} %multiply_convert_fusion) | copy-start | bytes 6291460
  123.6 1.4 copy-start.8
  128.6 52.5 %all-to-all-start.2 = ((bf16[8,128,1024]{2,1,0:T(8,128)(2,1)}), bf16[8,128,1024]{2,1,0:T(8,128)(2,1)S(1)}, u32[]{:S(2)}, u32[]{:S(2)}) async-start(bf16[8,128,1024]{2,1,0:T(8,128)(2,1)} %state_b.1), calls=%async_computation.2 | async-start | bytes 4194304 | tf_op jit(solution)/shard_map/all_to_all | solution.py:169
  155.5 3.5 %copy-start.6 = (bf16[1024,1024]{1,0:T(8,128)(2,1)}, bf16[1024,1024]{1,0:T(8,128)(2,1)S(1)}, u32[]{:S(2)}) copy-start(bf16[1024,1024]{1,0:T(8,128)(2,1)S(1)} %convolution_convert_fusion) | copy-start | bytes 6291460
  155.5 3.5 %copy-start.9 = (bf16[1024,1024]{1,0:T(8,128)(2,1)S(1)}, bf16[1024,1024]{1,0:T(8,128)(2,1)}, u32[]{:S(2)}) copy-start(bf16[1024,1024]{1,0:T(8,128)(2,1)} %fusion.3) | copy-start | bytes 6291460
  181.1 1.3 copy-start.3
  182.4 52.6 %all-to-all-start.4 = ((bf16[8,128,1024]{2,1,0:T(8,128)(2,1)}), bf16[8,128,1024]{2,1,0:T(8,128)(2,1)S(1)}, u32[]{:S(2)}, u32[]{:S(2)}) async-start(bf16[8,128,1024]{2,1,0:T(8,128)(2,1)} %bitcast.60), calls=%async_computation.4 | async-start | bytes 4194304 | tf_op jit(solution)/shard_map/all_to_all | solution.py:169
  188.5 2.2 copy-start.4
  190.7 1.6 copy-start.7
  235.1 52.2 %all-to-all-start.3 = ((bf16[8,128,1024]{2,1,0:T(8,128)(2,1)}), bf16[8,128,1024]{2,1,0:T(8,128)(2,1)}, u32[]{:S(2)}, u32[]{:S(2)}) async-start(bf16[8,128,1024]{2,1,0:T(8,128)(2,1)} %bitcast.61), calls=%async_computation.3 | async-start | bytes 4194304 | tf_op jit(solution)/shard_map/all_to_all | solution.py:169

commit v3 on v2

--- a/solution.py
+++ b/solution.py
@@ -7,10 +7,11 @@
 from jax.experimental.pallas import tpu as pltpu
 from jax.sharding import PartitionSpec as P
 
-ITERS = 2
 INNOV_ROWS = 16
 SLOT_CHUNK = 256
 MEMBER_TILE = 32
+TRANSFORM_CHUNK = 256
+ANALYSIS_TILE = 256
 MIB = 1024 * 1024
 
 
@@ -120,33 +121,136 @@
     )(part, *before)
 
 
-def ensemble_transform(obs_rows, innov_row, obs_weight):
-    count_k = obs_rows.shape[0]
-    identity = jnp.eye(count_k, dtype=jnp.float32)
-    weighted = (obs_rows.astype(jnp.float32) * obs_weight[None, :]).astype(jnp.bfloat16)
-    precision_mat = lax.dot_general(
-        weighted, obs_rows, (((1,), (1,)), ((), ())), preferred_element_type=jnp.float32
-    )
-    precision_mat = precision_mat + (count_k - 1.0) * identity
-    trace_mean = jnp.trace(precision_mat) / count_k
-    root_iter = (precision_mat / trace_mean).astype(jnp.bfloat16)
-    inverse_iter = identity.astype(jnp.bfloat16)
-    for repeat in range(ITERS):
-        product = jnp.dot(inverse_iter, root_iter, preferred_element_type=jnp.float32)
-        newton_step = (1.5 * identity - 0.5 * product).astype(jnp.bfloat16)
-        if repeat + 1 < ITERS:
-            root_iter = jnp.dot(root_iter, newton_step, preferred_element_type=jnp.float32).astype(
-                jnp.bfloat16
-            )
-        inverse_iter = jnp.dot(
-            newton_step, inverse_iter, preferred_element_type=jnp.float32
-        ).astype(jnp.bfloat16)
-    gain_vector = jnp.dot(weighted, innov_row, preferred_element_type=jnp.float32)
-    inv_root = inverse_iter.astype(jnp.float32)
-    inner = jnp.dot(inv_root, gain_vector, precision=lax.Precision.HIGHEST)
-    mean_weight = jnp.dot(inv_root, inner, precision=lax.Precision.HIGHEST) / trace_mean
-    spread_factor = jnp.sqrt((count_k - 1.0) / trace_mean)
-    return (spread_factor * inv_root + mean_weight[:, None]).astype(jnp.bfloat16)
+def transform_kernel(
+    tally_ref, weight_ref, innov_ref, obs_ref, out_ref,
+    weighted, precision, root, step, root_next, step_next, inverse,
+):
+    count_k, slots = obs_ref.shape
+    spare = count_k - 1.0
+    chunks = count_k // TRANSFORM_CHUNK
+    live = lax.broadcasted_iota(jnp.int32, (1, slots), 1) < tally_ref[0, 0]
+    obs_weight = jnp.where(live, weight_ref[...], 0.0)
+
+    def span(chunk):
+        return pl.ds(pl.multiple_of(chunk * TRANSFORM_CHUNK, TRANSFORM_CHUNK), TRANSFORM_CHUNK)
+
+    def on_diagonal(chunk, value):
+        rows = lax.broadcasted_iota(jnp.int32, (count_k, TRANSFORM_CHUNK), 0)
+        columns = lax.broadcasted_iota(jnp.int32, (count_k, TRANSFORM_CHUNK), 1)
+        return jnp.where(rows == columns + chunk * TRANSFORM_CHUNK, value, 0.0)
+
+    def matmul(left, right):
+        return jnp.dot(left, right, preferred_element_type=jnp.float32)
+
+    def by_rows(left, right):
+        return lax.dot_general(
+            left, right, (((1,), (1,)), ((), ())), preferred_element_type=jnp.float32
+        )
+
+    def precise(row, matrix):
+        high = row.astype(jnp.bfloat16)
+        rest = row - high.astype(jnp.float32)
+        middle = rest.astype(jnp.bfloat16)
+        low = (rest - middle.astype(jnp.float32)).astype(jnp.bfloat16)
+        return (matmul(low, matrix) + matmul(middle, matrix)) + matmul(high, matrix)
+
+    def weigh(chunk, trace):
+        at = span(chunk)
+        scaled = (obs_ref[at, :].astype(jnp.float32) * obs_weight).astype(jnp.bfloat16)
+        weighted[at, :] = scaled
+        product = by_rows(obs_ref[...], scaled)
+        precision[:, at] = product
+        return trace + jnp.sum(on_diagonal(chunk, product))
+
+    trace = lax.fori_loop(0, chunks, weigh, jnp.float32(0.0))
+    trace_mean = trace / count_k + spare
+    scale = 1.0 / trace_mean
+    gain = by_rows(innov_ref[...], weighted[...])
+
+    @pl.loop(0, chunks)
+    def _(chunk):
+        at = span(chunk)
+        first = ((precision[:, at] + on_diagonal(chunk, spare)) * scale).astype(jnp.bfloat16)
+        root[:, at] = first
+        step[:, at] = (on_diagonal(chunk, 1.5) - 0.5 * first.astype(jnp.float32)).astype(jnp.bfloat16)
+
+    @pl.loop(0, chunks)
+    def _(chunk):
+        at = span(chunk)
+        root_next[:, at] = matmul(step[...], root[:, at]).astype(jnp.bfloat16)
+
+    @pl.loop(0, chunks)
+    def _(chunk):
+        at = span(chunk)
+        product = matmul(root_next[...], step[:, at])
+        step_next[:, at] = (on_diagonal(chunk, 1.5) - 0.5 * product).astype(jnp.bfloat16)
+
+    @pl.loop(0, chunks)
+    def _(chunk):
+        at = span(chunk)
+        inverse[:, at] = matmul(step[...], step_next[:, at]).astype(jnp.bfloat16)
+
+    inner = precise(gain, inverse[...])
+    mean_weight = precise(inner, inverse[...])[:1] * scale
+    spread_factor = jnp.sqrt(jnp.full((1, slots), spare * scale, jnp.float32))
+    out_ref[...] = (
+        spread_factor[:, :count_k] * inverse[...].astype(jnp.float32) + mean_weight
+    ).astype(jnp.bfloat16)
+
+
+def ensemble_transform(tally, weight, innov, obs_rows):
+    count_k, slots = obs_rows.shape
+    vmem = pl.BlockSpec(memory_space=pltpu.VMEM)
+    square = pltpu.VMEM((count_k, count_k), jnp.bfloat16)
+    return pl.pallas_call(
+        transform_kernel,
+        in_specs=[pl.BlockSpec(memory_space=pltpu.SMEM), vmem, vmem, vmem],
+        out_specs=vmem,
+        out_shape=jax.ShapeDtypeStruct((count_k, count_k), jnp.bfloat16),
+        scratch_shapes=[
+            pltpu.VMEM((count_k, slots), jnp.bfloat16),
+            pltpu.VMEM((count_k, count_k), jnp.float32),
+            square, square, square, square, square,
+        ],
+        compiler_params=pltpu.CompilerParams(vmem_limit_bytes=40 * MIB),
+        cost_estimate=pl.CostEstimate(
+            flops=2 * count_k * count_k * (slots + 3 * count_k),
+            bytes_accessed=4 * count_k * (slots + count_k),
+            transcendentals=0,
+        ),
+        name="transform",
+    )(tally, weight, innov, obs_rows)
+
+
+def analysis_kernel(transform_ref, state_ref, out_ref):
+    state = state_ref[...].astype(jnp.float32)
+    state_mean = jnp.sum(state, axis=0, keepdims=True) * (1.0 / state.shape[0])
+    perturb = (state - state_mean).astype(jnp.bfloat16)
+    increment = jnp.dot(transform_ref[...], perturb, preferred_element_type=jnp.float32)
+    out_ref[...] = (state_mean + increment).astype(jnp.bfloat16)
+
+
+def analysed(transform, part, name):
+    blocks, members, width = part.shape
+    count_k = blocks * members
+    out = pl.pallas_call(
+        analysis_kernel,
+        grid=(width // ANALYSIS_TILE,),
+        in_specs=[
+            pl.BlockSpec(memory_space=pltpu.VMEM),
+            pl.BlockSpec((count_k, ANALYSIS_TILE), lambda i: (0, i)),
+        ],
+        out_specs=pl.BlockSpec((count_k, ANALYSIS_TILE), lambda i: (0, i)),
+        out_shape=jax.ShapeDtypeStruct((count_k, width), jnp.bfloat16),
+        compiler_params=pltpu.CompilerParams(vmem_limit_bytes=32 * MIB),
+        cost_estimate=pl.CostEstimate(
+            flops=2 * count_k * count_k * width,
+            bytes_accessed=2 * count_k * (2 * width + count_k),
+            transcendentals=0,
+        ),
+        name=name,
+    )(transform, part.reshape(count_k, width))
+    return out.reshape(part.shape)
 
 
 def body(
@@ -178,38 +282,26 @@
     def spread(row):
         return jnp.broadcast_to(row[:, None, :], (blocks, INNOV_ROWS, row.shape[1]))
 
-    width = entries // 4
+    quarter = entries // 4
     state = prior_members_field[:, 0]
-    state_a = exchange(to_blocks(state, 0, 2 * width, "state_a"))
+    state_a = exchange(to_blocks(state, 0, 2 * quarter, "state_a"))
     chosen, chosen_innov = gather_chosen(
         obs, up, down, spread(innov), spread(innov_up), spread(innov_down), measure_pool_indices[0]
     )
-    state_b = to_blocks(state, 2 * width, 2 * width, "state_b")
+    state_b = to_blocks(state, 2 * quarter, 2 * quarter, "state_b")
     obs_rows = exchange(chosen)
     obs_rows, state_b = lax.optimization_barrier((obs_rows, state_b))
     state_b = exchange(state_b)
-    innov_row = lax.dynamic_index_in_dim(chosen_innov[:, 0], place, 0, keepdims=False)
-    obs_rows = obs_rows.reshape(-1, use_count)
-    slots = jnp.arange(use_count, dtype=jnp.int32)
-    obs_weight = jnp.where(slots < active_measure_tally[0, 0], tapered_error_weight[0, 0], 0.0)
-    transform = ensemble_transform(obs_rows, innov_row, obs_weight)
-
-    def analysed(part):
-        shape = part.shape
-        part = part.reshape(-1, shape[2]).astype(jnp.float32)
-        state_mean = jnp.mean(part, axis=0)
-        perturb = (part - state_mean[None, :]).astype(jnp.bfloat16)
-        increment = lax.dot_general(
-            transform, perturb, (((0,), (0,)), ((), ())), preferred_element_type=jnp.float32
-        )
-        return (state_mean[None, :] + increment).astype(jnp.bfloat16).reshape(shape)
-
-    done_a = analysed(state_a)
+    innov_rows = lax.dynamic_index_in_dim(chosen_innov, place, 0, keepdims=False)
+    transform = ensemble_transform(
+        active_measure_tally, tapered_error_weight[0], innov_rows, obs_rows.reshape(-1, use_count)
+    )
+    done_a = analysed(transform, state_a, "analysed_a")
     done_a, state_b = lax.optimization_barrier((done_a, state_b))
     done_a = exchange(done_a)
-    done_b = exchange(analysed(state_b))
+    done_b = exchange(analysed(transform, state_b, "analysed_b"))
     whole = to_members(done_a, 0, entries, None, "analysis_a")
-    whole = to_members(done_b, 2 * width, entries, whole, "analysis_b")
+    whole = to_members(done_b, 2 * quarter, entries, whole, "analysis_b")
     return whole[:, None]
 
 

time: 296 us -> 303 us (1.024)
  matrix products: 43.2 us -> 0 us
  waiting for transfers between devices: 154 us -> 185 us
  Pallas kernels: 30.8 us -> 57 us
  other arithmetic: 9.9 us -> 0 us
  local copies, waits for them, and re-layouts: 11 us -> 14.1 us
    dot_general x10 -> x0, matrix products: 43.2 us -> none  [the longest x2 12.4 us: ensemble_transform(): jnp.dot(inverse_iter, root_iter, preferred_element_type=jnp.float32)]
    all_to_all x5, waiting for transfers between devices: 134 us -> 165 us  [exchange(): return lax.all_to_all(x, 'mem', split_axis=0, concat_axis=0, tiled=True)]
    pallas_call x0 -> x3, Pallas kernels: none -> 27 us  [the longest x1 16.8 us: ensemble_transform(): pl.pallas_call(transform_kernel, in_specs=[pl.BlockSpec(memory_space=pltp...]
    convert_element_type x4 -> x0, other arithmetic: 7.4 us -> none  [the longest x1 2.77 us: ensemble_transform(): root_iter = (precision_mat / trace_mean).astype(jnp.bfloat16)]
    unnamed x25 -> x21, local copies, waits for them, and re-layouts: 10.9 us -> 14 us
  transfers between devices with their start and end apart: 9 -> 9, of which waited for: 6 -> 7; matrix products, arithmetic and copies ran while one was open for 14% -> 0% of each run, Pallas kernels for 8% -> 11%
where the time goes in v3:
time: 303 us; the launch traced here: 299 us
  waiting for transfers between devices  185 us (61%)
  Pallas kernels  57 us (19%)
  starting transfers between devices  42.3 us (14%)
  local copies, waits for them, and re-layouts  14.1 us (5%)
    all_to_all x5, waiting for transfers between devices, exchange(): return lax.all_to_all(x, 'mem', split_axis=0, concat_axis=0, tiled=True)  165 us
    all_to_all x5, starting transfers between devices, exchange(): return lax.all_to_all(x, 'mem', split_axis=0, concat_axis=0, tiled=True)  31.1 us
    pallas_call x1, Pallas kernels, gather_chosen(): pl.pallas_call(gather_kernel, grid=(blocks,), in_specs=[vmem] * 7, out_sp...  19.5 us
    pallas_call x1, Pallas kernels, ensemble_transform(): pl.pallas_call(transform_kernel, in_specs=[pl.BlockSpec(memory_space=pltp...  16.8 us
    ppermute x1, waiting for transfers between devices, body(): innov_up = lax.ppermute(innov, 'reg', to_next)  15.6 us
    unnamed x21, local copies, waits for them, and re-layouts  14 us
    pallas_call x2, Pallas kernels, analysed(): pl.pallas_call(analysis_kernel, grid=(width // ANALYSIS_TILE,), in_specs=...  10.1 us
    pallas_call x2, Pallas kernels, to_members(): pl.pallas_call(to_members_kernel, grid=(members // MEMBER_TILE,), in_spec...  6.1 us
  transfers between devices with their start and end apart: 9, of which 7 were waited for; matrix products, arithmetic and copies ran while one was open for 0% of the time, Pallas kernels for 11%

profile of v3, /device:TPU:9, one launch (start us, length us, event | category | flops | bytes accessed | tf_op | source)
XLA Modules:
  0.0 299.0 jit_solution(408651608938403565)
XLA Ops:
  0.0 0.0 copy-start.9
  0.0 0.0 copy-start.5
  0.0 2.8 copy.11
  2.8 3.7 %collective-permute-start = (bf16[8,128,1024]{2,1,0:T(8,128)(2,1)S(1)}, bf16[8,128,1024]{2,1,0:T(8,128)(2,1)S(1)}, u32[]{:S(2)}, u32[]{:S(2)}) collective-permute-start(bf16[8,128,1024]{2,1,0:T(8,128)(2,1)S(1)} %bitcast.22), channel_id=1, source_target_pairs={{0,1},{1,2},{2,3},{4,5},{5,6},{6,7},{8,9},{9,10},{10,11},{12,13},{... | collective-permute-start | bytes 6291464 | tf_op jit(solution)/shard_map/ppermute | solution.py:276
  6.5 1.9 collective-permute-start.1
  8.4 0.0 copy-done.9
  8.4 3.6 %collective-permute-start.2 = (bf16[8,1024]{1,0:T(8,128)(2,1)S(1)}, bf16[8,1024]{1,0:T(8,128)(2,1)S(1)}, u32[]{:S(2)}, u32[]{:S(2)}) collective-permute-start(bf16[8,1024]{1,0:T(8,128)(2,1)S(1)} %bitcast.29), channel_id=1, source_target_pairs={{0,1},{1,2},{2,3},{4,5},{5,6},{6,7},{8,9},{9,10},{10,11},{12,13},{... | collective-permute-start | bytes 49160 | tf_op jit(solution)/shard_map/ppermute | solution.py:279
  12.0 1.9 collective-permute-start.3
  14.0 15.6 %collective-permute-done.2 = bf16[8,1024]{1,0:T(8,128)(2,1)S(1)} collective-permute-done((bf16[8,1024]{1,0:T(8,128)(2,1)S(1)}, bf16[8,1024]{1,0:T(8,128)(2,1)S(1)}, u32[]{:S(2)}, u32[]{:S(2)}) %collective-permute-start.2) | collective-permute-done | bytes 16416 | tf_op jit(solution)/shard_map/ppermute | solution.py:279
  29.6 4.4 %collective-permute-done.3 = bf16[8,1024]{1,0:T(8,128)(2,1)S(1)} collective-permute-done((bf16[8,1024]{1,0:T(8,128)(2,1)S(1)}, bf16[8,1024]{1,0:T(8,128)(2,1)S(1)}, u32[]{:S(2)}, u32[]{:S(2)}) %collective-permute-start.3) | collective-permute-done | bytes 16416 | tf_op jit(solution)/shard_map/ppermute | solution.py:280
  34.0 0.0 collective-permute-done.up_ref
  34.0 0.0 collective-permute-done.1.down_ref
  34.1 0.0 copy-done.5
  34.1 19.5 %gather_chosen.1 = (bf16[8,128,1024]{2,1,0:T(8,128)(2,1)S(1)}, bf16[8,16,1024]{2,1,0:T(8,128)(2,1)S(1)}) custom-call(bf16[8,128,1024]{2,1,0:T(8,128)(2,1)S(1)} %bitcast.24, bf16[8,128,1024]{2,1,0:T(8,128)(2,1)S(1)} %collective-permute-done.up_ref, bf16[8,128,1024]{2,1,0:T(8,128)(2,1)S(1)} %collective-permute-done.1.down_ref, ...), custom_call_target="tpu_custom_call" | custom-call | flops 10737418240 | bytes 8388608 | tf_op jit(solution)/shard_map/gather_chosen/pallas_call | solution.py:55
  53.6 0.0 copy-start.2
  53.6 1.3 copy-done.2
  54.9 5.7 %all-to-all-start = ((bf16[8,128,1024]{2,1,0:T(8,128)(2,1)}), bf16[8,128,1024]{2,1,0:T(8,128)(2,1)S(1)}, u32[]{:S(2)}, u32[]{:S(2)}) async-start(bf16[8,128,1024]{2,1,0:T(8,128)(2,1)} %copy-done.2), calls=%async_computation | async-start | bytes 4194304 | tf_op jit(solution)/shard_map/all_to_all | solution.py:273
  60.6 0.0 copy-start
  60.6 2.2 copy-done
  62.8 2.2 state_a.1
  65.0 24.2 %all-to-all-done = bf16[8,128,1024]{2,1,0:T(8,128)(2,1)S(1)} async-done(((bf16[8,128,1024]{2,1,0:T(8,128)(2,1)}), bf16[8,128,1024]{2,1,0:T(8,128)(2,1)S(1)}, u32[]{:S(2)}, u32[]{:S(2)}) %all-to-all-start) | async-done | bytes 2097184 | tf_op jit(solution)/shard_map/all_to_all | solution.py:273
  89.2 6.5 %all-to-all-start.1 = ((bf16[8,128,1024]{2,1,0:T(8,128)(2,1)}), bf16[8,128,1024]{2,1,0:T(8,128)(2,1)}, u32[]{:S(2)}, u32[]{:S(2)}) async-start(bf16[8,128,1024]{2,1,0:T(8,128)(2,1)} %state_a.1), calls=%async_computation.1 | async-start | bytes 4194304 | tf_op jit(solution)/shard_map/all_to_all | solution.py:273
  95.8 0.0 copy-start.1
  95.8 2.2 copy-done.1
  98.0 2.2 state_b.1
  100.1 0.0 copy-start.6
  100.2 36.4 %all-to-all-done.1 = bf16[8,128,1024]{2,1,0:T(8,128)(2,1)} async-done(((bf16[8,128,1024]{2,1,0:T(8,128)(2,1)}), bf16[8,128,1024]{2,1,0:T(8,128)(2,1)}, u32[]{:S(2)}, u32[]{:S(2)}) %all-to-all-start.1) | async-done | bytes 2097184 | tf_op jit(solution)/shard_map/all_to_all | solution.py:273
  136.5 7.0 %all-to-all-start.2 = ((bf16[8,128,1024]{2,1,0:T(8,128)(2,1)}), bf16[8,128,1024]{2,1,0:T(8,128)(2,1)}, u32[]{:S(2)}, u32[]{:S(2)}) async-start(bf16[8,128,1024]{2,1,0:T(8,128)(2,1)} %state_b.1), calls=%async_computation.2 | async-start | bytes 4194304 | tf_op jit(solution)/shard_map/all_to_all | solution.py:273
  144.2 0.0 copy-done.6
  144.2 16.8 %transform.1.transform_ref = bf16[1024,1024]{1,0:T(8,128)(2,1)S(1)} custom-call(s32[1,1]{1,0:T(1,128)S(6)} %copy.13.tally_ref, f32[1,1024]{1,0:T(1,128)S(1)} %bitcast.28, bf16[16,1024]{1,0:T(8,128)(2,1)S(1)} %dynamic-slice_bitcast_fusion.innov_ref, bf16[1024,1024]{1,0:T(8,128)(2,1)S(1)} %bitcast.21), custom_call_target="tpu_custom_call" | custom-call | flops 8589934592 | bytes 8388608 | tf_op jit(solution)/shard_map/transform/pallas_call | solution.py:205
  161.1 5.1 %analysed_a.1 = bf16[1024,1024]{1,0:T(8,128)(2,1)S(1)} custom-call(bf16[1024,1024]{1,0:T(8,128)(2,1)S(1)} %transform.1.transform_ref, bf16[1024,1024]{1,0:T(8,128)(2,1)} %bitcast.9.state_ref), custom_call_target="tpu_custom_call" | custom-call | flops 2147483648 | bytes 6291456 | tf_op jit(solution)/shard_map/analysed_a/pallas_call | solution.py:236
  166.1 0.0 copy-start.3
  166.2 1.3 copy-done.3
  167.5 0.0 copy-start.7
  167.5 1.3 copy-done.7
  168.8 21.4 %all-to-all-done.2 = bf16[8,128,1024]{2,1,0:T(8,128)(2,1)} async-done(((bf16[8,128,1024]{2,1,0:T(8,128)(2,1)}), bf16[8,128,1024]{2,1,0:T(8,128)(2,1)}, u32[]{:S(2)}, u32[]{:S(2)}) %all-to-all-start.2) | async-done | bytes 2097184 | tf_op jit(solution)/shard_map/all_to_all | solution.py:273
  190.1 6.2 %all-to-all-start.4 = ((bf16[8,128,1024]{2,1,0:T(8,128)(2,1)}), bf16[8,128,1024]{2,1,0:T(8,128)(2,1)S(1)}, u32[]{:S(2)}, u32[]{:S(2)}) async-start(bf16[8,128,1024]{2,1,0:T(8,128)(2,1)} %bitcast.25), calls=%async_computation.4 | async-start | bytes 4194304 | tf_op jit(solution)/shard_map/all_to_all | solution.py:273
  196.3 0.0 copy-start.8
  196.3 1.6 copy-done.8
  197.9 5.1 %analysed_b.1 = bf16[1024,1024]{1,0:T(8,128)(2,1)S(1)} custom-call(bf16[1024,1024]{1,0:T(8,128)(2,1)S(1)} %copy-done.8, bf16[1024,1024]{1,0:T(8,128)(2,1)} %bitcast.11.state_ref), custom_call_target="tpu_custom_call" | custom-call | flops 2147483648 | bytes 6291456 | tf_op jit(solution)/shard_map/analysed_b/pallas_call | solution.py:236
  203.0 0.0 copy-start.4
  203.0 1.3 copy-done.4
  204.3 38.6 %all-to-all-done.4.part_ref = bf16[8,128,1024]{2,1,0:T(8,128)(2,1)S(1)} async-done(((bf16[8,128,1024]{2,1,0:T(8,128)(2,1)}), bf16[8,128,1024]{2,1,0:T(8,128)(2,1)S(1)}, u32[]{:S(2)}, u32[]{:S(2)}) %all-to-all-start.4) | async-done | bytes 2097184 | tf_op jit(solution)/shard_map/all_to_all | solution.py:273
  242.9 5.6 %all-to-all-start.3 = ((bf16[8,128,1024]{2,1,0:T(8,128)(2,1)}), bf16[8,128,1024]{2,1,0:T(8,128)(2,1)}, u32[]{:S(2)}, u32[]{:S(2)}) async-start(bf16[8,128,1024]{2,1,0:T(8,128)(2,1)} %bitcast.26), calls=%async_computation.3 | async-start | bytes 4194304 | tf_op jit(solution)/shard_map/all_to_all | solution.py:273
  248.5 2.1 analysis_a.1.refs_0_
  250.6 44.4 %all-to-all-done.3.part_ref = bf16[8,128,1024]{2,1,0:T(8,128)(2,1)} async-done(((bf16[8,128,1024]{2,1,0:T(8,128)(2,1)}), bf16[8,128,1024]{2,1,0:T(8,128)(2,1)}, u32[]{:S(2)}, u32[]{:S(2)}) %all-to-all-start.3) | async-done | bytes 2097184 | tf_op jit(solution)/shard_map/all_to_all | solution.py:273
  295.0 4.0 %analysis_b.1 = bf16[128,8,2048]{2,1,0:T(8,128)(2,1)} custom-call(bf16[8,128,1024]{2,1,0:T(8,128)(2,1)} %all-to-all-done.3.part_ref, bf16[128,8,2048]{2,1,0:T(8,128)(2,1)} %analysis_a.1.refs_0_), custom_call_target="tpu_custom_call", output_to_operand_aliasing={{}: (1, {})} | custom-call | bytes 4194304 | tf_op jit(solution)/shard_map/analysis_b/pallas_call | solution.py:108
  (4 shorter events, 0.1 us)
Async XLA Ops:
  0.0 8.4 %copy-start.9 = (bf16[1,8,1024]{2,1,0:T(8,128)(2,1)S(1)}, bf16[1,8,1024]{2,1,0:T(8,128)(2,1)}, u32[]{:S(2)}) copy-start(bf16[1,8,1024]{2,1,0:T(8,128)(2,1)} %param.8) | copy-start | bytes 49156
  0.0 34.1 %copy-start.5 = (s32[1,8,1024]{2,1,0:T(8,128)S(1)}, s32[1,8,1024]{2,1,0:T(8,128)}, u32[]{:S(2)}) copy-start(s32[1,8,1024]{2,1,0:T(8,128)} %param.9) | copy-start | bytes 98308
  2.8 31.2 %collective-permute-start = (bf16[8,128,1024]{2,1,0:T(8,128)(2,1)S(1)}, bf16[8,128,1024]{2,1,0:T(8,128)(2,1)S(1)}, u32[]{:S(2)}, u32[]{:S(2)}) collective-permute-start(bf16[8,128,1024]{2,1,0:T(8,128)(2,1)S(1)} %bitcast.22), channel_id=1, source_target_pairs={{0,1},{1,2},{2,3},{4,5},{5,6},{6,7},{8,9},{9,10},{10,11},{12,13},{... | collective-permute-start | bytes 6291464 | tf_op jit(solution)/shard_map/ppermute | solution.py:276
  6.5 27.5 %collective-permute-start.1 = (bf16[8,128,1024]{2,1,0:T(8,128)(2,1)S(1)}, bf16[8,128,1024]{2,1,0:T(8,128)(2,1)S(1)}, u32[]{:S(2)}, u32[]{:S(2)}) collective-permute-start(bf16[8,128,1024]{2,1,0:T(8,128)(2,1)S(1)} %bitcast.23), channel_id=1, source_target_pairs={{1,0},{2,1},{3,2},{5,4},{6,5},{7,6},{9,8},{10,9},{11,10},{13,12},{... | collective-permute-start | bytes 6291464 | tf_op jit(solution)/shard_map/ppermute | solution.py:277
  8.4 21.2 %collective-permute-start.2 = (bf16[8,1024]{1,0:T(8,128)(2,1)S(1)}, bf16[8,1024]{1,0:T(8,128)(2,1)S(1)}, u32[]{:S(2)}, u32[]{:S(2)}) collective-permute-start(bf16[8,1024]{1,0:T(8,128)(2,1)S(1)} %bitcast.29), channel_id=1, source_target_pairs={{0,1},{1,2},{2,3},{4,5},{5,6},{6,7},{8,9},{9,10},{10,11},{12,13},{... | collective-permute-start | bytes 49160 | tf_op jit(solution)/shard_map/ppermute | solution.py:279
  12.0 21.9 %collective-permute-start.3 = (bf16[8,1024]{1,0:T(8,128)(2,1)S(1)}, bf16[8,1024]{1,0:T(8,128)(2,1)S(1)}, u32[]{:S(2)}, u32[]{:S(2)}) collective-permute-start(bf16[8,1024]{1,0:T(8,128)(2,1)S(1)} %bitcast.30), channel_id=1, source_target_pairs={{1,0},{2,1},{3,2},{5,4},{6,5},{7,6},{9,8},{10,9},{11,10},{13,12},{... | collective-permute-start | bytes 49160 | tf_op jit(solution)/shard_map/ppermute | solution.py:280
  53.6 1.3 copy-start.2
  54.9 34.3 %all-to-all-start = ((bf16[8,128,1024]{2,1,0:T(8,128)(2,1)}), bf16[8,128,1024]{2,1,0:T(8,128)(2,1)S(1)}, u32[]{:S(2)}, u32[]{:S(2)}) async-start(bf16[8,128,1024]{2,1,0:T(8,128)(2,1)} %copy-done.2), calls=%async_computation | async-start | bytes 4194304 | tf_op jit(solution)/shard_map/all_to_all | solution.py:273
  60.6 2.2 copy-start
  89.2 47.3 %all-to-all-start.1 = ((bf16[8,128,1024]{2,1,0:T(8,128)(2,1)}), bf16[8,128,1024]{2,1,0:T(8,128)(2,1)}, u32[]{:S(2)}, u32[]{:S(2)}) async-start(bf16[8,128,1024]{2,1,0:T(8,128)(2,1)} %state_a.1), calls=%async_computation.1 | async-start | bytes 4194304 | tf_op jit(solution)/shard_map/all_to_all | solution.py:273
  95.8 2.2 copy-start.1
  100.1 44.1 %copy-start.6 = (f32[1,1,1024]{2,1,0:T(1,128)S(1)}, f32[1,1,1024]{2,1,0:T(1,128)}, u32[]{:S(2)}) copy-start(f32[1,1,1024]{2,1,0:T(1,128)} %param.11) | copy-start | bytes 12292
  136.5 53.6 %all-to-all-start.2 = ((bf16[8,128,1024]{2,1,0:T(8,128)(2,1)}), bf16[8,128,1024]{2,1,0:T(8,128)(2,1)}, u32[]{:S(2)}, u32[]{:S(2)}) async-start(bf16[8,128,1024]{2,1,0:T(8,128)(2,1)} %state_b.1), calls=%async_computation.2 | async-start | bytes 4194304 | tf_op jit(solution)/shard_map/all_to_all | solution.py:273
  166.1 1.3 copy-start.3
  167.5 1.3 copy-start.7
  190.1 52.7 %all-to-all-start.4 = ((bf16[8,128,1024]{2,1,0:T(8,128)(2,1)}), bf16[8,128,1024]{2,1,0:T(8,128)(2,1)S(1)}, u32[]{:S(2)}, u32[]{:S(2)}) async-start(bf16[8,128,1024]{2,1,0:T(8,128)(2,1)} %bitcast.25), calls=%async_computation.4 | async-start | bytes 4194304 | tf_op jit(solution)/shard_map/all_to_all | solution.py:273
  196.3 1.6 copy-start.8
  203.0 1.3 copy-start.4
  242.9 52.2 %all-to-all-start.3 = ((bf16[8,128,1024]{2,1,0:T(8,128)(2,1)}), bf16[8,128,1024]{2,1,0:T(8,128)(2,1)}, u32[]{:S(2)}, u32[]{:S(2)}) async-start(bf16[8,128,1024]{2,1,0:T(8,128)(2,1)} %bitcast.26), calls=%async_computation.3 | async-start | bytes 4194304 | tf_op jit(solution)/shard_map/all_to_all | solution.py:273

commit v4 on v3

--- a/solution.py
+++ b/solution.py
@@ -10,52 +10,79 @@
 INNOV_ROWS = 16
 SLOT_CHUNK = 256
 MEMBER_TILE = 32
+POOL_TILE = 256
 TRANSFORM_CHUNK = 256
 ANALYSIS_TILE = 256
 MIB = 1024 * 1024
 
 
-def gather_kernel(own_ref, up_ref, down_ref, inn_own, inn_up, inn_down, idx_ref, out_ref, inn_ref):
+def pool_kernel(obs_ref, innov_ref, out_ref):
+    members = obs_ref.shape[0]
+    out_ref[:, :members, :] = jnp.swapaxes(obs_ref[...], 0, 1)
+    shape = (out_ref.shape[0], INNOV_ROWS, out_ref.shape[2])
+    out_ref[:, members:, :] = jnp.broadcast_to(innov_ref[...][:, None, :], shape)
+
+
+def pool_rows(obs, innov):
+    members, blocks, depth = obs.shape
+    rows = members + INNOV_ROWS
+    return pl.pallas_call(
+        pool_kernel,
+        grid=(depth // POOL_TILE,),
+        in_specs=[
+            pl.BlockSpec((members, blocks, POOL_TILE), lambda i: (0, 0, i)),
+            pl.BlockSpec((blocks, POOL_TILE), lambda i: (0, i)),
+        ],
+        out_specs=pl.BlockSpec((blocks, rows, POOL_TILE), lambda i: (0, 0, i)),
+        out_shape=jax.ShapeDtypeStruct((blocks, rows, depth), obs.dtype),
+        compiler_params=pltpu.CompilerParams(vmem_limit_bytes=60 * MIB),
+        cost_estimate=pl.CostEstimate(
+            flops=0, bytes_accessed=4 * rows * blocks * depth, transcendentals=0
+        ),
+        name="pool_rows",
+    )(obs, innov)
+
+
+def gather_kernel(own_ref, up_ref, down_ref, idx_ref, out_ref, inn_ref):
     block = pl.program_id(0)
-    blocks = own_ref.shape[0]
-    depth = own_ref.shape[2]
-    members = own_ref.shape[1]
+    blocks, rows, depth = own_ref.shape
+    members = out_ref.shape[1]
+    slots = out_ref.shape[2]
     west = jnp.maximum(block - 1, 0)
     east = jnp.minimum(block + 1, blocks - 1)
-    slots = out_ref.shape[2]
     sources = (
-        (own_ref, inn_own, block, None),
-        (up_ref, inn_up, block, None),
-        (down_ref, inn_down, block, None),
-        (own_ref, inn_own, west, block > 0),
-        (own_ref, inn_own, east, block < blocks - 1),
+        (own_ref, block, None),
+        (up_ref, block, None),
+        (down_ref, block, None),
+        (own_ref, west, block > 0),
+        (own_ref, east, block < blocks - 1),
     )
-    rows = lax.broadcasted_iota(jnp.int32, (depth, SLOT_CHUNK), 0)
+    columns = lax.broadcasted_iota(jnp.int32, (depth, SLOT_CHUNK), 0)
 
     @pl.loop(0, slots // SLOT_CHUNK)
     def _(chunk):
         where = pl.ds(pl.multiple_of(chunk * SLOT_CHUNK, SLOT_CHUNK), SLOT_CHUNK)
         picks = idx_ref[pl.ds(block, 1), where]
-        acc = jnp.zeros((members + INNOV_ROWS, SLOT_CHUNK), jnp.float32)
-        for number, (ref, inn, at, live) in enumerate(sources):
+        acc = jnp.zeros((rows, SLOT_CHUNK), jnp.float32)
+        for number, (ref, at, live) in enumerate(sources):
             local = picks - number * depth
             if live is not None:
                 local = jnp.where(live, local, -1)
-            one_hot = jnp.where(rows == local, 1.0, 0.0).astype(jnp.bfloat16)
-            lhs = jnp.concatenate([ref[at], inn[at]], axis=0)
-            acc += jnp.dot(lhs, one_hot, preferred_element_type=jnp.float32)
+            one_hot = jnp.where(columns == local, 1.0, 0.0).astype(jnp.bfloat16)
+            acc += jnp.dot(ref[at], one_hot, preferred_element_type=jnp.float32)
         out_ref[0, :, where] = acc[:members].astype(jnp.bfloat16)
         inn_ref[0, :, where] = acc[members:].astype(jnp.bfloat16)
 
 
-def gather_chosen(own, up, down, inn_own, inn_up, inn_down, picks):
-    blocks, members, depth = own.shape
+def gather_chosen(own, up, down, picks):
+    blocks, rows, depth = own.shape
+    members = rows - INNOV_ROWS
     slots = picks.shape[1]
     vmem = pl.BlockSpec(memory_space=pltpu.VMEM)
     return pl.pallas_call(
         gather_kernel,
         grid=(blocks,),
-        in_specs=[vmem] * 7,
+        in_specs=[vmem] * 4,
         out_specs=[
             pl.BlockSpec((1, members, slots), lambda b: (b, 0, 0)),
             pl.BlockSpec((1, INNOV_ROWS, slots), lambda b: (b, 0, 0)),
@@ -66,12 +93,12 @@
         ],
         compiler_params=pltpu.CompilerParams(vmem_limit_bytes=40 * MIB),
         cost_estimate=pl.CostEstimate(
-            flops=2 * blocks * members * depth * 5 * slots,
-            bytes_accessed=2 * blocks * members * (3 * depth + slots),
+            flops=2 * blocks * rows * depth * 5 * slots,
+            bytes_accessed=2 * blocks * rows * (3 * depth + slots),
             transcendentals=0,
         ),
         name="gather_chosen",
-    )(own, up, down, inn_own, inn_up, inn_down, picks)
+    )(own, up, down, picks)
 
 
 def to_blocks_kernel(in_ref, out_ref):
@@ -90,7 +117,7 @@
         ],
         out_specs=pl.BlockSpec((blocks, MEMBER_TILE, width), lambda i: (0, i, 0)),
         out_shape=jax.ShapeDtypeStruct((blocks, members, width), state.dtype),
-        compiler_params=pltpu.CompilerParams(vmem_limit_bytes=32 * MIB),
+        compiler_params=pltpu.CompilerParams(vmem_limit_bytes=60 * MIB),
         cost_estimate=pl.CostEstimate(
             flops=0, bytes_accessed=4 * members * blocks * width, transcendentals=0
         ),
@@ -272,24 +299,18 @@
     def exchange(x):
         return lax.all_to_all(x, "mem", split_axis=0, concat_axis=0, tiled=True)
 
-    obs = jnp.swapaxes(measure_space_deviations[:, 0], 0, 1)
-    up = lax.ppermute(obs, "reg", to_next)
-    down = lax.ppermute(obs, "reg", to_last)
-    innov = measured_minus_predicted[0]
-    innov_up = lax.ppermute(innov, "reg", to_next)
-    innov_down = lax.ppermute(innov, "reg", to_last)
-
-    def spread(row):
-        return jnp.broadcast_to(row[:, None, :], (blocks, INNOV_ROWS, row.shape[1]))
-
     quarter = entries // 4
     state = prior_members_field[:, 0]
-    state_a = exchange(to_blocks(state, 0, 2 * quarter, "state_a"))
-    chosen, chosen_innov = gather_chosen(
-        obs, up, down, spread(innov), spread(innov_up), spread(innov_down), measure_pool_indices[0]
-    )
+    state_a = to_blocks(state, 0, 2 * quarter, "state_a")
+    devs, state_a = lax.optimization_barrier((measure_space_deviations[:, 0], state_a))
+    state_a = exchange(state_a)
+    pool = pool_rows(devs, measured_minus_predicted[0])
+    up = lax.ppermute(pool, "reg", to_next)
+    down = lax.ppermute(pool, "reg", to_last)
+    chosen, chosen_innov = gather_chosen(pool, up, down, measure_pool_indices[0])
+    chosen, state_a = lax.optimization_barrier((chosen, state_a))
+    obs_rows = exchange(chosen)
     state_b = to_blocks(state, 2 * quarter, 2 * quarter, "state_b")
-    obs_rows = exchange(chosen)
     obs_rows, state_b = lax.optimization_barrier((obs_rows, state_b))
     state_b = exchange(state_b)
     innov_rows = lax.dynamic_index_in_dim(chosen_innov, place, 0, keepdims=False)

time: 303 us -> 272 us (0.90)
  waiting for transfers between devices: 185 us -> 157 us
  Pallas kernels: 57 us -> 65.4 us
  starting transfers between devices: 42.3 us -> 36.7 us
  local copies, waits for them, and re-layouts: 14.1 us -> 8.58 us
    all_to_all x5, waiting for transfers between devices: 165 us -> 128 us  [exchange(): return lax.all_to_all(x, 'mem', split_axis=0, concat_axis=0, tiled=True)]
    ppermute x4 -> x2, waiting for transfers between devices: 20 us -> 28.7 us  [the longest x1 24.2 us: body(): up = lax.ppermute(pool, 'reg', to_next)]
    unnamed x21 -> x16, local copies, waits for them, and re-layouts: 14 us -> 8.57 us
    ppermute x4 -> x2, starting transfers between devices: 11.2 us -> 6.15 us  [the longest x1 4.23 us: body(): up = lax.ppermute(pool, 'reg', to_next)]
    pallas_call x1 -> x2, Pallas kernels: 19.5 us -> 23.5 us  [the longest x1 19.5 us: gather_chosen(): pl.pallas_call(gather_kernel, grid=(blocks,), in_specs=[vmem] * 4, out_sp...]
    pallas_call x2, Pallas kernels: 4.41 us -> 8.01 us  [to_blocks(): pl.pallas_call(to_blocks_kernel, grid=(members // MEMBER_TILE,), in_specs...]
  transfers between devices with their start and end apart: 9 -> 7, of which waited for: 7 -> 6; matrix products, arithmetic and copies ran while one was open for 0% -> 0% of each run, Pallas kernels for 11% -> 21%
where the time goes in v4:
time: 272 us; the launch traced here: 268 us
  waiting for transfers between devices  157 us (58%)
  Pallas kernels  65.4 us (24%)
  starting transfers between devices  36.7 us (13%)
  local copies, waits for them, and re-layouts  8.58 us (3%)
    all_to_all x5, waiting for transfers between devices, exchange(): return lax.all_to_all(x, 'mem', split_axis=0, concat_axis=0, tiled=True)  128 us
    all_to_all x5, starting transfers between devices, exchange(): return lax.all_to_all(x, 'mem', split_axis=0, concat_axis=0, tiled=True)  30.6 us
    ppermute x1, waiting for transfers between devices, body(): up = lax.ppermute(pool, 'reg', to_next)  24.2 us
    pallas_call x1, Pallas kernels, gather_chosen(): pl.pallas_call(gather_kernel, grid=(blocks,), in_specs=[vmem] * 4, out_sp...  19.5 us
    pallas_call x1, Pallas kernels, ensemble_transform(): pl.pallas_call(transform_kernel, in_specs=[pl.BlockSpec(memory_space=pltp...  18.4 us
    pallas_call x2, Pallas kernels, analysed(): pl.pallas_call(analysis_kernel, grid=(width // ANALYSIS_TILE,), in_specs=...  9.31 us
    unnamed x16, local copies, waits for them, and re-layouts  8.57 us
    pallas_call x2, Pallas kernels, to_blocks(): pl.pallas_call(to_blocks_kernel, grid=(members // MEMBER_TILE,), in_specs...  8.01 us
  transfers between devices with their start and end apart: 7, of which 6 were waited for; matrix products, arithmetic and copies ran while one was open for 0% of the time, Pallas kernels for 21%

profile of v4, /device:TPU:9, one launch (start us, length us, event | category | flops | bytes accessed | tf_op | source)
XLA Modules:
  0.0 268.1 jit_solution(3150240900035484246)
XLA Ops:
  0.0 4.0 %state_a.1 = bf16[8,128,1024]{2,1,0:T(8,128)(2,1)} custom-call(bf16[128,8,2048]{2,1,0:T(8,128)(2,1)} %bitcast.20), custom_call_target="tpu_custom_call" | custom-call | bytes 4194304 | tf_op jit(solution)/shard_map/state_a/pallas_call | solution.py:110
  4.0 5.7 %all-to-all-start = ((bf16[8,128,1024]{2,1,0:T(8,128)(2,1)}), bf16[8,128,1024]{2,1,0:T(8,128)(2,1)S(1)}, u32[]{:S(2)}, u32[]{:S(2)}) async-start(bf16[8,128,1024]{2,1,0:T(8,128)(2,1)} %state_a.1), calls=%async_computation | async-start | bytes 4194304 | tf_op jit(solution)/shard_map/all_to_all | solution.py:300
  9.7 0.0 copy-start.4
  9.7 4.1 %pool_rows.1.own_ref = bf16[8,144,1024]{2,1,0:T(8,128)(2,1)} custom-call(bf16[128,8,1024]{2,1,0:T(8,128)(2,1)} %bitcast.22, bf16[8,1024]{1,0:T(8,128)(2,1)} %bitcast.23), custom_call_target="tpu_custom_call" | custom-call | bytes 4718592 | tf_op jit(solution)/shard_map/pool_rows/pallas_call | solution.py:29
  13.8 4.2 %collective-permute-start = (bf16[8,144,1024]{2,1,0:T(8,128)(2,1)}, bf16[8,144,1024]{2,1,0:T(8,128)(2,1)S(1)}, u32[]{:S(2)}, u32[]{:S(2)}) collective-permute-start(bf16[8,144,1024]{2,1,0:T(8,128)(2,1)} %pool_rows.1.own_ref), channel_id=1, source_target_pairs={{0,1},{1,2},{2,3},{4,5},{5,6},{6,7},{8,9},{9,10},{10,11},{12,13},{... | collective-permute-start | bytes 7077896 | tf_op jit(solution)/shard_map/ppermute | solution.py:308
  18.0 1.9 collective-permute-start.1
  20.0 24.2 %collective-permute-done.up_ref = bf16[8,144,1024]{2,1,0:T(8,128)(2,1)S(1)} collective-permute-done((bf16[8,144,1024]{2,1,0:T(8,128)(2,1)}, bf16[8,144,1024]{2,1,0:T(8,128)(2,1)S(1)}, u32[]{:S(2)}, u32[]{:S(2)}) %collective-permute-start) | collective-permute-done | bytes 2359328 | tf_op jit(solution)/shard_map/ppermute | solution.py:308
  44.1 4.6 %collective-permute-done.1.down_ref = bf16[8,144,1024]{2,1,0:T(8,128)(2,1)S(1)} collective-permute-done((bf16[8,144,1024]{2,1,0:T(8,128)(2,1)}, bf16[8,144,1024]{2,1,0:T(8,128)(2,1)S(1)}, u32[]{:S(2)}, u32[]{:S(2)}) %collective-permute-start.1) | collective-permute-done | bytes 2359328 | tf_op jit(solution)/shard_map/ppermute | solution.py:309
  48.7 0.0 copy-done.4
  48.7 0.0 copy-start
  48.7 1.7 copy-done
  50.4 19.5 %gather_chosen.1 = (bf16[8,128,1024]{2,1,0:T(8,128)(2,1)S(1)}, bf16[8,16,1024]{2,1,0:T(8,128)(2,1)S(1)}) custom-call(bf16[8,144,1024]{2,1,0:T(8,128)(2,1)S(1)} %copy-done, bf16[8,144,1024]{2,1,0:T(8,128)(2,1)S(1)} %collective-permute-done.up_ref, bf16[8,144,1024]{2,1,0:T(8,128)(2,1)S(1)} %collective-permute-done.1.down_ref, s32[8,1024]{1,0:T(8,128)S(1)} %bitcast.18), custom_call_target="tpu_custom_call" | custom-call | flops 12079595520 | bytes 9437184 | tf_op jit(solution)/shard_map/gather_chosen/pallas_call | solution.py:82
  69.9 0.0 copy-start.1
  69.9 1.3 copy-done.1
  71.2 0.0 all-to-all-done
  71.2 5.4 %all-to-all-start.1 = ((bf16[8,128,1024]{2,1,0:T(8,128)(2,1)}), bf16[8,128,1024]{2,1,0:T(8,128)(2,1)}, u32[]{:S(2)}, u32[]{:S(2)}) async-start(bf16[8,128,1024]{2,1,0:T(8,128)(2,1)} %copy-done.1), calls=%async_computation.1 | async-start | bytes 4194304 | tf_op jit(solution)/shard_map/all_to_all | solution.py:300
  76.6 4.0 %state_b.1 = bf16[8,128,1024]{2,1,0:T(8,128)(2,1)} custom-call(bf16[128,8,2048]{2,1,0:T(8,128)(2,1)} %bitcast.21), custom_call_target="tpu_custom_call" | custom-call | bytes 4194304 | tf_op jit(solution)/shard_map/state_b/pallas_call | solution.py:110
  80.6 0.0 copy-start.5
  80.6 29.7 %all-to-all-done.1 = bf16[8,128,1024]{2,1,0:T(8,128)(2,1)} async-done(((bf16[8,128,1024]{2,1,0:T(8,128)(2,1)}), bf16[8,128,1024]{2,1,0:T(8,128)(2,1)}, u32[]{:S(2)}, u32[]{:S(2)}) %all-to-all-start.1) | async-done | bytes 2097184 | tf_op jit(solution)/shard_map/all_to_all | solution.py:300
  110.3 6.7 %all-to-all-start.2 = ((bf16[8,128,1024]{2,1,0:T(8,128)(2,1)}), bf16[8,128,1024]{2,1,0:T(8,128)(2,1)}, u32[]{:S(2)}, u32[]{:S(2)}) async-start(bf16[8,128,1024]{2,1,0:T(8,128)(2,1)} %state_b.1), calls=%async_computation.2 | async-start | bytes 4194304 | tf_op jit(solution)/shard_map/all_to_all | solution.py:300
  117.7 0.0 copy-done.5
  117.7 18.4 %transform.1.transform_ref = bf16[1024,1024]{1,0:T(8,128)(2,1)S(1)} custom-call(s32[1,1]{1,0:T(1,128)S(6)} %copy.10.tally_ref, f32[1,1024]{1,0:T(1,128)S(1)} %bitcast.19, bf16[16,1024]{1,0:T(8,128)(2,1)S(1)} %dynamic-slice_bitcast_fusion.innov_ref, bf16[1024,1024]{1,0:T(8,128)(2,1)} %bitcast.6.obs_ref), custom_call_target="tpu_custom_call" | custom-call | flops 8589934592 | bytes 8388608 | tf_op jit(solution)/shard_map/transform/pallas_call | solution.py:232
  136.1 4.3 %analysed_a.1 = bf16[1024,1024]{1,0:T(8,128)(2,1)S(1)} custom-call(bf16[1024,1024]{1,0:T(8,128)(2,1)S(1)} %transform.1.transform_ref, bf16[1024,1024]{1,0:T(8,128)(2,1)S(1)} %bitcast.15), custom_call_target="tpu_custom_call" | custom-call | flops 2147483648 | bytes 6291456 | tf_op jit(solution)/shard_map/analysed_a/pallas_call | solution.py:263
  140.3 0.0 copy-start.2
  140.3 1.3 copy-done.2
  141.7 0.0 copy-start.6
  141.7 1.3 copy-done.6
  143.0 15.2 %all-to-all-done.2 = bf16[8,128,1024]{2,1,0:T(8,128)(2,1)} async-done(((bf16[8,128,1024]{2,1,0:T(8,128)(2,1)}), bf16[8,128,1024]{2,1,0:T(8,128)(2,1)}, u32[]{:S(2)}, u32[]{:S(2)}) %all-to-all-start.2) | async-done | bytes 2097184 | tf_op jit(solution)/shard_map/all_to_all | solution.py:300
  158.2 6.9 %all-to-all-start.4 = ((bf16[8,128,1024]{2,1,0:T(8,128)(2,1)}), bf16[8,128,1024]{2,1,0:T(8,128)(2,1)S(1)}, u32[]{:S(2)}, u32[]{:S(2)}) async-start(bf16[8,128,1024]{2,1,0:T(8,128)(2,1)} %bitcast.16), calls=%async_computation.4 | async-start | bytes 4194304 | tf_op jit(solution)/shard_map/all_to_all | solution.py:300
  165.1 0.0 copy-start.7
  165.1 1.6 copy-done.7
  166.7 5.1 %analysed_b.1 = bf16[1024,1024]{1,0:T(8,128)(2,1)S(1)} custom-call(bf16[1024,1024]{1,0:T(8,128)(2,1)S(1)} %copy-done.7, bf16[1024,1024]{1,0:T(8,128)(2,1)} %bitcast.9.state_ref), custom_call_target="tpu_custom_call" | custom-call | flops 2147483648 | bytes 6291456 | tf_op jit(solution)/shard_map/analysed_b/pallas_call | solution.py:263
  171.8 0.0 copy-start.3
  171.8 1.3 copy-done.3
  173.1 38.6 %all-to-all-done.4.part_ref = bf16[8,128,1024]{2,1,0:T(8,128)(2,1)S(1)} async-done(((bf16[8,128,1024]{2,1,0:T(8,128)(2,1)}), bf16[8,128,1024]{2,1,0:T(8,128)(2,1)S(1)}, u32[]{:S(2)}, u32[]{:S(2)}) %all-to-all-start.4) | async-done | bytes 2097184 | tf_op jit(solution)/shard_map/all_to_all | solution.py:300
  211.7 5.8 %all-to-all-start.3 = ((bf16[8,128,1024]{2,1,0:T(8,128)(2,1)}), bf16[8,128,1024]{2,1,0:T(8,128)(2,1)}, u32[]{:S(2)}, u32[]{:S(2)}) async-start(bf16[8,128,1024]{2,1,0:T(8,128)(2,1)} %bitcast.17), calls=%async_computation.3 | async-start | bytes 4194304 | tf_op jit(solution)/shard_map/all_to_all | solution.py:300
  217.6 2.1 analysis_a.1.refs_0_
  219.7 44.4 %all-to-all-done.3.part_ref = bf16[8,128,1024]{2,1,0:T(8,128)(2,1)} async-done(((bf16[8,128,1024]{2,1,0:T(8,128)(2,1)}), bf16[8,128,1024]{2,1,0:T(8,128)(2,1)}, u32[]{:S(2)}, u32[]{:S(2)}) %all-to-all-start.3) | async-done | bytes 2097184 | tf_op jit(solution)/shard_map/all_to_all | solution.py:300
  264.1 4.0 %analysis_b.1 = bf16[128,8,2048]{2,1,0:T(8,128)(2,1)} custom-call(bf16[8,128,1024]{2,1,0:T(8,128)(2,1)} %all-to-all-done.3.part_ref, bf16[128,8,2048]{2,1,0:T(8,128)(2,1)} %analysis_a.1.refs_0_), custom_call_target="tpu_custom_call", output_to_operand_aliasing={{}: (1, {})} | custom-call | bytes 4194304 | tf_op jit(solution)/shard_map/analysis_b/pallas_call | solution.py:135
  (1 shorter events, 0.0 us)
Async XLA Ops:
  4.0 67.2 %all-to-all-start = ((bf16[8,128,1024]{2,1,0:T(8,128)(2,1)}), bf16[8,128,1024]{2,1,0:T(8,128)(2,1)S(1)}, u32[]{:S(2)}, u32[]{:S(2)}) async-start(bf16[8,128,1024]{2,1,0:T(8,128)(2,1)} %state_a.1), calls=%async_computation | async-start | bytes 4194304 | tf_op jit(solution)/shard_map/all_to_all | solution.py:300
  9.7 39.0 %copy-start.4 = (s32[1,8,1024]{2,1,0:T(8,128)S(1)}, s32[1,8,1024]{2,1,0:T(8,128)}, u32[]{:S(2)}) copy-start(s32[1,8,1024]{2,1,0:T(8,128)} %param.9) | copy-start | bytes 98308
  13.8 30.3 %collective-permute-start = (bf16[8,144,1024]{2,1,0:T(8,128)(2,1)}, bf16[8,144,1024]{2,1,0:T(8,128)(2,1)S(1)}, u32[]{:S(2)}, u32[]{:S(2)}) collective-permute-start(bf16[8,144,1024]{2,1,0:T(8,128)(2,1)} %pool_rows.1.own_ref), channel_id=1, source_target_pairs={{0,1},{1,2},{2,3},{4,5},{5,6},{6,7},{8,9},{9,10},{10,11},{12,13},{... | collective-permute-start | bytes 7077896 | tf_op jit(solution)/shard_map/ppermute | solution.py:308
  18.0 30.7 %collective-permute-start.1 = (bf16[8,144,1024]{2,1,0:T(8,128)(2,1)}, bf16[8,144,1024]{2,1,0:T(8,128)(2,1)S(1)}, u32[]{:S(2)}, u32[]{:S(2)}) collective-permute-start(bf16[8,144,1024]{2,1,0:T(8,128)(2,1)} %pool_rows.1.own_ref), channel_id=1, source_target_pairs={{1,0},{2,1},{3,2},{5,4},{6,5},{7,6},{9,8},{10,9},{11,10},{13,12},{... | collective-permute-start | bytes 7077896 | tf_op jit(solution)/shard_map/ppermute | solution.py:309
  48.7 1.7 copy-start
  69.9 1.3 copy-start.1
  71.2 39.1 %all-to-all-start.1 = ((bf16[8,128,1024]{2,1,0:T(8,128)(2,1)}), bf16[8,128,1024]{2,1,0:T(8,128)(2,1)}, u32[]{:S(2)}, u32[]{:S(2)}) async-start(bf16[8,128,1024]{2,1,0:T(8,128)(2,1)} %copy-done.1), calls=%async_computation.1 | async-start | bytes 4194304 | tf_op jit(solution)/shard_map/all_to_all | solution.py:300
  80.6 37.0 %copy-start.5 = (f32[1,1,1024]{2,1,0:T(1,128)S(1)}, f32[1,1,1024]{2,1,0:T(1,128)}, u32[]{:S(2)}) copy-start(f32[1,1,1024]{2,1,0:T(1,128)} %param.11) | copy-start | bytes 12292
  110.3 47.9 %all-to-all-start.2 = ((bf16[8,128,1024]{2,1,0:T(8,128)(2,1)}), bf16[8,128,1024]{2,1,0:T(8,128)(2,1)}, u32[]{:S(2)}, u32[]{:S(2)}) async-start(bf16[8,128,1024]{2,1,0:T(8,128)(2,1)} %state_b.1), calls=%async_computation.2 | async-start | bytes 4194304 | tf_op jit(solution)/shard_map/all_to_all | solution.py:300
  140.3 1.4 copy-start.2
  141.7 1.3 copy-start.6
  158.2 53.5 %all-to-all-start.4 = ((bf16[8,128,1024]{2,1,0:T(8,128)(2,1)}), bf16[8,128,1024]{2,1,0:T(8,128)(2,1)S(1)}, u32[]{:S(2)}, u32[]{:S(2)}) async-start(bf16[8,128,1024]{2,1,0:T(8,128)(2,1)} %bitcast.16), calls=%async_computation.4 | async-start | bytes 4194304 | tf_op jit(solution)/shard_map/all_to_all | solution.py:300
  165.1 1.6 copy-start.7
  171.8 1.3 copy-start.3
  211.7 52.4 %all-to-all-start.3 = ((bf16[8,128,1024]{2,1,0:T(8,128)(2,1)}), bf16[8,128,1024]{2,1,0:T(8,128)(2,1)}, u32[]{:S(2)}, u32[]{:S(2)}) async-start(bf16[8,128,1024]{2,1,0:T(8,128)(2,1)} %bitcast.17), calls=%async_computation.3 | async-start | bytes 4194304 | tf_op jit(solution)/shard_map/all_to_all | solution.py:300

commit v5 on v4

--- a/solution.py
+++ b/solution.py
@@ -43,11 +43,13 @@
     )(obs, innov)
 
 
-def gather_kernel(own_ref, up_ref, down_ref, idx_ref, out_ref, inn_ref):
-    block = pl.program_id(0)
+def gather_kernel(first, place_ref, own_ref, up_ref, down_ref, idx_ref, out_ref, *inn_refs):
+    block = (pl.program_id(0) + first) ^ place_ref[0]
     blocks, rows, depth = own_ref.shape
     members = out_ref.shape[1]
     slots = out_ref.shape[2]
+    if not inn_refs:
+        rows = members
     west = jnp.maximum(block - 1, 0)
     east = jnp.minimum(block + 1, blocks - 1)
     sources = (
@@ -69,36 +71,39 @@
             if live is not None:
                 local = jnp.where(live, local, -1)
             one_hot = jnp.where(columns == local, 1.0, 0.0).astype(jnp.bfloat16)
-            acc += jnp.dot(ref[at], one_hot, preferred_element_type=jnp.float32)
+            acc += jnp.dot(ref[at, :rows], one_hot, preferred_element_type=jnp.float32)
         out_ref[0, :, where] = acc[:members].astype(jnp.bfloat16)
-        inn_ref[0, :, where] = acc[members:].astype(jnp.bfloat16)
-
-
-def gather_chosen(own, up, down, picks):
+        for inn_ref in inn_refs:
+
+            @pl.when(pl.program_id(0) == 0)
+            def _():
+                inn_ref[:, where] = acc[members:].astype(jnp.bfloat16)
+
+
+def gather_chosen(place, own, up, down, picks, first, count, name):
     blocks, rows, depth = own.shape
     members = rows - INNOV_ROWS
     slots = picks.shape[1]
     vmem = pl.BlockSpec(memory_space=pltpu.VMEM)
-    return pl.pallas_call(
-        gather_kernel,
-        grid=(blocks,),
-        in_specs=[vmem] * 4,
-        out_specs=[
-            pl.BlockSpec((1, members, slots), lambda b: (b, 0, 0)),
-            pl.BlockSpec((1, INNOV_ROWS, slots), lambda b: (b, 0, 0)),
-        ],
-        out_shape=[
-            jax.ShapeDtypeStruct((blocks, members, slots), jnp.bfloat16),
-            jax.ShapeDtypeStruct((blocks, INNOV_ROWS, slots), jnp.bfloat16),
-        ],
+    out_specs = [pl.BlockSpec((1, members, slots), lambda k: (k, 0, 0))]
+    out_shape = [jax.ShapeDtypeStruct((count, members, slots), jnp.bfloat16)]
+    if first == 0:
+        out_specs.append(pl.BlockSpec((INNOV_ROWS, slots), lambda k: (0, 0)))
+        out_shape.append(jax.ShapeDtypeStruct((INNOV_ROWS, slots), jnp.bfloat16))
+    return pl.pallas_call(
+        functools.partial(gather_kernel, first),
+        grid=(count,),
+        in_specs=[pl.BlockSpec(memory_space=pltpu.SMEM)] + [vmem] * 4,
+        out_specs=out_specs,
+        out_shape=out_shape,
         compiler_params=pltpu.CompilerParams(vmem_limit_bytes=40 * MIB),
         cost_estimate=pl.CostEstimate(
-            flops=2 * blocks * rows * depth * 5 * slots,
-            bytes_accessed=2 * blocks * rows * (3 * depth + slots),
+            flops=0,
+            bytes_accessed=rows * slots,
             transcendentals=0,
         ),
-        name="gather_chosen",
-    )(own, up, down, picks)
+        name=name,
+    )(place, own, up, down, picks)
 
 
 def to_blocks_kernel(in_ref, out_ref):
@@ -129,30 +134,60 @@
     refs[-1][...] = jnp.swapaxes(part_ref[...], 0, 1)
 
 
+def pairs_to_members_kernel(place_ref, *refs):
+    *part_refs, out_ref, stage = refs
+    for number, ref in enumerate(part_refs):
+        stage[place_ref[0] ^ number] = ref[...]
+    out_ref[...] = jnp.swapaxes(stage[...], 0, 1)
+
+
 def to_members(part, start, entries, whole, name):
     blocks, members, width = part.shape
-    before = [] if whole is None else [whole]
     return pl.pallas_call(
         to_members_kernel,
         grid=(members // MEMBER_TILE,),
-        in_specs=[pl.BlockSpec((blocks, MEMBER_TILE, width), lambda i: (0, i, 0))]
-        + [pl.BlockSpec(memory_space=pl.ANY)] * len(before),
+        in_specs=[
+            pl.BlockSpec((blocks, MEMBER_TILE, width), lambda i: (0, i, 0)),
+            pl.BlockSpec(memory_space=pl.ANY),
+        ],
         out_specs=pl.BlockSpec((MEMBER_TILE, blocks, width), lambda i: (i, 0, start // width)),
         out_shape=jax.ShapeDtypeStruct((members, blocks, entries), part.dtype),
-        input_output_aliases={1: 0} if before else {},
+        input_output_aliases={1: 0},
         compiler_params=pltpu.CompilerParams(vmem_limit_bytes=32 * MIB),
         cost_estimate=pl.CostEstimate(
             flops=0, bytes_accessed=4 * members * blocks * width, transcendentals=0
         ),
         name=name,
-    )(part, *before)
-
-
-def transform_kernel(
-    tally_ref, weight_ref, innov_ref, obs_ref, out_ref,
-    weighted, precision, root, step, root_next, step_next, inverse,
-):
+    )(part, whole)
+
+
+def pairs_to_members(place, parts, start, entries, name):
+    blocks = len(parts)
+    members, width = parts[0].shape
+    return pl.pallas_call(
+        pairs_to_members_kernel,
+        grid=(members // MEMBER_TILE,),
+        in_specs=[pl.BlockSpec(memory_space=pltpu.SMEM)]
+        + [pl.BlockSpec((MEMBER_TILE, width), lambda i: (i, 0))] * blocks,
+        out_specs=pl.BlockSpec((MEMBER_TILE, blocks, width), lambda i: (i, 0, start // width)),
+        out_shape=jax.ShapeDtypeStruct((members, blocks, entries), parts[0].dtype),
+        scratch_shapes=[pltpu.VMEM((blocks, MEMBER_TILE, width), parts[0].dtype)],
+        compiler_params=pltpu.CompilerParams(vmem_limit_bytes=32 * MIB),
+        cost_estimate=pl.CostEstimate(
+            flops=0, bytes_accessed=4 * members * blocks * width, transcendentals=0
+        ),
+        name=name,
+    )(place, *parts)
+
+
+def transform_kernel(place_ref, tally_ref, weight_ref, innov_ref, *refs):
+    *part_refs, out_ref, obs_ref = refs[:-7]
+    weighted, precision, root, step, root_next, step_next, inverse = refs[-7:]
     count_k, slots = obs_ref.shape
+    members = count_k // len(part_refs)
+    for number, ref in enumerate(part_refs):
+        at = pl.multiple_of((place_ref[0] ^ number) * members, members)
+        obs_ref[pl.ds(at, members), :] = ref[...]
     spare = count_k - 1.0
     chunks = count_k // TRANSFORM_CHUNK
     live = lax.broadcasted_iota(jnp.int32, (1, slots), 1) < tally_ref[0, 0]
@@ -225,50 +260,61 @@
     ).astype(jnp.bfloat16)
 
 
-def ensemble_transform(tally, weight, innov, obs_rows):
-    count_k, slots = obs_rows.shape
+def ensemble_transform(place, tally, weight, innov, parts):
+    members, slots = parts[0].shape
+    count_k = members * len(parts)
     vmem = pl.BlockSpec(memory_space=pltpu.VMEM)
     square = pltpu.VMEM((count_k, count_k), jnp.bfloat16)
     return pl.pallas_call(
         transform_kernel,
-        in_specs=[pl.BlockSpec(memory_space=pltpu.SMEM), vmem, vmem, vmem],
+        in_specs=[pl.BlockSpec(memory_space=pltpu.SMEM)] * 2 + [vmem] * (2 + len(parts)),
         out_specs=vmem,
         out_shape=jax.ShapeDtypeStruct((count_k, count_k), jnp.bfloat16),
         scratch_shapes=[
             pltpu.VMEM((count_k, slots), jnp.bfloat16),
+            pltpu.VMEM((count_k, slots), jnp.bfloat16),
             pltpu.VMEM((count_k, count_k), jnp.float32),
             square, square, square, square, square,
         ],
         compiler_params=pltpu.CompilerParams(vmem_limit_bytes=40 * MIB),
         cost_estimate=pl.CostEstimate(
-            flops=2 * count_k * count_k * (slots + 3 * count_k),
-            bytes_accessed=4 * count_k * (slots + count_k),
+            flops=0,
+            bytes_accessed=count_k * slots,
             transcendentals=0,
         ),
         name="transform",
-    )(tally, weight, innov, obs_rows)
-
-
-def analysis_kernel(transform_ref, state_ref, out_ref):
+    )(place, tally, weight, innov, *parts)
+
+
+def analysis_kernel(in_pairs, place_ref, transform_ref, state_ref, out_ref, stage):
+    blocks, members, width = out_ref.shape
     state = state_ref[...].astype(jnp.float32)
     state_mean = jnp.sum(state, axis=0, keepdims=True) * (1.0 / state.shape[0])
     perturb = (state - state_mean).astype(jnp.bfloat16)
     increment = jnp.dot(transform_ref[...], perturb, preferred_element_type=jnp.float32)
-    out_ref[...] = (state_mean + increment).astype(jnp.bfloat16)
-
-
-def analysed(transform, part, name):
+    result = (state_mean + increment).astype(jnp.bfloat16).reshape(out_ref.shape)
+    if in_pairs:
+        stage[...] = result
+        for number in range(blocks):
+            out_ref[number] = stage[place_ref[0] ^ number]
+    else:
+        out_ref[...] = result
+
+
+def analysed(place, transform, part, in_pairs, name):
     blocks, members, width = part.shape
     count_k = blocks * members
-    out = pl.pallas_call(
-        analysis_kernel,
+    return pl.pallas_call(
+        functools.partial(analysis_kernel, in_pairs),
         grid=(width // ANALYSIS_TILE,),
         in_specs=[
+            pl.BlockSpec(memory_space=pltpu.SMEM),
             pl.BlockSpec(memory_space=pltpu.VMEM),
             pl.BlockSpec((count_k, ANALYSIS_TILE), lambda i: (0, i)),
         ],
-        out_specs=pl.BlockSpec((count_k, ANALYSIS_TILE), lambda i: (0, i)),
-        out_shape=jax.ShapeDtypeStruct((count_k, width), jnp.bfloat16),
+        out_specs=pl.BlockSpec((blocks, members, ANALYSIS_TILE), lambda i: (0, 0, i)),
+        out_shape=jax.ShapeDtypeStruct(part.shape, jnp.bfloat16),
+        scratch_shapes=[pltpu.VMEM((blocks, members, ANALYSIS_TILE), jnp.bfloat16)],
         compiler_params=pltpu.CompilerParams(vmem_limit_bytes=32 * MIB),
         cost_estimate=pl.CostEstimate(
             flops=2 * count_k * count_k * width,
@@ -276,8 +322,7 @@
             transcendentals=0,
         ),
         name=name,
-    )(transform, part.reshape(count_k, width))
-    return out.reshape(part.shape)
+    )(place, transform, part.reshape(count_k, width))
 
 
 def body(
@@ -288,17 +333,20 @@
     active_measure_tally,
     tapered_error_weight,
 ):
-    place = lax.axis_index("mem")
+    place = lax.axis_index("mem").astype(jnp.int32).reshape(1)
     strips = lax.axis_size("reg")
-    blocks = prior_members_field.shape[2]
+    devices = lax.axis_size("mem")
     entries = prior_members_field.shape[3]
-    use_count = measure_pool_indices.shape[2]
     to_next = [(i, i + 1) for i in range(strips - 1)]
     to_last = [(i + 1, i) for i in range(strips - 1)]
 
     def exchange(x):
         return lax.all_to_all(x, "mem", split_axis=0, concat_axis=0, tiled=True)
 
+    def swap(x, number):
+        return lax.ppermute(x, "mem", [(i, i ^ number) for i in range(devices)])
+
+    half = devices // 2
     quarter = entries // 4
     state = prior_members_field[:, 0]
     state_a = to_blocks(state, 0, 2 * quarter, "state_a")
@@ -307,21 +355,22 @@
     pool = pool_rows(devs, measured_minus_predicted[0])
     up = lax.ppermute(pool, "reg", to_next)
     down = lax.ppermute(pool, "reg", to_last)
-    chosen, chosen_innov = gather_chosen(pool, up, down, measure_pool_indices[0])
-    chosen, state_a = lax.optimization_barrier((chosen, state_a))
-    obs_rows = exchange(chosen)
+    picks = measure_pool_indices[0]
+    far = gather_chosen(place, pool, up, down, picks, half, half, "gather_far")[0]
+    far = [swap(far[k], k + half) for k in range(half)]
+    near, innov = gather_chosen(place, pool, up, down, picks, 0, half, "gather_near")
+    near = [near[0]] + [swap(near[k], k) for k in range(1, half)]
     state_b = to_blocks(state, 2 * quarter, 2 * quarter, "state_b")
-    obs_rows, state_b = lax.optimization_barrier((obs_rows, state_b))
+    state_b, state_a, near, far = lax.optimization_barrier((state_b, state_a, near, far))
     state_b = exchange(state_b)
-    innov_rows = lax.dynamic_index_in_dim(chosen_innov, place, 0, keepdims=False)
     transform = ensemble_transform(
-        active_measure_tally, tapered_error_weight[0], innov_rows, obs_rows.reshape(-1, use_count)
+        place, active_measure_tally, tapered_error_weight[0], innov, near + far
     )
-    done_a = analysed(transform, state_a, "analysed_a")
+    done_a = analysed(place, transform, state_a, True, "analysed_a")
     done_a, state_b = lax.optimization_barrier((done_a, state_b))
-    done_a = exchange(done_a)
-    done_b = exchange(analysed(transform, state_b, "analysed_b"))
-    whole = to_members(done_a, 0, entries, None, "analysis_a")
+    done_a = [done_a[0]] + [swap(done_a[k], k) for k in range(1, devices)]
+    done_b = exchange(analysed(place, transform, state_b, False, "analysed_b"))
+    whole = pairs_to_members(place, done_a, 0, entries, "analysis_a")
     whole = to_members(done_b, 2 * quarter, entries, whole, "analysis_b")
     return whole[:, None]
 

time: 272 us -> 255 us (0.938); the launches traced: 268 us -> 254 us
  waiting for transfers between devices: 157 us -> 135 us
  local copies, waits for them, and re-layouts: 8.58 us -> 14.8 us
    all_to_all x5 -> x3, waiting for transfers between devices: 128 us -> 6.28 us  [exchange(): return lax.all_to_all(x, 'mem', split_axis=0, concat_axis=0, tiled=True)]
    ppermute x0 -> x14, waiting for transfers between devices: none -> 100 us  [swap(): return lax.ppermute(x, 'mem', [(i, i ^ number) for i in range(devices)])]
    ppermute x0 -> x14, starting transfers between devices: none -> 16.7 us  [swap(): return lax.ppermute(x, 'mem', [(i, i ^ number) for i in range(devices)])]
    all_to_all x5 -> x3, starting transfers between devices: 30.6 us -> 15.8 us  [exchange(): return lax.all_to_all(x, 'mem', split_axis=0, concat_axis=0, tiled=True)]
    pallas_call x3 -> x5, Pallas kernels: 28.8 us -> 33.5 us  [the longest x2 21.9 us: gather_chosen(): pl.pallas_call(functools.partial(gather_kernel, first), grid=(count,), in...]
    pallas_call x2 -> x1, Pallas kernels: 6.1 us -> 2.14 us  [to_members(): pl.pallas_call(to_members_kernel, grid=(members // MEMBER_TILE,), in_spec...]
    unnamed x16 -> x26, local copies, waits for them, and re-layouts: 8.57 us -> 12.2 us
  transfers between devices with their start and end apart: 7 -> 19, of which waited for: 6 -> 13; matrix products, arithmetic and copies ran while one was open for 0% -> 1% of each run, Pallas kernels for 21% -> 21%
where the time goes in v5:
time: 255 us; the launch traced here: 254 us
  waiting for transfers between devices  135 us (53%)
  Pallas kernels  64.7 us (25%)
  starting transfers between devices  38.7 us (15%)
  local copies, waits for them, and re-layouts  14.8 us (6%)
    ppermute x14, waiting for transfers between devices, swap(): return lax.ppermute(x, 'mem', [(i, i ^ number) for i in range(devices)])  100 us
    ppermute x1, waiting for transfers between devices, body(): up = lax.ppermute(pool, 'reg', to_next)  24.1 us
    pallas_call x2, Pallas kernels, gather_chosen(): pl.pallas_call(functools.partial(gather_kernel, first), grid=(count,), in...  21.9 us
    pallas_call x1, Pallas kernels, ensemble_transform(): pl.pallas_call(transform_kernel, in_specs=[pl.BlockSpec(memory_space=pltp...  16.9 us
    ppermute x14, starting transfers between devices, swap(): return lax.ppermute(x, 'mem', [(i, i ^ number) for i in range(devices)])  16.7 us
    all_to_all x3, starting transfers between devices, exchange(): return lax.all_to_all(x, 'mem', split_axis=0, concat_axis=0, tiled=True)  15.8 us
    unnamed x26, local copies, waits for them, and re-layouts  12.2 us
    pallas_call x2, Pallas kernels, analysed(): pl.pallas_call(functools.partial(analysis_kernel, in_pairs), grid=(width...  9.43 us
  transfers between devices with their start and end apart: 19, of which 13 were waited for; matrix products, arithmetic and copies ran while one was open for 1% of the time, Pallas kernels for 21%

profile of v5, /device:TPU:9, one launch (start us, length us, event | category | flops | bytes accessed | tf_op | source)
XLA Modules:
  0.0 254.3 jit_solution(4114516772064737610)
XLA Ops:
  0.0 4.1 %state_a.1 = bf16[8,128,1024]{2,1,0:T(8,128)(2,1)} custom-call(bf16[128,8,2048]{2,1,0:T(8,128)(2,1)} %bitcast.47), custom_call_target="tpu_custom_call" | custom-call | bytes 4194304 | tf_op jit(solution)/shard_map/state_a/pallas_call | solution.py:115
  4.1 5.7 %all-to-all-start = ((bf16[8,128,1024]{2,1,0:T(8,128)(2,1)}), bf16[8,128,1024]{2,1,0:T(8,128)(2,1)}, u32[]{:S(2)}, u32[]{:S(2)}) async-start(bf16[8,128,1024]{2,1,0:T(8,128)(2,1)} %state_a.1), calls=%async_computation | async-start | bytes 4194304 | tf_op jit(solution)/shard_map/all_to_all | solution.py:344
  9.8 4.1 %pool_rows.1.own_ref = bf16[8,144,1024]{2,1,0:T(8,128)(2,1)} custom-call(bf16[128,8,1024]{2,1,0:T(8,128)(2,1)} %bitcast.49, bf16[8,1024]{1,0:T(8,128)(2,1)} %bitcast.50), custom_call_target="tpu_custom_call" | custom-call | bytes 4718592 | tf_op jit(solution)/shard_map/pool_rows/pallas_call | solution.py:29
  13.9 4.2 %collective-permute-start = (bf16[8,144,1024]{2,1,0:T(8,128)(2,1)}, bf16[8,144,1024]{2,1,0:T(8,128)(2,1)S(1)}, u32[]{:S(2)}, u32[]{:S(2)}) collective-permute-start(bf16[8,144,1024]{2,1,0:T(8,128)(2,1)} %pool_rows.1.own_ref), channel_id=1, source_target_pairs={{0,1},{1,2},{2,3},{4,5},{5,6},{6,7},{8,9},{9,10},{10,11},{12,13},{... | collective-permute-start | bytes 7077896 | tf_op jit(solution)/shard_map/ppermute | solution.py:356
  18.1 1.9 collective-permute-start.1
  20.0 24.1 %collective-permute-done.up_ref = bf16[8,144,1024]{2,1,0:T(8,128)(2,1)S(1)} collective-permute-done((bf16[8,144,1024]{2,1,0:T(8,128)(2,1)}, bf16[8,144,1024]{2,1,0:T(8,128)(2,1)S(1)}, u32[]{:S(2)}, u32[]{:S(2)}) %collective-permute-start) | collective-permute-done | bytes 2359328 | tf_op jit(solution)/shard_map/ppermute | solution.py:356
  44.2 4.7 %collective-permute-done.1.down_ref = bf16[8,144,1024]{2,1,0:T(8,128)(2,1)} collective-permute-done((bf16[8,144,1024]{2,1,0:T(8,128)(2,1)}, bf16[8,144,1024]{2,1,0:T(8,128)(2,1)}, u32[]{:S(2)}, u32[]{:S(2)}) %collective-permute-start.1) | collective-permute-done | bytes 2359328 | tf_op jit(solution)/shard_map/ppermute | solution.py:357
  48.9 1.7 copy-done
  50.5 11.4 %gather_near.1 = (bf16[4,128,1024]{2,1,0:T(8,128)(2,1)S(1)}, bf16[16,1024]{1,0:T(8,128)(2,1)S(1)}) custom-call(s32[1]{0:T(128)} %bitcast.place_ref, bf16[8,144,1024]{2,1,0:T(8,128)(2,1)S(1)} %copy-done, bf16[8,144,1024]{2,1,0:T(8,128)(2,1)S(1)} %collective-permute-done.up_ref, bf16[8,144,1024]{2,1,0:T(8,128)(2,1)} %collective-permute-done.1.down_ref, ...), custom_call_target="tpu_custom_call" | custom-call | bytes 147456 | tf_op jit(solution)/shard_map/gather_near/pallas_call | solution.py:93
  62.0 0.8 slice_bitcast_fusion.12
  62.8 1.0 collective-permute-start.2
  63.7 0.5 collective-permute-start.3
  64.2 1.2 collective-permute-start.4
  65.4 10.5 %gather_far.1 = bf16[4,128,1024]{2,1,0:T(8,128)(2,1)S(1)} custom-call(s32[1]{0:T(128)} %bitcast.place_ref, bf16[8,144,1024]{2,1,0:T(8,128)(2,1)S(1)} %copy-done, bf16[8,144,1024]{2,1,0:T(8,128)(2,1)S(1)} %collective-permute-done.up_ref, bf16[8,144,1024]{2,1,0:T(8,128)(2,1)} %collective-permute-done.1.down_ref, s32[8,1024]{1,0:T(8,128)S(1)} %bitcast.45), custom_call_target="tpu_custom_call" | custom-call | bytes 147456 | tf_op jit(solution)/shard_map/gather_far/pallas_call | solution.py:93
  75.9 0.1 slice_bitcast_fusion
  76.0 2.0 collective-permute-start.5
  78.0 1.1 collective-permute-start.6
  79.1 0.0 collective-permute-done.2.refs_1_
  79.1 1.3 collective-permute-start.7
  80.4 0.0 collective-permute-done.3.refs_2_
  80.4 0.4 collective-permute-start.8
  80.8 4.0 %state_b.1 = bf16[8,128,1024]{2,1,0:T(8,128)(2,1)} custom-call(bf16[128,8,2048]{2,1,0:T(8,128)(2,1)} %bitcast.48), custom_call_target="tpu_custom_call" | custom-call | bytes 4194304 | tf_op jit(solution)/shard_map/state_b/pallas_call | solution.py:115
  84.8 0.0 collective-permute-done.4.refs_3_
  84.8 8.1 %collective-permute-done.5.refs_4_ = bf16[128,1024]{1,0:T(8,128)(2,1)S(1)} collective-permute-done((bf16[128,1024]{1,0:T(8,128)(2,1)S(1)}, bf16[128,1024]{1,0:T(8,128)(2,1)S(1)}, u32[]{:S(2)}, u32[]{:S(2)}) %collective-permute-start.5) | collective-permute-done | bytes 262176 | tf_op jit(solution)/shard_map/ppermute | solution.py:347
  93.0 2.8 %collective-permute-done.6.refs_5_ = bf16[128,1024]{1,0:T(8,128)(2,1)S(1)} collective-permute-done((bf16[128,1024]{1,0:T(8,128)(2,1)S(1)}, bf16[128,1024]{1,0:T(8,128)(2,1)S(1)}, u32[]{:S(2)}, u32[]{:S(2)}) %collective-permute-start.6) | collective-permute-done | bytes 262176 | tf_op jit(solution)/shard_map/ppermute | solution.py:347
  95.8 0.7 copy-done.5
  96.5 2.9 %collective-permute-done.7.refs_6_ = bf16[128,1024]{1,0:T(8,128)(2,1)S(1)} collective-permute-done((bf16[128,1024]{1,0:T(8,128)(2,1)S(1)}, bf16[128,1024]{1,0:T(8,128)(2,1)S(1)}, u32[]{:S(2)}, u32[]{:S(2)}) %collective-permute-start.7) | collective-permute-done | bytes 262176 | tf_op jit(solution)/shard_map/ppermute | solution.py:347
  99.3 0.7 copy-done.7
  100.0 7.6 %collective-permute-done.8.refs_7_ = bf16[128,1024]{1,0:T(8,128)(2,1)S(1)} collective-permute-done((bf16[128,1024]{1,0:T(8,128)(2,1)S(1)}, bf16[128,1024]{1,0:T(8,128)(2,1)S(1)}, u32[]{:S(2)}, u32[]{:S(2)}) %collective-permute-start.8) | collective-permute-done | bytes 262176 | tf_op jit(solution)/shard_map/ppermute | solution.py:347
  107.6 0.7 copy-done.9
  108.3 0.0 all-to-all-done
  108.3 4.9 %all-to-all-start.1 = ((bf16[8,128,1024]{2,1,0:T(8,128)(2,1)}), bf16[8,128,1024]{2,1,0:T(8,128)(2,1)S(1)}, u32[]{:S(2)}, u32[]{:S(2)}) async-start(bf16[8,128,1024]{2,1,0:T(8,128)(2,1)} %state_b.1), calls=%async_computation.1 | async-start | bytes 4194304 | tf_op jit(solution)/shard_map/all_to_all | solution.py:344
  113.9 0.0 copy-done.12
  113.9 0.0 copy-start.6
  113.9 0.9 copy-done.6
  114.9 0.9 copy-done.8
  115.8 0.9 copy-done.10
  116.8 16.9 %transform.1.transform_ref = bf16[1024,1024]{1,0:T(8,128)(2,1)S(1)} custom-call(s32[1]{0:T(128)} %bitcast.place_ref, s32[1,1]{1,0:T(1,128)S(6)} %copy.10.tally_ref, f32[1,1024]{1,0:T(1,128)S(1)} %bitcast.46, bf16[16,1024]{1,0:T(8,128)(2,1)S(1)} %get-tuple-element.22.innov_ref, bf16[128,1024]{1,0:T(8,128)(2,1)S(1)} %get-tuple-element.25.refs_0_, ...), custom_call_target="tpu_custom_call" | custom-call | bytes 1048576 | tf_op jit(solution)/shard_map/transform/pallas_call | solution.py:268
  133.7 5.2 %analysed_a.1 = bf16[8,128,1024]{2,1,0:T(8,128)(2,1)S(1)} custom-call(s32[1]{0:T(128)} %bitcast.place_ref, bf16[1024,1024]{1,0:T(8,128)(2,1)S(1)} %transform.1.transform_ref, bf16[1024,1024]{1,0:T(8,128)(2,1)} %bitcast.14.state_ref), custom_call_target="tpu_custom_call" | custom-call | flops 2147483648 | bytes 6291456 | tf_op jit(solution)/shard_map/analysed_a/pallas_call | solution.py:307
  138.9 1.3 copy-done.2
  140.2 1.3 copy-done.3
  141.6 6.3 %all-to-all-done.1 = bf16[8,128,1024]{2,1,0:T(8,128)(2,1)S(1)} async-done(((bf16[8,128,1024]{2,1,0:T(8,128)(2,1)}), bf16[8,128,1024]{2,1,0:T(8,128)(2,1)S(1)}, u32[]{:S(2)}, u32[]{:S(2)}) %all-to-all-start.1) | async-done | bytes 2097184 | tf_op jit(solution)/shard_map/all_to_all | solution.py:344
  147.8 1.6 copy-done.4
  149.4 4.2 %analysed_b.1 = bf16[8,128,1024]{2,1,0:T(8,128)(2,1)S(1)} custom-call(s32[1]{0:T(128)} %bitcast.place_ref, bf16[1024,1024]{1,0:T(8,128)(2,1)S(1)} %copy-done.4, bf16[1024,1024]{1,0:T(8,128)(2,1)S(1)} %bitcast.43), custom_call_target="tpu_custom_call" | custom-call | flops 2147483648 | bytes 6291456 | tf_op jit(solution)/shard_map/analysed_b/pallas_call | solution.py:307
  153.7 1.4 copy-done.1
  155.0 5.2 %all-to-all-start.2 = ((bf16[8,128,1024]{2,1,0:T(8,128)(2,1)}), bf16[8,128,1024]{2,1,0:T(8,128)(2,1)S(1)}, u32[]{:S(2)}, u32[]{:S(2)}) async-start(bf16[8,128,1024]{2,1,0:T(8,128)(2,1)} %copy-done.1), calls=%async_computation.2 | async-start | bytes 4194304 | tf_op jit(solution)/shard_map/all_to_all | solution.py:344
  160.2 1.7 slice_bitcast_fusion.4
  161.9 0.1 collective-permute-start.10
  162.0 2.4 collective-permute-start.11
  164.4 2.1 collective-permute-start.12
  166.5 0.3 collective-permute-start.13
  166.7 1.2 collective-permute-start.14
  167.9 33.2 %collective-permute-done.10.refs_2_ = bf16[128,1024]{1,0:T(8,128)(2,1)S(1)} collective-permute-done((bf16[128,1024]{1,0:T(8,128)(2,1)S(1)}, bf16[128,1024]{1,0:T(8,128)(2,1)S(1)}, u32[]{:S(2)}, u32[]{:S(2)}) %collective-permute-start.10) | collective-permute-done | bytes 262176 | tf_op jit(solution)/shard_map/ppermute | solution.py:347
  201.1 3.3 %collective-permute-start.15 = (bf16[128,1024]{1,0:T(8,128)(2,1)S(1)}, bf16[128,1024]{1,0:T(8,128)(2,1)S(1)}, u32[]{:S(2)}, u32[]{:S(2)}) collective-permute-start(bf16[128,1024]{1,0:T(8,128)(2,1)S(1)} %get-tuple-element.37), channel_id=1, source_target_pairs={{0,28},{4,24},{8,20},{12,16},{16,12},{20,8},{24,4},{28,0},{1,29},{... | collective-permute-start | bytes 786440 | tf_op jit(solution)/shard_map/ppermute | solution.py:347
  204.4 3.5 %collective-permute-done.11.refs_3_ = bf16[128,1024]{1,0:T(8,128)(2,1)S(1)} collective-permute-done((bf16[128,1024]{1,0:T(8,128)(2,1)S(1)}, bf16[128,1024]{1,0:T(8,128)(2,1)S(1)}, u32[]{:S(2)}, u32[]{:S(2)}) %collective-permute-start.11) | collective-permute-done | bytes 262176 | tf_op jit(solution)/shard_map/ppermute | solution.py:347
  207.9 0.0 collective-permute-start.9
  207.9 23.2 %collective-permute-done.12.refs_4_ = bf16[128,1024]{1,0:T(8,128)(2,1)S(1)} collective-permute-done((bf16[128,1024]{1,0:T(8,128)(2,1)S(1)}, bf16[128,1024]{1,0:T(8,128)(2,1)S(1)}, u32[]{:S(2)}, u32[]{:S(2)}) %collective-permute-start.12) | collective-permute-done | bytes 262176 | tf_op jit(solution)/shard_map/ppermute | solution.py:347
  231.1 5.6 %collective-permute-done.13.refs_5_ = bf16[128,1024]{1,0:T(8,128)(2,1)S(1)} collective-permute-done((bf16[128,1024]{1,0:T(8,128)(2,1)S(1)}, bf16[128,1024]{1,0:T(8,128)(2,1)S(1)}, u32[]{:S(2)}, u32[]{:S(2)}) %collective-permute-start.13) | collective-permute-done | bytes 262176 | tf_op jit(solution)/shard_map/ppermute | solution.py:347
  236.7 10.4 %collective-permute-done.14.refs_6_ = bf16[128,1024]{1,0:T(8,128)(2,1)S(1)} collective-permute-done((bf16[128,1024]{1,0:T(8,128)(2,1)S(1)}, bf16[128,1024]{1,0:T(8,128)(2,1)S(1)}, u32[]{:S(2)}, u32[]{:S(2)}) %collective-permute-start.14) | collective-permute-done | bytes 262176 | tf_op jit(solution)/shard_map/ppermute | solution.py:347
  247.1 2.9 %collective-permute-done.15.refs_7_ = bf16[128,1024]{1,0:T(8,128)(2,1)S(1)} collective-permute-done((bf16[128,1024]{1,0:T(8,128)(2,1)S(1)}, bf16[128,1024]{1,0:T(8,128)(2,1)S(1)}, u32[]{:S(2)}, u32[]{:S(2)}) %collective-permute-start.15) | collective-permute-done | bytes 262176 | tf_op jit(solution)/shard_map/ppermute | solution.py:347
  250.0 0.0 collective-permute-done.9.refs_1_
  250.0 2.2 analysis_a.1.refs_0_
  252.1 0.0 all-to-all-done.2.part_ref
  252.1 2.1 analysis_b.1
  (13 shorter events, 0.0 us)
Async XLA Ops:
  4.1 104.3 %all-to-all-start = ((bf16[8,128,1024]{2,1,0:T(8,128)(2,1)}), bf16[8,128,1024]{2,1,0:T(8,128)(2,1)}, u32[]{:S(2)}, u32[]{:S(2)}) async-start(bf16[8,128,1024]{2,1,0:T(8,128)(2,1)} %state_a.1), calls=%async_computation | async-start | bytes 4194304 | tf_op jit(solution)/shard_map/all_to_all | solution.py:344
  9.8 39.1 %copy-start.11 = (s32[1,8,1024]{2,1,0:T(8,128)S(1)}, s32[1,8,1024]{2,1,0:T(8,128)}, u32[]{:S(2)}) copy-start(s32[1,8,1024]{2,1,0:T(8,128)} %param.9) | copy-start | bytes 98308
  13.9 30.3 %collective-permute-start = (bf16[8,144,1024]{2,1,0:T(8,128)(2,1)}, bf16[8,144,1024]{2,1,0:T(8,128)(2,1)S(1)}, u32[]{:S(2)}, u32[]{:S(2)}) collective-permute-start(bf16[8,144,1024]{2,1,0:T(8,128)(2,1)} %pool_rows.1.own_ref), channel_id=1, source_target_pairs={{0,1},{1,2},{2,3},{4,5},{5,6},{6,7},{8,9},{9,10},{10,11},{12,13},{... | collective-permute-start | bytes 7077896 | tf_op jit(solution)/shard_map/ppermute | solution.py:356
  18.1 30.8 %collective-permute-start.1 = (bf16[8,144,1024]{2,1,0:T(8,128)(2,1)}, bf16[8,144,1024]{2,1,0:T(8,128)(2,1)}, u32[]{:S(2)}, u32[]{:S(2)}) collective-permute-start(bf16[8,144,1024]{2,1,0:T(8,128)(2,1)} %pool_rows.1.own_ref), channel_id=1, source_target_pairs={{1,0},{2,1},{3,2},{5,4},{6,5},{7,6},{9,8},{10,9},{11,10},{13,12},{... | collective-permute-start | bytes 7077896 | tf_op jit(solution)/shard_map/ppermute | solution.py:357
  48.9 1.7 copy-start
  62.8 16.3 %collective-permute-start.2 = (bf16[128,1024]{1,0:T(8,128)(2,1)S(1)}, bf16[128,1024]{1,0:T(8,128)(2,1)S(1)}, u32[]{:S(2)}, u32[]{:S(2)}) collective-permute-start(bf16[128,1024]{1,0:T(8,128)(2,1)S(1)} %get-tuple-element.51), channel_id=1, source_target_pairs={{0,4},{4,0},{8,12},{12,8},{16,20},{20,16},{24,28},{28,24},{1,5},{5... | collective-permute-start | bytes 786440 | tf_op jit(solution)/shard_map/ppermute | solution.py:347
  63.7 16.7 %collective-permute-start.3 = (bf16[128,1024]{1,0:T(8,128)(2,1)S(1)}, bf16[128,1024]{1,0:T(8,128)(2,1)S(1)}, u32[]{:S(2)}, u32[]{:S(2)}) collective-permute-start(bf16[128,1024]{1,0:T(8,128)(2,1)S(1)} %get-tuple-element.50), channel_id=1, source_target_pairs={{0,8},{4,12},{8,0},{12,4},{16,24},{20,28},{24,16},{28,20},{1,9},{5... | collective-permute-start | bytes 786440 | tf_op jit(solution)/shard_map/ppermute | solution.py:347
  64.2 20.6 %collective-permute-start.4 = (bf16[128,1024]{1,0:T(8,128)(2,1)}, bf16[128,1024]{1,0:T(8,128)(2,1)S(1)}, u32[]{:S(2)}, u32[]{:S(2)}) collective-permute-start(bf16[128,1024]{1,0:T(8,128)(2,1)} %get-tuple-element.49), channel_id=1, source_target_pairs={{0,12},{4,8},{8,4},{12,0},{16,28},{20,24},{24,20},{28,16},{1,13},{... | collective-permute-start | bytes 786440 | tf_op jit(solution)/shard_map/ppermute | solution.py:347
  76.0 17.0 %collective-permute-start.5 = (bf16[128,1024]{1,0:T(8,128)(2,1)S(1)}, bf16[128,1024]{1,0:T(8,128)(2,1)S(1)}, u32[]{:S(2)}, u32[]{:S(2)}) collective-permute-start(bf16[128,1024]{1,0:T(8,128)(2,1)S(1)} %get-tuple-element.48), channel_id=1, source_target_pairs={{0,16},{4,20},{8,24},{12,28},{16,0},{20,4},{24,8},{28,12},{1,17},{... | collective-permute-start | bytes 786440 | tf_op jit(solution)/shard_map/ppermute | solution.py:347
  78.0 17.7 %collective-permute-start.6 = (bf16[128,1024]{1,0:T(8,128)(2,1)S(1)}, bf16[128,1024]{1,0:T(8,128)(2,1)S(1)}, u32[]{:S(2)}, u32[]{:S(2)}) collective-permute-start(bf16[128,1024]{1,0:T(8,128)(2,1)S(1)} %get-tuple-element.47), channel_id=1, source_target_pairs={{0,20},{4,16},{8,28},{12,24},{16,4},{20,0},{24,12},{28,8},{1,21},{... | collective-permute-start | bytes 786440 | tf_op jit(solution)/shard_map/ppermute | solution.py:347
  79.1 20.2 %collective-permute-start.7 = (bf16[128,1024]{1,0:T(8,128)(2,1)S(1)}, bf16[128,1024]{1,0:T(8,128)(2,1)S(1)}, u32[]{:S(2)}, u32[]{:S(2)}) collective-permute-start(bf16[128,1024]{1,0:T(8,128)(2,1)S(1)} %get-tuple-element.46), channel_id=1, source_target_pairs={{0,24},{4,28},{8,16},{12,20},{16,8},{20,12},{24,0},{28,4},{1,25},{... | collective-permute-start | bytes 786440 | tf_op jit(solution)/shard_map/ppermute | solution.py:347
  80.4 27.2 %collective-permute-start.8 = (bf16[128,1024]{1,0:T(8,128)(2,1)S(1)}, bf16[128,1024]{1,0:T(8,128)(2,1)S(1)}, u32[]{:S(2)}, u32[]{:S(2)}) collective-permute-start(bf16[128,1024]{1,0:T(8,128)(2,1)S(1)} %get-tuple-element.45), channel_id=1, source_target_pairs={{0,28},{4,24},{8,20},{12,16},{16,12},{20,8},{24,4},{28,0},{1,29},{... | collective-permute-start | bytes 786440 | tf_op jit(solution)/shard_map/ppermute | solution.py:347
  95.8 0.7 copy-start.5
  99.3 0.7 copy-start.7
  107.6 0.7 copy-start.9
  108.3 5.6 %copy-start.12 = (f32[1,1,1024]{2,1,0:T(1,128)S(1)}, f32[1,1,1024]{2,1,0:T(1,128)}, u32[]{:S(2)}) copy-start(f32[1,1,1024]{2,1,0:T(1,128)} %param.11) | copy-start | bytes 12292
  108.3 39.5 %all-to-all-start.1 = ((bf16[8,128,1024]{2,1,0:T(8,128)(2,1)}), bf16[8,128,1024]{2,1,0:T(8,128)(2,1)S(1)}, u32[]{:S(2)}, u32[]{:S(2)}) async-start(bf16[8,128,1024]{2,1,0:T(8,128)(2,1)} %state_b.1), calls=%async_computation.1 | async-start | bytes 4194304 | tf_op jit(solution)/shard_map/all_to_all | solution.py:344
  113.9 1.0 copy-start.6
  114.9 0.9 copy-start.8
  115.8 0.9 copy-start.10
  138.9 1.3 copy-start.2
  140.2 1.3 copy-start.3
  147.8 1.6 copy-start.4
  153.7 1.4 copy-start.1
  155.0 97.1 %all-to-all-start.2 = ((bf16[8,128,1024]{2,1,0:T(8,128)(2,1)}), bf16[8,128,1024]{2,1,0:T(8,128)(2,1)S(1)}, u32[]{:S(2)}, u32[]{:S(2)}) async-start(bf16[8,128,1024]{2,1,0:T(8,128)(2,1)} %copy-done.1), calls=%async_computation.2 | async-start | bytes 4194304 | tf_op jit(solution)/shard_map/all_to_all | solution.py:344
  161.9 39.2 %collective-permute-start.10 = (bf16[128,1024]{1,0:T(8,128)(2,1)S(1)}, bf16[128,1024]{1,0:T(8,128)(2,1)S(1)}, u32[]{:S(2)}, u32[]{:S(2)}) collective-permute-start(bf16[128,1024]{1,0:T(8,128)(2,1)S(1)} %get-tuple-element.42), channel_id=1, source_target_pairs={{0,8},{4,12},{8,0},{12,4},{16,24},{20,28},{24,16},{28,20},{1,9},{5... | collective-permute-start | bytes 786440 | tf_op jit(solution)/shard_map/ppermute | solution.py:347
  162.0 45.9 %collective-permute-start.11 = (bf16[128,1024]{1,0:T(8,128)(2,1)S(1)}, bf16[128,1024]{1,0:T(8,128)(2,1)S(1)}, u32[]{:S(2)}, u32[]{:S(2)}) collective-permute-start(bf16[128,1024]{1,0:T(8,128)(2,1)S(1)} %get-tuple-element.41), channel_id=1, source_target_pairs={{0,12},{4,8},{8,4},{12,0},{16,28},{20,24},{24,20},{28,16},{1,13},{... | collective-permute-start | bytes 786440 | tf_op jit(solution)/shard_map/ppermute | solution.py:347
  164.4 66.7 %collective-permute-start.12 = (bf16[128,1024]{1,0:T(8,128)(2,1)S(1)}, bf16[128,1024]{1,0:T(8,128)(2,1)S(1)}, u32[]{:S(2)}, u32[]{:S(2)}) collective-permute-start(bf16[128,1024]{1,0:T(8,128)(2,1)S(1)} %get-tuple-element.40), channel_id=1, source_target_pairs={{0,16},{4,20},{8,24},{12,28},{16,0},{20,4},{24,8},{28,12},{1,17},{... | collective-permute-start | bytes 786440 | tf_op jit(solution)/shard_map/ppermute | solution.py:347
  166.5 70.3 %collective-permute-start.13 = (bf16[128,1024]{1,0:T(8,128)(2,1)S(1)}, bf16[128,1024]{1,0:T(8,128)(2,1)S(1)}, u32[]{:S(2)}, u32[]{:S(2)}) collective-permute-start(bf16[128,1024]{1,0:T(8,128)(2,1)S(1)} %get-tuple-element.39), channel_id=1, source_target_pairs={{0,20},{4,16},{8,28},{12,24},{16,4},{20,0},{24,12},{28,8},{1,21},{... | collective-permute-start | bytes 786440 | tf_op jit(solution)/shard_map/ppermute | solution.py:347
  166.7 80.4 %collective-permute-start.14 = (bf16[128,1024]{1,0:T(8,128)(2,1)S(1)}, bf16[128,1024]{1,0:T(8,128)(2,1)S(1)}, u32[]{:S(2)}, u32[]{:S(2)}) collective-permute-start(bf16[128,1024]{1,0:T(8,128)(2,1)S(1)} %get-tuple-element.38), channel_id=1, source_target_pairs={{0,24},{4,28},{8,16},{12,20},{16,8},{20,12},{24,0},{28,4},{1,25},{... | collective-permute-start | bytes 786440 | tf_op jit(solution)/shard_map/ppermute | solution.py:347
  201.1 48.8 %collective-permute-start.15 = (bf16[128,1024]{1,0:T(8,128)(2,1)S(1)}, bf16[128,1024]{1,0:T(8,128)(2,1)S(1)}, u32[]{:S(2)}, u32[]{:S(2)}) collective-permute-start(bf16[128,1024]{1,0:T(8,128)(2,1)S(1)} %get-tuple-element.37), channel_id=1, source_target_pairs={{0,28},{4,24},{8,20},{12,16},{16,12},{20,8},{24,4},{28,0},{1,29},{... | collective-permute-start | bytes 786440 | tf_op jit(solution)/shard_map/ppermute | solution.py:347
  207.9 42.1 %collective-permute-start.9 = (bf16[128,1024]{1,0:T(8,128)(2,1)S(1)}, bf16[128,1024]{1,0:T(8,128)(2,1)S(1)}, u32[]{:S(2)}, u32[]{:S(2)}) collective-permute-start(bf16[128,1024]{1,0:T(8,128)(2,1)S(1)} %get-tuple-element.43), channel_id=1, source_target_pairs={{0,4},{4,0},{8,12},{12,8},{16,20},{20,16},{24,28},{28,24},{1,5},{5... | collective-permute-start | bytes 786440 | tf_op jit(solution)/shard_map/ppermute | solution.py:347

commit v6 on v5

--- a/solution.py
+++ b/solution.py
@@ -181,13 +181,20 @@
 
 
 def transform_kernel(place_ref, tally_ref, weight_ref, innov_ref, *refs):
-    *part_refs, out_ref, obs_ref = refs[:-7]
-    weighted, precision, root, step, root_next, step_next, inverse = refs[-7:]
+    *part_refs, out_ref, obs_ref = refs[:-8]
+    weighted, precision, root, step, root_next, step_next, inverse, arrived = refs[-8:]
     count_k, slots = obs_ref.shape
     members = count_k // len(part_refs)
+    copies = []
     for number, ref in enumerate(part_refs):
         at = pl.multiple_of((place_ref[0] ^ number) * members, members)
-        obs_ref[pl.ds(at, members), :] = ref[...]
+        copies.append(
+            pltpu.make_async_copy(ref, obs_ref.at[pl.ds(at, members)], arrived.at[number])
+        )
+    for copy in copies:
+        copy.start()
+    for copy in copies:
+        copy.wait()
     spare = count_k - 1.0
     chunks = count_k // TRANSFORM_CHUNK
     live = lax.broadcasted_iota(jnp.int32, (1, slots), 1) < tally_ref[0, 0]
@@ -267,7 +274,9 @@
     square = pltpu.VMEM((count_k, count_k), jnp.bfloat16)
     return pl.pallas_call(
         transform_kernel,
-        in_specs=[pl.BlockSpec(memory_space=pltpu.SMEM)] * 2 + [vmem] * (2 + len(parts)),
+        in_specs=[pl.BlockSpec(memory_space=pltpu.SMEM)] * 2
+        + [vmem] * 2
+        + [pl.BlockSpec(memory_space=pl.ANY)] * len(parts),
         out_specs=vmem,
         out_shape=jax.ShapeDtypeStruct((count_k, count_k), jnp.bfloat16),
         scratch_shapes=[
@@ -275,6 +284,7 @@
             pltpu.VMEM((count_k, slots), jnp.bfloat16),
             pltpu.VMEM((count_k, count_k), jnp.float32),
             square, square, square, square, square,
+            pltpu.SemaphoreType.DMA((len(parts),)),
         ],
         compiler_params=pltpu.CompilerParams(vmem_limit_bytes=40 * MIB),
         cost_estimate=pl.CostEstimate(
@@ -317,8 +327,8 @@
         scratch_shapes=[pltpu.VMEM((blocks, members, ANALYSIS_TILE), jnp.bfloat16)],
         compiler_params=pltpu.CompilerParams(vmem_limit_bytes=32 * MIB),
         cost_estimate=pl.CostEstimate(
-            flops=2 * count_k * count_k * width,
-            bytes_accessed=2 * count_k * (2 * width + count_k),
+            flops=0,
+            bytes_accessed=count_k * width,
             transcendentals=0,
         ),
         name=name,
@@ -357,6 +367,7 @@
     down = lax.ppermute(pool, "reg", to_last)
     picks = measure_pool_indices[0]
     far = gather_chosen(place, pool, up, down, picks, half, half, "gather_far")[0]
+    pool, far = lax.optimization_barrier((pool, far))
     far = [swap(far[k], k + half) for k in range(half)]
     near, innov = gather_chosen(place, pool, up, down, picks, 0, half, "gather_near")
     near = [near[0]] + [swap(near[k], k) for k in range(1, half)]
@@ -367,9 +378,13 @@
         place, active_measure_tally, tapered_error_weight[0], innov, near + far
     )
     done_a = analysed(place, transform, state_a, True, "analysed_a")
-    done_a, state_b = lax.optimization_barrier((done_a, state_b))
+    transform, done_a = lax.optimization_barrier((transform, done_a))
     done_a = [done_a[0]] + [swap(done_a[k], k) for k in range(1, devices)]
-    done_b = exchange(analysed(place, transform, state_b, False, "analysed_b"))
+    done_b = analysed(place, transform, state_b, False, "analysed_b")
+    done_b, *done_a[half : half + 2] = lax.optimization_barrier(
+        (done_b, *done_a[half : half + 2])
+    )
+    done_b = exchange(done_b)
     whole = pairs_to_members(place, done_a, 0, entries, "analysis_a")
     whole = to_members(done_b, 2 * quarter, entries, whole, "analysis_b")
     return whole[:, None]

time: 255 us -> 249 us (0.976); the launches traced: 254 us -> 245 us
  local copies, waits for them, and re-layouts: 14.8 us -> 9.34 us
  waiting for transfers between devices: 135 us -> 131 us
    ppermute x14, waiting for transfers between devices: 100 us -> 78.6 us  [swap(): return lax.ppermute(x, 'mem', [(i, i ^ number) for i in range(devices)])]
    all_to_all x3, waiting for transfers between devices: 6.28 us -> 23.6 us  [exchange(): return lax.all_to_all(x, 'mem', split_axis=0, concat_axis=0, tiled=True)]
    unnamed x26 -> x24, local copies, waits for them, and re-layouts: 12.2 us -> 8.04 us
  transfers between devices with their start and end apart: 19 -> 19, of which waited for: 13 -> 13; matrix products, arithmetic and copies ran while one was open for 1% -> 1% of each run, Pallas kernels for 21% -> 24%
where the time goes in v6:
time: 249 us; the launch traced here: 245 us
  waiting for transfers between devices  131 us (53%)
  Pallas kernels  65.6 us (26%)
  starting transfers between devices  37.8 us (15%)
  local copies, waits for them, and re-layouts  9.34 us (4%)
    ppermute x14, waiting for transfers between devices, swap(): return lax.ppermute(x, 'mem', [(i, i ^ number) for i in range(devices)])  78.6 us
    ppermute x1, waiting for transfers between devices, body(): up = lax.ppermute(pool, 'reg', to_next)  24.1 us
    all_to_all x3, waiting for transfers between devices, exchange(): return lax.all_to_all(x, 'mem', split_axis=0, concat_axis=0, tiled=True)  23.6 us
    pallas_call x2, Pallas kernels, gather_chosen(): pl.pallas_call(functools.partial(gather_kernel, first), grid=(count,), in...  21.9 us
    pallas_call x1, Pallas kernels, ensemble_transform(): pl.pallas_call(transform_kernel, in_specs=[pl.BlockSpec(memory_space=pltp...  17.1 us
    all_to_all x3, starting transfers between devices, exchange(): return lax.all_to_all(x, 'mem', split_axis=0, concat_axis=0, tiled=True)  15.8 us
    ppermute x14, starting transfers between devices, swap(): return lax.ppermute(x, 'mem', [(i, i ^ number) for i in range(devices)])  15.8 us
    pallas_call x2, Pallas kernels, analysed(): pl.pallas_call(functools.partial(analysis_kernel, in_pairs), grid=(width...  10.3 us
  transfers between devices with their start and end apart: 19, of which 13 were waited for; matrix products, arithmetic and copies ran while one was open for 1% of the time, Pallas kernels for 24%

profile of v6, /device:TPU:9, one launch (start us, length us, event | category | flops | bytes accessed | tf_op | source)
XLA Modules:
  0.0 244.5 jit_solution(11077872058893098660)
XLA Ops:
  0.0 4.0 %state_a.1 = bf16[8,128,1024]{2,1,0:T(8,128)(2,1)} custom-call(bf16[128,8,2048]{2,1,0:T(8,128)(2,1)} %bitcast.46), custom_call_target="tpu_custom_call" | custom-call | bytes 4194304 | tf_op jit(solution)/shard_map/state_a/pallas_call | solution.py:115
  4.0 5.7 %all-to-all-start = ((bf16[8,128,1024]{2,1,0:T(8,128)(2,1)}), bf16[8,128,1024]{2,1,0:T(8,128)(2,1)}, u32[]{:S(2)}, u32[]{:S(2)}) async-start(bf16[8,128,1024]{2,1,0:T(8,128)(2,1)} %state_a.1), calls=%async_computation | async-start | bytes 4194304 | tf_op jit(solution)/shard_map/all_to_all | solution.py:354
  9.8 4.1 %pool_rows.1.own_ref = bf16[8,144,1024]{2,1,0:T(8,128)(2,1)} custom-call(bf16[128,8,1024]{2,1,0:T(8,128)(2,1)} %bitcast.48, bf16[8,1024]{1,0:T(8,128)(2,1)} %bitcast.49), custom_call_target="tpu_custom_call" | custom-call | bytes 4718592 | tf_op jit(solution)/shard_map/pool_rows/pallas_call | solution.py:29
  13.8 4.2 %collective-permute-start = (bf16[8,144,1024]{2,1,0:T(8,128)(2,1)}, bf16[8,144,1024]{2,1,0:T(8,128)(2,1)S(1)}, u32[]{:S(2)}, u32[]{:S(2)}) collective-permute-start(bf16[8,144,1024]{2,1,0:T(8,128)(2,1)} %pool_rows.1.own_ref), channel_id=1, source_target_pairs={{0,1},{1,2},{2,3},{4,5},{5,6},{6,7},{8,9},{9,10},{10,11},{12,13},{... | collective-permute-start | bytes 7077896 | tf_op jit(solution)/shard_map/ppermute | solution.py:366
  18.1 1.9 collective-permute-start.1
  20.0 24.1 %collective-permute-done.up_ref = bf16[8,144,1024]{2,1,0:T(8,128)(2,1)S(1)} collective-permute-done((bf16[8,144,1024]{2,1,0:T(8,128)(2,1)}, bf16[8,144,1024]{2,1,0:T(8,128)(2,1)S(1)}, u32[]{:S(2)}, u32[]{:S(2)}) %collective-permute-start) | collective-permute-done | bytes 2359328 | tf_op jit(solution)/shard_map/ppermute | solution.py:366
  44.1 4.7 %collective-permute-done.1.down_ref = bf16[8,144,1024]{2,1,0:T(8,128)(2,1)} collective-permute-done((bf16[8,144,1024]{2,1,0:T(8,128)(2,1)}, bf16[8,144,1024]{2,1,0:T(8,128)(2,1)}, u32[]{:S(2)}, u32[]{:S(2)}) %collective-permute-start.1) | collective-permute-done | bytes 2359328 | tf_op jit(solution)/shard_map/ppermute | solution.py:367
  48.8 0.0 copy-done.8
  48.8 1.7 copy-done
  50.5 10.5 %gather_far.1 = bf16[4,128,1024]{2,1,0:T(8,128)(2,1)S(1)} custom-call(s32[1]{0:T(128)} %bitcast.place_ref, bf16[8,144,1024]{2,1,0:T(8,128)(2,1)S(1)} %copy-done, bf16[8,144,1024]{2,1,0:T(8,128)(2,1)S(1)} %collective-permute-done.up_ref, bf16[8,144,1024]{2,1,0:T(8,128)(2,1)} %collective-permute-done.1.down_ref, s32[8,1024]{1,0:T(8,128)S(1)} %bitcast.43), custom_call_target="tpu_custom_call" | custom-call | bytes 147456 | tf_op jit(solution)/shard_map/gather_far/pallas_call | solution.py:93
  61.0 11.5 %gather_near.1 = (bf16[4,128,1024]{2,1,0:T(8,128)(2,1)S(1)}, bf16[16,1024]{1,0:T(8,128)(2,1)S(1)}) custom-call(s32[1]{0:T(128)} %bitcast.place_ref, bf16[8,144,1024]{2,1,0:T(8,128)(2,1)S(1)} %copy-done, bf16[8,144,1024]{2,1,0:T(8,128)(2,1)S(1)} %collective-permute-done.up_ref, bf16[8,144,1024]{2,1,0:T(8,128)(2,1)} %collective-permute-done.1.down_ref, ...), custom_call_target="tpu_custom_call" | custom-call | bytes 147456 | tf_op jit(solution)/shard_map/gather_near/pallas_call | solution.py:93
  72.4 0.1 slice_bitcast_fusion.12
  72.5 0.9 collective-permute-start.2
  73.5 0.6 collective-permute-start.3
  74.1 1.2 collective-permute-start.4
  75.3 0.1 slice_bitcast_fusion.8
  75.3 1.9 collective-permute-start.5
  77.3 1.2 collective-permute-start.6
  78.5 4.0 %collective-permute-done.2.refs_1_ = bf16[128,1024]{1,0:T(8,128)(2,1)S(1)} collective-permute-done((bf16[128,1024]{1,0:T(8,128)(2,1)S(1)}, bf16[128,1024]{1,0:T(8,128)(2,1)S(1)}, u32[]{:S(2)}, u32[]{:S(2)}) %collective-permute-start.2) | collective-permute-done | bytes 262176 | tf_op jit(solution)/shard_map/ppermute | solution.py:357
  82.4 2.2 collective-permute-start.7
  84.6 0.0 collective-permute-done.3.refs_2_
  84.6 0.9 collective-permute-start.8
  85.5 4.0 %state_b.1 = bf16[8,128,1024]{2,1,0:T(8,128)(2,1)} custom-call(bf16[128,8,2048]{2,1,0:T(8,128)(2,1)} %bitcast.47), custom_call_target="tpu_custom_call" | custom-call | bytes 4194304 | tf_op jit(solution)/shard_map/state_b/pallas_call | solution.py:115
  89.5 0.0 collective-permute-done.4.refs_3_
  89.5 0.0 collective-permute-done.5.refs_4_
  89.5 14.3 %collective-permute-done.6.refs_5_ = bf16[128,1024]{1,0:T(8,128)(2,1)S(1)} collective-permute-done((bf16[128,1024]{1,0:T(8,128)(2,1)S(1)}, bf16[128,1024]{1,0:T(8,128)(2,1)S(1)}, u32[]{:S(2)}, u32[]{:S(2)}) %collective-permute-start.6) | collective-permute-done | bytes 262176 | tf_op jit(solution)/shard_map/ppermute | solution.py:357
  103.8 0.7 copy-done.2
  104.6 11.0 %collective-permute-done.7.refs_6_ = bf16[128,1024]{1,0:T(8,128)(2,1)S(1)} collective-permute-done((bf16[128,1024]{1,0:T(8,128)(2,1)S(1)}, bf16[128,1024]{1,0:T(8,128)(2,1)S(1)}, u32[]{:S(2)}, u32[]{:S(2)}) %collective-permute-start.7) | collective-permute-done | bytes 262176 | tf_op jit(solution)/shard_map/ppermute | solution.py:357
  115.5 0.7 copy-done.4
  116.3 12.4 %collective-permute-done.8.refs_7_ = bf16[128,1024]{1,0:T(8,128)(2,1)S(1)} collective-permute-done((bf16[128,1024]{1,0:T(8,128)(2,1)S(1)}, bf16[128,1024]{1,0:T(8,128)(2,1)S(1)}, u32[]{:S(2)}, u32[]{:S(2)}) %collective-permute-start.8) | collective-permute-done | bytes 262176 | tf_op jit(solution)/shard_map/ppermute | solution.py:357
  128.7 0.7 copy-done.6
  129.4 0.0 all-to-all-done
  129.4 4.4 %all-to-all-start.1 = ((bf16[8,128,1024]{2,1,0:T(8,128)(2,1)}), bf16[8,128,1024]{2,1,0:T(8,128)(2,1)}, u32[]{:S(2)}, u32[]{:S(2)}) async-start(bf16[8,128,1024]{2,1,0:T(8,128)(2,1)} %state_b.1), calls=%async_computation.1 | async-start | bytes 4194304 | tf_op jit(solution)/shard_map/all_to_all | solution.py:354
  134.5 0.0 copy-done.9
  134.5 0.0 copy-start.3
  134.5 0.9 copy-done.3
  135.5 0.9 copy-done.5
  136.4 0.9 copy-done.7
  137.4 17.1 %transform.1.transform_ref = bf16[1024,1024]{1,0:T(8,128)(2,1)S(1)} custom-call(s32[1]{0:T(128)} %bitcast.place_ref, s32[1,1]{1,0:T(1,128)S(6)} %copy.10.tally_ref, f32[1,1024]{1,0:T(1,128)S(1)} %bitcast.45, bf16[16,1024]{1,0:T(8,128)(2,1)S(1)} %get-tuple-element.28.innov_ref, bf16[128,1024]{1,0:T(8,128)(2,1)S(1)} %get-tuple-element.32.refs_0_, ...), custom_call_target="tpu_custom_call" | custom-call | bytes 1048576 | tf_op jit(solution)/shard_map/transform/pallas_call | solution.py:275
  154.4 5.2 %analysed_a.1 = bf16[8,128,1024]{2,1,0:T(8,128)(2,1)S(1)} custom-call(s32[1]{0:T(128)} %bitcast.place_ref, bf16[1024,1024]{1,0:T(8,128)(2,1)S(1)} %transform.1.transform_ref, bf16[1024,1024]{1,0:T(8,128)(2,1)} %bitcast.14.state_ref), custom_call_target="tpu_custom_call" | custom-call | bytes 1048576 | tf_op jit(solution)/shard_map/analysed_a/pallas_call | solution.py:317
  159.6 1.1 slice_bitcast_fusion
  160.8 1.5 collective-permute-start.10
  162.3 0.3 collective-permute-start.9
  162.6 23.6 %all-to-all-done.1 = bf16[8,128,1024]{2,1,0:T(8,128)(2,1)} async-done(((bf16[8,128,1024]{2,1,0:T(8,128)(2,1)}), bf16[8,128,1024]{2,1,0:T(8,128)(2,1)}, u32[]{:S(2)}, u32[]{:S(2)}) %all-to-all-start.1) | async-done | bytes 2097184 | tf_op jit(solution)/shard_map/all_to_all | solution.py:354
  186.2 5.1 %analysed_b.1 = bf16[8,128,1024]{2,1,0:T(8,128)(2,1)S(1)} custom-call(s32[1]{0:T(128)} %bitcast.place_ref, bf16[1024,1024]{1,0:T(8,128)(2,1)S(1)} %transform.1.transform_ref, bf16[1024,1024]{1,0:T(8,128)(2,1)} %bitcast.15.state_ref), custom_call_target="tpu_custom_call" | custom-call | bytes 1048576 | tf_op jit(solution)/shard_map/analysed_b/pallas_call | solution.py:317
  191.3 0.0 copy-start.1
  191.3 1.4 copy-done.1
  192.6 0.0 collective-permute-done.10.refs_5_
  192.6 4.8 %collective-permute-done.9.refs_4_ = bf16[128,1024]{1,0:T(8,128)(2,1)S(1)} collective-permute-done((bf16[128,1024]{1,0:T(8,128)(2,1)S(1)}, bf16[128,1024]{1,0:T(8,128)(2,1)S(1)}, u32[]{:S(2)}, u32[]{:S(2)}) %collective-permute-start.9) | collective-permute-done | bytes 262176 | tf_op jit(solution)/shard_map/ppermute | solution.py:357
  197.5 5.7 %all-to-all-start.2 = ((bf16[8,128,1024]{2,1,0:T(8,128)(2,1)}), bf16[8,128,1024]{2,1,0:T(8,128)(2,1)S(1)}, u32[]{:S(2)}, u32[]{:S(2)}) async-start(bf16[8,128,1024]{2,1,0:T(8,128)(2,1)} %copy-done.1), calls=%async_computation.2 | async-start | bytes 4194304 | tf_op jit(solution)/shard_map/all_to_all | solution.py:354
  203.2 1.2 collective-permute-start.11
  204.4 0.3 collective-permute-start.12
  204.6 1.2 collective-permute-start.13
  205.8 0.0 copy-done.11
  205.8 1.2 collective-permute-start.14
  207.0 1.2 collective-permute-start.15
  208.2 7.0 %collective-permute-done.11.refs_1_ = bf16[128,1024]{1,0:T(8,128)(2,1)S(1)} collective-permute-done((bf16[128,1024]{1,0:T(8,128)(2,1)}, bf16[128,1024]{1,0:T(8,128)(2,1)S(1)}, u32[]{:S(2)}, u32[]{:S(2)}) %collective-permute-start.11) | collective-permute-done | bytes 262176 | tf_op jit(solution)/shard_map/ppermute | solution.py:357
  215.2 10.1 %collective-permute-done.12.refs_2_ = bf16[128,1024]{1,0:T(8,128)(2,1)S(1)} collective-permute-done((bf16[128,1024]{1,0:T(8,128)(2,1)}, bf16[128,1024]{1,0:T(8,128)(2,1)S(1)}, u32[]{:S(2)}, u32[]{:S(2)}) %collective-permute-start.12) | collective-permute-done | bytes 262176 | tf_op jit(solution)/shard_map/ppermute | solution.py:357
  225.3 3.7 %collective-permute-done.13.refs_3_ = bf16[128,1024]{1,0:T(8,128)(2,1)S(1)} collective-permute-done((bf16[128,1024]{1,0:T(8,128)(2,1)}, bf16[128,1024]{1,0:T(8,128)(2,1)S(1)}, u32[]{:S(2)}, u32[]{:S(2)}) %collective-permute-start.13) | collective-permute-done | bytes 262176 | tf_op jit(solution)/shard_map/ppermute | solution.py:357
  229.1 7.7 %collective-permute-done.14.refs_6_ = bf16[128,1024]{1,0:T(8,128)(2,1)S(1)} collective-permute-done((bf16[128,1024]{1,0:T(8,128)(2,1)S(1)}, bf16[128,1024]{1,0:T(8,128)(2,1)S(1)}, u32[]{:S(2)}, u32[]{:S(2)}) %collective-permute-start.14) | collective-permute-done | bytes 262176 | tf_op jit(solution)/shard_map/ppermute | solution.py:357
  236.7 3.5 %collective-permute-done.15.refs_7_ = bf16[128,1024]{1,0:T(8,128)(2,1)S(1)} collective-permute-done((bf16[128,1024]{1,0:T(8,128)(2,1)S(1)}, bf16[128,1024]{1,0:T(8,128)(2,1)S(1)}, u32[]{:S(2)}, u32[]{:S(2)}) %collective-permute-start.15) | collective-permute-done | bytes 262176 | tf_op jit(solution)/shard_map/ppermute | solution.py:357
  240.2 2.2 analysis_a.1.refs_0_
  242.4 0.0 all-to-all-done.2.part_ref
  242.4 2.1 analysis_b.1
  (11 shorter events, 0.0 us)
Async XLA Ops:
  4.0 125.4 %all-to-all-start = ((bf16[8,128,1024]{2,1,0:T(8,128)(2,1)}), bf16[8,128,1024]{2,1,0:T(8,128)(2,1)}, u32[]{:S(2)}, u32[]{:S(2)}) async-start(bf16[8,128,1024]{2,1,0:T(8,128)(2,1)} %state_a.1), calls=%async_computation | async-start | bytes 4194304 | tf_op jit(solution)/shard_map/all_to_all | solution.py:354
  9.8 39.1 %copy-start.8 = (s32[1,8,1024]{2,1,0:T(8,128)S(1)}, s32[1,8,1024]{2,1,0:T(8,128)}, u32[]{:S(2)}) copy-start(s32[1,8,1024]{2,1,0:T(8,128)} %param.9) | copy-start | bytes 98308
  13.8 30.3 %collective-permute-start = (bf16[8,144,1024]{2,1,0:T(8,128)(2,1)}, bf16[8,144,1024]{2,1,0:T(8,128)(2,1)S(1)}, u32[]{:S(2)}, u32[]{:S(2)}) collective-permute-start(bf16[8,144,1024]{2,1,0:T(8,128)(2,1)} %pool_rows.1.own_ref), channel_id=1, source_target_pairs={{0,1},{1,2},{2,3},{4,5},{5,6},{6,7},{8,9},{9,10},{10,11},{12,13},{... | collective-permute-start | bytes 7077896 | tf_op jit(solution)/shard_map/ppermute | solution.py:366
  18.1 30.8 %collective-permute-start.1 = (bf16[8,144,1024]{2,1,0:T(8,128)(2,1)}, bf16[8,144,1024]{2,1,0:T(8,128)(2,1)}, u32[]{:S(2)}, u32[]{:S(2)}) collective-permute-start(bf16[8,144,1024]{2,1,0:T(8,128)(2,1)} %pool_rows.1.own_ref), channel_id=1, source_target_pairs={{1,0},{2,1},{3,2},{5,4},{6,5},{7,6},{9,8},{10,9},{11,10},{13,12},{... | collective-permute-start | bytes 7077896 | tf_op jit(solution)/shard_map/ppermute | solution.py:367
  48.8 1.7 copy-start
  72.5 9.9 %collective-permute-start.2 = (bf16[128,1024]{1,0:T(8,128)(2,1)S(1)}, bf16[128,1024]{1,0:T(8,128)(2,1)S(1)}, u32[]{:S(2)}, u32[]{:S(2)}) collective-permute-start(bf16[128,1024]{1,0:T(8,128)(2,1)S(1)} %get-tuple-element.61), channel_id=1, source_target_pairs={{0,4},{4,0},{8,12},{12,8},{16,20},{20,16},{24,28},{28,24},{1,5},{5... | collective-permute-start | bytes 786440 | tf_op jit(solution)/shard_map/ppermute | solution.py:357
  73.5 11.1 %collective-permute-start.3 = (bf16[128,1024]{1,0:T(8,128)(2,1)S(1)}, bf16[128,1024]{1,0:T(8,128)(2,1)S(1)}, u32[]{:S(2)}, u32[]{:S(2)}) collective-permute-start(bf16[128,1024]{1,0:T(8,128)(2,1)S(1)} %get-tuple-element.60), channel_id=1, source_target_pairs={{0,8},{4,12},{8,0},{12,4},{16,24},{20,28},{24,16},{28,20},{1,9},{5... | collective-permute-start | bytes 786440 | tf_op jit(solution)/shard_map/ppermute | solution.py:357
  74.1 15.4 %collective-permute-start.4 = (bf16[128,1024]{1,0:T(8,128)(2,1)S(1)}, bf16[128,1024]{1,0:T(8,128)(2,1)S(1)}, u32[]{:S(2)}, u32[]{:S(2)}) collective-permute-start(bf16[128,1024]{1,0:T(8,128)(2,1)S(1)} %get-tuple-element.59), channel_id=1, source_target_pairs={{0,12},{4,8},{8,4},{12,0},{16,28},{20,24},{24,20},{28,16},{1,13},{... | collective-permute-start | bytes 786440 | tf_op jit(solution)/shard_map/ppermute | solution.py:357
  75.3 14.2 %collective-permute-start.5 = (bf16[128,1024]{1,0:T(8,128)(2,1)S(1)}, bf16[128,1024]{1,0:T(8,128)(2,1)S(1)}, u32[]{:S(2)}, u32[]{:S(2)}) collective-permute-start(bf16[128,1024]{1,0:T(8,128)(2,1)S(1)} %get-tuple-element.58), channel_id=1, source_target_pairs={{0,16},{4,20},{8,24},{12,28},{16,0},{20,4},{24,8},{28,12},{1,17},{... | collective-permute-start | bytes 786440 | tf_op jit(solution)/shard_map/ppermute | solution.py:357
  77.3 26.6 %collective-permute-start.6 = (bf16[128,1024]{1,0:T(8,128)(2,1)S(1)}, bf16[128,1024]{1,0:T(8,128)(2,1)S(1)}, u32[]{:S(2)}, u32[]{:S(2)}) collective-permute-start(bf16[128,1024]{1,0:T(8,128)(2,1)S(1)} %get-tuple-element.57), channel_id=1, source_target_pairs={{0,20},{4,16},{8,28},{12,24},{16,4},{20,0},{24,12},{28,8},{1,21},{... | collective-permute-start | bytes 786440 | tf_op jit(solution)/shard_map/ppermute | solution.py:357
  82.4 33.1 %collective-permute-start.7 = (bf16[128,1024]{1,0:T(8,128)(2,1)S(1)}, bf16[128,1024]{1,0:T(8,128)(2,1)S(1)}, u32[]{:S(2)}, u32[]{:S(2)}) collective-permute-start(bf16[128,1024]{1,0:T(8,128)(2,1)S(1)} %get-tuple-element.56), channel_id=1, source_target_pairs={{0,24},{4,28},{8,16},{12,20},{16,8},{20,12},{24,0},{28,4},{1,25},{... | collective-permute-start | bytes 786440 | tf_op jit(solution)/shard_map/ppermute | solution.py:357
  84.6 44.1 %collective-permute-start.8 = (bf16[128,1024]{1,0:T(8,128)(2,1)S(1)}, bf16[128,1024]{1,0:T(8,128)(2,1)S(1)}, u32[]{:S(2)}, u32[]{:S(2)}) collective-permute-start(bf16[128,1024]{1,0:T(8,128)(2,1)S(1)} %get-tuple-element.55), channel_id=1, source_target_pairs={{0,28},{4,24},{8,20},{12,16},{16,12},{20,8},{24,4},{28,0},{1,29},{... | collective-permute-start | bytes 786440 | tf_op jit(solution)/shard_map/ppermute | solution.py:357
  103.8 0.7 copy-start.2
  115.5 0.7 copy-start.4
  128.7 0.7 copy-start.6
  129.4 5.1 %copy-start.9 = (f32[1,1,1024]{2,1,0:T(1,128)S(1)}, f32[1,1,1024]{2,1,0:T(1,128)}, u32[]{:S(2)}) copy-start(f32[1,1,1024]{2,1,0:T(1,128)} %param.11) | copy-start | bytes 12292
  129.4 56.8 %all-to-all-start.1 = ((bf16[8,128,1024]{2,1,0:T(8,128)(2,1)}), bf16[8,128,1024]{2,1,0:T(8,128)(2,1)}, u32[]{:S(2)}, u32[]{:S(2)}) async-start(bf16[8,128,1024]{2,1,0:T(8,128)(2,1)} %state_b.1), calls=%async_computation.1 | async-start | bytes 4194304 | tf_op jit(solution)/shard_map/all_to_all | solution.py:354
  134.5 1.0 copy-start.3
  135.5 0.9 copy-start.5
  136.4 0.9 copy-start.7
  160.8 31.9 %collective-permute-start.10 = (bf16[128,1024]{1,0:T(8,128)(2,1)S(1)}, bf16[128,1024]{1,0:T(8,128)(2,1)S(1)}, u32[]{:S(2)}, u32[]{:S(2)}) collective-permute-start(bf16[128,1024]{1,0:T(8,128)(2,1)S(1)} %get-tuple-element.53), channel_id=1, source_target_pairs={{0,20},{4,16},{8,28},{12,24},{16,4},{20,0},{24,12},{28,8},{1,21},{... | collective-permute-start | bytes 786440 | tf_op jit(solution)/shard_map/ppermute | solution.py:357
  162.3 35.2 %collective-permute-start.9 = (bf16[128,1024]{1,0:T(8,128)(2,1)S(1)}, bf16[128,1024]{1,0:T(8,128)(2,1)S(1)}, u32[]{:S(2)}, u32[]{:S(2)}) collective-permute-start(bf16[128,1024]{1,0:T(8,128)(2,1)S(1)} %get-tuple-element.54), channel_id=1, source_target_pairs={{0,16},{4,20},{8,24},{12,28},{16,0},{20,4},{24,8},{28,12},{1,17},{... | collective-permute-start | bytes 786440 | tf_op jit(solution)/shard_map/ppermute | solution.py:357
  191.3 1.4 copy-start.1
  192.6 13.2 %copy-start.11 = (bf16[128,1024]{1,0:T(8,128)(2,1)S(1)}, bf16[128,1024]{1,0:T(8,128)(2,1)}, u32[]{:S(2)}) copy-start(bf16[128,1024]{1,0:T(8,128)(2,1)} %get-tuple-element.48) | copy-start | bytes 786436
  192.6 14.4 %copy-start.10 = (bf16[128,1024]{1,0:T(8,128)(2,1)S(1)}, bf16[128,1024]{1,0:T(8,128)(2,1)}, u32[]{:S(2)}) copy-start(bf16[128,1024]{1,0:T(8,128)(2,1)} %get-tuple-element.47) | copy-start | bytes 786436
  197.5 44.9 %all-to-all-start.2 = ((bf16[8,128,1024]{2,1,0:T(8,128)(2,1)}), bf16[8,128,1024]{2,1,0:T(8,128)(2,1)S(1)}, u32[]{:S(2)}, u32[]{:S(2)}) async-start(bf16[8,128,1024]{2,1,0:T(8,128)(2,1)} %copy-done.1), calls=%async_computation.2 | async-start | bytes 4194304 | tf_op jit(solution)/shard_map/all_to_all | solution.py:354
  203.2 12.1 %collective-permute-start.11 = (bf16[128,1024]{1,0:T(8,128)(2,1)}, bf16[128,1024]{1,0:T(8,128)(2,1)S(1)}, u32[]{:S(2)}, u32[]{:S(2)}) collective-permute-start(bf16[128,1024]{1,0:T(8,128)(2,1)} %get-tuple-element.51), channel_id=1, source_target_pairs={{0,4},{4,0},{8,12},{12,8},{16,20},{20,16},{24,28},{28,24},{1,5},{5... | collective-permute-start | bytes 786440 | tf_op jit(solution)/shard_map/ppermute | solution.py:357
  204.4 21.0 %collective-permute-start.12 = (bf16[128,1024]{1,0:T(8,128)(2,1)}, bf16[128,1024]{1,0:T(8,128)(2,1)S(1)}, u32[]{:S(2)}, u32[]{:S(2)}) collective-permute-start(bf16[128,1024]{1,0:T(8,128)(2,1)} %get-tuple-element.50), channel_id=1, source_target_pairs={{0,8},{4,12},{8,0},{12,4},{16,24},{20,28},{24,16},{28,20},{1,9},{5... | collective-permute-start | bytes 786440 | tf_op jit(solution)/shard_map/ppermute | solution.py:357
  204.6 24.4 %collective-permute-start.13 = (bf16[128,1024]{1,0:T(8,128)(2,1)}, bf16[128,1024]{1,0:T(8,128)(2,1)S(1)}, u32[]{:S(2)}, u32[]{:S(2)}) collective-permute-start(bf16[128,1024]{1,0:T(8,128)(2,1)} %get-tuple-element.49), channel_id=1, source_target_pairs={{0,12},{4,8},{8,4},{12,0},{16,28},{20,24},{24,20},{28,16},{1,13},{... | collective-permute-start | bytes 786440 | tf_op jit(solution)/shard_map/ppermute | solution.py:357
  205.8 30.9 %collective-permute-start.14 = (bf16[128,1024]{1,0:T(8,128)(2,1)S(1)}, bf16[128,1024]{1,0:T(8,128)(2,1)S(1)}, u32[]{:S(2)}, u32[]{:S(2)}) collective-permute-start(bf16[128,1024]{1,0:T(8,128)(2,1)S(1)} %copy-done.11), channel_id=1, source_target_pairs={{0,24},{4,28},{8,16},{12,20},{16,8},{20,12},{24,0},{28,4},{1,25},{... | collective-permute-start | bytes 786440 | tf_op jit(solution)/shard_map/ppermute | solution.py:357
  207.0 33.2 %collective-permute-start.15 = (bf16[128,1024]{1,0:T(8,128)(2,1)S(1)}, bf16[128,1024]{1,0:T(8,128)(2,1)S(1)}, u32[]{:S(2)}, u32[]{:S(2)}) collective-permute-start(bf16[128,1024]{1,0:T(8,128)(2,1)S(1)} %copy-done.10), channel_id=1, source_target_pairs={{0,28},{4,24},{8,20},{12,16},{16,12},{20,8},{24,4},{28,0},{1,29},{... | collective-permute-start | bytes 786440 | tf_op jit(solution)/shard_map/ppermute | solution.py:357

commit v7 on v6

--- a/solution.py
+++ b/solution.py
@@ -10,31 +10,76 @@
 INNOV_ROWS = 16
 SLOT_CHUNK = 256
 MEMBER_TILE = 32
-POOL_TILE = 256
 TRANSFORM_CHUNK = 256
 ANALYSIS_TILE = 256
 MIB = 1024 * 1024
 
 
-def pool_kernel(obs_ref, innov_ref, out_ref):
+def fetch_tiles(source_ref, start, stage, arrived, use):
+    width = stage.shape[2]
+    tiles = []
+    for number in range(stage.shape[0] // MEMBER_TILE):
+        rows = pl.ds(number * MEMBER_TILE, MEMBER_TILE)
+        copy = pltpu.make_async_copy(
+            source_ref.at[rows, :, pl.ds(start, width)], stage.at[rows], arrived.at[number]
+        )
+        copy.start()
+        tiles.append((copy, rows))
+    for copy, rows in tiles:
+        copy.wait()
+        use(rows)
+
+
+def to_blocks_kernel(start, state_ref, out_ref, stage, arrived):
+    def use(rows):
+        out_ref[:, rows, :] = jnp.swapaxes(stage[rows], 0, 1)
+
+    fetch_tiles(state_ref, start, stage, arrived, use)
+
+
+def to_blocks(state, start, width, name):
+    members, blocks, _ = state.shape
+    return pl.pallas_call(
+        functools.partial(to_blocks_kernel, start),
+        in_specs=[pl.BlockSpec(memory_space=pltpu.HBM)],
+        out_specs=pl.BlockSpec(memory_space=pltpu.VMEM),
+        out_shape=jax.ShapeDtypeStruct((blocks, members, width), state.dtype),
+        scratch_shapes=[
+            pltpu.VMEM((members, blocks, width), state.dtype),
+            pltpu.SemaphoreType.DMA((members // MEMBER_TILE,)),
+        ],
+        compiler_params=pltpu.CompilerParams(vmem_limit_bytes=60 * MIB),
+        cost_estimate=pl.CostEstimate(
+            flops=0, bytes_accessed=4 * members * blocks * width, transcendentals=0
+        ),
+        name=name,
+    )(state)
+
+
+def pool_kernel(obs_ref, innov_ref, out_ref, stage, arrived):
     members = obs_ref.shape[0]
-    out_ref[:, :members, :] = jnp.swapaxes(obs_ref[...], 0, 1)
+
+    def use(rows):
+        out_ref[:, rows, :] = jnp.swapaxes(stage[rows], 0, 1)
+
     shape = (out_ref.shape[0], INNOV_ROWS, out_ref.shape[2])
     out_ref[:, members:, :] = jnp.broadcast_to(innov_ref[...][:, None, :], shape)
+    fetch_tiles(obs_ref, 0, stage, arrived, use)
 
 
 def pool_rows(obs, innov):
     members, blocks, depth = obs.shape
     rows = members + INNOV_ROWS
+    vmem = pl.BlockSpec(memory_space=pltpu.VMEM)
     return pl.pallas_call(
         pool_kernel,
-        grid=(depth // POOL_TILE,),
-        in_specs=[
-            pl.BlockSpec((members, blocks, POOL_TILE), lambda i: (0, 0, i)),
-            pl.BlockSpec((blocks, POOL_TILE), lambda i: (0, i)),
-        ],
-        out_specs=pl.BlockSpec((blocks, rows, POOL_TILE), lambda i: (0, 0, i)),
+        in_specs=[pl.BlockSpec(memory_space=pltpu.HBM), vmem],
+        out_specs=vmem,
         out_shape=jax.ShapeDtypeStruct((blocks, rows, depth), obs.dtype),
+        scratch_shapes=[
+            pltpu.VMEM((members, blocks, depth), obs.dtype),
+            pltpu.SemaphoreType.DMA((members // MEMBER_TILE,)),
+        ],
         compiler_params=pltpu.CompilerParams(vmem_limit_bytes=60 * MIB),
         cost_estimate=pl.CostEstimate(
             flops=0, bytes_accessed=4 * rows * blocks * depth, transcendentals=0
@@ -106,54 +151,50 @@
     )(place, own, up, down, picks)
 
 
-def to_blocks_kernel(in_ref, out_ref):
-    out_ref[...] = jnp.swapaxes(in_ref[...], 0, 1)
-
-
-def to_blocks(state, start, width, name):
-    members, blocks, _ = state.shape
-    return pl.pallas_call(
-        to_blocks_kernel,
-        grid=(members // MEMBER_TILE,),
-        in_specs=[
-            pl.BlockSpec((MEMBER_TILE, blocks, pl.Element(width)), lambda i: (i, 0, start))
-            if start % width
-            else pl.BlockSpec((MEMBER_TILE, blocks, width), lambda i: (i, 0, start // width))
-        ],
-        out_specs=pl.BlockSpec((blocks, MEMBER_TILE, width), lambda i: (0, i, 0)),
-        out_shape=jax.ShapeDtypeStruct((blocks, members, width), state.dtype),
-        compiler_params=pltpu.CompilerParams(vmem_limit_bytes=60 * MIB),
-        cost_estimate=pl.CostEstimate(
-            flops=0, bytes_accessed=4 * members * blocks * width, transcendentals=0
-        ),
-        name=name,
-    )(state)
-
-
-def to_members_kernel(part_ref, *refs):
-    refs[-1][...] = jnp.swapaxes(part_ref[...], 0, 1)
-
-
-def pairs_to_members_kernel(place_ref, *refs):
-    *part_refs, out_ref, stage = refs
-    for number, ref in enumerate(part_refs):
-        stage[place_ref[0] ^ number] = ref[...]
-    out_ref[...] = jnp.swapaxes(stage[...], 0, 1)
-
-
-def to_members(part, start, entries, whole, name):
+def store_tiles(out_ref, start, stage, sent, make):
+    width = stage.shape[2]
+    copies = []
+    for number in range(stage.shape[0] // MEMBER_TILE):
+        rows = pl.ds(number * MEMBER_TILE, MEMBER_TILE)
+        stage[rows] = make(rows)
+        copy = pltpu.make_async_copy(
+            stage.at[rows], out_ref.at[rows, :, pl.ds(start, width)], sent.at[number]
+        )
+        copy.start()
+        copies.append(copy)
+    for copy in copies:
+        copy.wait()
+
+
+def to_members_kernel(start, part_ref, whole_ref, out_ref, stage, sent):
+    store_tiles(out_ref, start, stage, sent, lambda rows: jnp.swapaxes(part_ref[:, rows, :], 0, 1))
+
+
+def pairs_to_members_kernel(start, place_ref, *refs):
+    *part_refs, out_ref, turned, stage, sent = refs
+
+    def make(rows):
+        for number, ref in enumerate(part_refs):
+            turned[place_ref[0] ^ number] = ref[rows]
+        return jnp.swapaxes(turned[...], 0, 1)
+
+    store_tiles(out_ref, start, stage, sent, make)
+
+
+def to_members(part, start, whole, name):
     blocks, members, width = part.shape
-    return pl.pallas_call(
-        to_members_kernel,
-        grid=(members // MEMBER_TILE,),
-        in_specs=[
-            pl.BlockSpec((blocks, MEMBER_TILE, width), lambda i: (0, i, 0)),
-            pl.BlockSpec(memory_space=pl.ANY),
-        ],
-        out_specs=pl.BlockSpec((MEMBER_TILE, blocks, width), lambda i: (i, 0, start // width)),
-        out_shape=jax.ShapeDtypeStruct((members, blocks, entries), part.dtype),
+    hbm = pl.BlockSpec(memory_space=pltpu.HBM)
+    return pl.pallas_call(
+        functools.partial(to_members_kernel, start),
+        in_specs=[pl.BlockSpec(memory_space=pltpu.VMEM), hbm],
+        out_specs=hbm,
+        out_shape=jax.ShapeDtypeStruct(whole.shape, part.dtype),
+        scratch_shapes=[
+            pltpu.VMEM((members, blocks, width), part.dtype),
+            pltpu.SemaphoreType.DMA((members // MEMBER_TILE,)),
+        ],
         input_output_aliases={1: 0},
-        compiler_params=pltpu.CompilerParams(vmem_limit_bytes=32 * MIB),
+        compiler_params=pltpu.CompilerParams(vmem_limit_bytes=16 * MIB),
         cost_estimate=pl.CostEstimate(
             flops=0, bytes_accessed=4 * members * blocks * width, transcendentals=0
         ),
@@ -165,14 +206,17 @@
     blocks = len(parts)
     members, width = parts[0].shape
     return pl.pallas_call(
-        pairs_to_members_kernel,
-        grid=(members // MEMBER_TILE,),
+        functools.partial(pairs_to_members_kernel, start),
         in_specs=[pl.BlockSpec(memory_space=pltpu.SMEM)]
-        + [pl.BlockSpec((MEMBER_TILE, width), lambda i: (i, 0))] * blocks,
-        out_specs=pl.BlockSpec((MEMBER_TILE, blocks, width), lambda i: (i, 0, start // width)),
+        + [pl.BlockSpec(memory_space=pltpu.VMEM)] * blocks,
+        out_specs=pl.BlockSpec(memory_space=pltpu.HBM),
         out_shape=jax.ShapeDtypeStruct((members, blocks, entries), parts[0].dtype),
-        scratch_shapes=[pltpu.VMEM((blocks, MEMBER_TILE, width), parts[0].dtype)],
-        compiler_params=pltpu.CompilerParams(vmem_limit_bytes=32 * MIB),
+        scratch_shapes=[
+            pltpu.VMEM((blocks, MEMBER_TILE, width), parts[0].dtype),
+            pltpu.VMEM((members, blocks, width), parts[0].dtype),
+            pltpu.SemaphoreType.DMA((members // MEMBER_TILE,)),
+        ],
+        compiler_params=pltpu.CompilerParams(vmem_limit_bytes=16 * MIB),
         cost_estimate=pl.CostEstimate(
             flops=0, bytes_accessed=4 * members * blocks * width, transcendentals=0
         ),
@@ -357,9 +401,9 @@
         return lax.ppermute(x, "mem", [(i, i ^ number) for i in range(devices)])
 
     half = devices // 2
-    quarter = entries // 4
+    width = entries // 2
     state = prior_members_field[:, 0]
-    state_a = to_blocks(state, 0, 2 * quarter, "state_a")
+    state_a = to_blocks(state, 0, width, "state_a")
     devs, state_a = lax.optimization_barrier((measure_space_deviations[:, 0], state_a))
     state_a = exchange(state_a)
     pool = pool_rows(devs, measured_minus_predicted[0])
@@ -371,8 +415,8 @@
     far = [swap(far[k], k + half) for k in range(half)]
     near, innov = gather_chosen(place, pool, up, down, picks, 0, half, "gather_near")
     near = [near[0]] + [swap(near[k], k) for k in range(1, half)]
-    state_b = to_blocks(state, 2 * quarter, 2 * quarter, "state_b")
-    state_b, state_a, near, far = lax.optimization_barrier((state_b, state_a, near, far))
+    state_b = to_blocks(state, width, entries - width, "state_b")
+    near, far, state_a, state_b = lax.optimization_barrier((near, far, state_a, state_b))
     state_b = exchange(state_b)
     transform = ensemble_transform(
         place, active_measure_tally, tapered_error_weight[0], innov, near + far
@@ -386,7 +430,7 @@
     )
     done_b = exchange(done_b)
     whole = pairs_to_members(place, done_a, 0, entries, "analysis_a")
-    whole = to_members(done_b, 2 * quarter, entries, whole, "analysis_b")
+    whole = to_members(done_b, width, whole, "analysis_b")
     return whole[:, None]
 
 

time: 249 us -> 247 us (level)
  the two profiles are of different devices: /device:TPU:9 before, /device:TPU:10 now
where the time goes in v7:
time: 247 us; the launch traced here: 246 us
  waiting for transfers between devices  132 us (53%)
  Pallas kernels  62.1 us (25%)
  starting transfers between devices  42.4 us (17%)
  local copies, waits for them, and re-layouts  9.34 us (4%)
    ppermute x14, waiting for transfers between devices, swap(): return lax.ppermute(x, 'mem', [(i, i ^ number) for i in range(devices)])  80.3 us
    all_to_all x3, waiting for transfers between devices, exchange(): return lax.all_to_all(x, 'mem', split_axis=0, concat_axis=0, tiled=True)  24.8 us
    ppermute x1, waiting for transfers between devices, body(): up = lax.ppermute(pool, 'reg', to_next)  24.8 us
    pallas_call x2, Pallas kernels, gather_chosen(): pl.pallas_call(functools.partial(gather_kernel, first), grid=(count,), in...  21.9 us
    ppermute x14, starting transfers between devices, swap(): return lax.ppermute(x, 'mem', [(i, i ^ number) for i in range(devices)])  19.7 us
    all_to_all x3, starting transfers between devices, exchange(): return lax.all_to_all(x, 'mem', split_axis=0, concat_axis=0, tiled=True)  17.1 us
    pallas_call x1, Pallas kernels, ensemble_transform(): pl.pallas_call(transform_kernel, in_specs=[pl.BlockSpec(memory_space=pltp...  17.1 us
    pallas_call x2, Pallas kernels, analysed(): pl.pallas_call(functools.partial(analysis_kernel, in_pairs), grid=(width...  10.3 us
  transfers between devices with their start and end apart: 19, of which 14 were waited for; matrix products, arithmetic and copies ran while one was open for 1% of the time, Pallas kernels for 23%

profile of v7, /device:TPU:10, one launch (start us, length us, event | category | flops | bytes accessed | tf_op | source)
XLA Modules:
  0.0 246.4 jit_solution(16664058539160648100)
XLA Ops:
  0.0 3.0 %state_a.1 = bf16[8,128,1024]{2,1,0:T(8,128)(2,1)} custom-call(bf16[128,8,2048]{2,1,0:T(8,128)(2,1)} %bitcast.46), custom_call_target="tpu_custom_call" | custom-call | bytes 4194304 | tf_op jit(solution)/shard_map/state_a/pallas_call | solution.py:42
  3.0 6.3 %all-to-all-start = ((bf16[8,128,1024]{2,1,0:T(8,128)(2,1)}), bf16[8,128,1024]{2,1,0:T(8,128)(2,1)}, u32[]{:S(2)}, u32[]{:S(2)}) async-start(bf16[8,128,1024]{2,1,0:T(8,128)(2,1)} %state_a.1), calls=%async_computation | async-start | bytes 4194304 | tf_op jit(solution)/shard_map/all_to_all | solution.py:398
  9.3 3.8 %pool_rows.1.own_ref = bf16[8,144,1024]{2,1,0:T(8,128)(2,1)} custom-call(bf16[128,8,1024]{2,1,0:T(8,128)(2,1)} %bitcast.48, bf16[8,1024]{1,0:T(8,128)(2,1)} %bitcast.49), custom_call_target="tpu_custom_call" | custom-call | bytes 4718592 | tf_op jit(solution)/shard_map/pool_rows/pallas_call | solution.py:74
  13.1 1.9 collective-permute-start
  15.1 3.6 %collective-permute-start.1 = (bf16[8,144,1024]{2,1,0:T(8,128)(2,1)}, bf16[8,144,1024]{2,1,0:T(8,128)(2,1)}, u32[]{:S(2)}, u32[]{:S(2)}) collective-permute-start(bf16[8,144,1024]{2,1,0:T(8,128)(2,1)} %pool_rows.1.own_ref), channel_id=1, source_target_pairs={{1,0},{2,1},{3,2},{5,4},{6,5},{7,6},{9,8},{10,9},{11,10},{13,12},{... | collective-permute-start | bytes 7077896 | tf_op jit(solution)/shard_map/ppermute | solution.py:411
  18.7 24.8 %collective-permute-done.up_ref = bf16[8,144,1024]{2,1,0:T(8,128)(2,1)S(1)} collective-permute-done((bf16[8,144,1024]{2,1,0:T(8,128)(2,1)}, bf16[8,144,1024]{2,1,0:T(8,128)(2,1)S(1)}, u32[]{:S(2)}, u32[]{:S(2)}) %collective-permute-start) | collective-permute-done | bytes 2359328 | tf_op jit(solution)/shard_map/ppermute | solution.py:410
  43.5 1.9 collective-permute-done.1.down_ref
  45.4 0.0 copy-done.8
  45.4 1.7 copy-done
  47.0 10.5 %gather_far.1 = bf16[4,128,1024]{2,1,0:T(8,128)(2,1)S(1)} custom-call(s32[1]{0:T(128)} %bitcast.place_ref, bf16[8,144,1024]{2,1,0:T(8,128)(2,1)S(1)} %copy-done, bf16[8,144,1024]{2,1,0:T(8,128)(2,1)S(1)} %collective-permute-done.up_ref, bf16[8,144,1024]{2,1,0:T(8,128)(2,1)} %collective-permute-done.1.down_ref, s32[8,1024]{1,0:T(8,128)S(1)} %bitcast.43), custom_call_target="tpu_custom_call" | custom-call | bytes 147456 | tf_op jit(solution)/shard_map/gather_far/pallas_call | solution.py:138
  57.5 11.5 %gather_near.1 = (bf16[4,128,1024]{2,1,0:T(8,128)(2,1)S(1)}, bf16[16,1024]{1,0:T(8,128)(2,1)S(1)}) custom-call(s32[1]{0:T(128)} %bitcast.place_ref, bf16[8,144,1024]{2,1,0:T(8,128)(2,1)S(1)} %copy-done, bf16[8,144,1024]{2,1,0:T(8,128)(2,1)S(1)} %collective-permute-done.up_ref, bf16[8,144,1024]{2,1,0:T(8,128)(2,1)} %collective-permute-done.1.down_ref, ...), custom_call_target="tpu_custom_call" | custom-call | bytes 147456 | tf_op jit(solution)/shard_map/gather_near/pallas_call | solution.py:138
  69.0 0.1 slice_bitcast_fusion.12
  69.1 1.5 collective-permute-start.2
  70.6 0.6 collective-permute-start.3
  71.2 1.5 collective-permute-start.4
  72.6 0.1 slice_bitcast_fusion.8
  72.7 2.4 collective-permute-start.5
  75.1 1.5 collective-permute-start.6
  76.6 0.0 collective-permute-done.2.refs_1_
  76.6 1.5 collective-permute-start.7
  78.1 0.0 collective-permute-done.3.refs_2_
  78.1 0.6 collective-permute-start.8
  78.6 3.0 %state_b.1 = bf16[8,128,1024]{2,1,0:T(8,128)(2,1)} custom-call(bf16[128,8,2048]{2,1,0:T(8,128)(2,1)} %bitcast.47), custom_call_target="tpu_custom_call" | custom-call | bytes 4194304 | tf_op jit(solution)/shard_map/state_b/pallas_call | solution.py:42
  81.6 0.4 collective-permute-done.4.refs_3_
  82.0 11.4 %collective-permute-done.5.refs_4_ = bf16[128,1024]{1,0:T(8,128)(2,1)S(1)} collective-permute-done((bf16[128,1024]{1,0:T(8,128)(2,1)S(1)}, bf16[128,1024]{1,0:T(8,128)(2,1)S(1)}, u32[]{:S(2)}, u32[]{:S(2)}) %collective-permute-start.5) | collective-permute-done | bytes 262176 | tf_op jit(solution)/shard_map/ppermute | solution.py:401
  93.4 15.3 %collective-permute-done.6.refs_5_ = bf16[128,1024]{1,0:T(8,128)(2,1)S(1)} collective-permute-done((bf16[128,1024]{1,0:T(8,128)(2,1)S(1)}, bf16[128,1024]{1,0:T(8,128)(2,1)S(1)}, u32[]{:S(2)}, u32[]{:S(2)}) %collective-permute-start.6) | collective-permute-done | bytes 262176 | tf_op jit(solution)/shard_map/ppermute | solution.py:401
  108.7 0.7 copy-done.2
  109.4 5.0 %collective-permute-done.7.refs_6_ = bf16[128,1024]{1,0:T(8,128)(2,1)S(1)} collective-permute-done((bf16[128,1024]{1,0:T(8,128)(2,1)S(1)}, bf16[128,1024]{1,0:T(8,128)(2,1)S(1)}, u32[]{:S(2)}, u32[]{:S(2)}) %collective-permute-start.7) | collective-permute-done | bytes 262176 | tf_op jit(solution)/shard_map/ppermute | solution.py:401
  114.5 0.7 copy-done.4
  115.2 12.0 %collective-permute-done.8.refs_7_ = bf16[128,1024]{1,0:T(8,128)(2,1)S(1)} collective-permute-done((bf16[128,1024]{1,0:T(8,128)(2,1)S(1)}, bf16[128,1024]{1,0:T(8,128)(2,1)S(1)}, u32[]{:S(2)}, u32[]{:S(2)}) %collective-permute-start.8) | collective-permute-done | bytes 262176 | tf_op jit(solution)/shard_map/ppermute | solution.py:401
  127.2 0.7 copy-done.6
  127.9 0.0 all-to-all-done
  127.9 4.7 %all-to-all-start.1 = ((bf16[8,128,1024]{2,1,0:T(8,128)(2,1)}), bf16[8,128,1024]{2,1,0:T(8,128)(2,1)}, u32[]{:S(2)}, u32[]{:S(2)}) async-start(bf16[8,128,1024]{2,1,0:T(8,128)(2,1)} %state_b.1), calls=%async_computation.1 | async-start | bytes 4194304 | tf_op jit(solution)/shard_map/all_to_all | solution.py:398
  133.3 0.0 copy-done.9
  133.3 0.0 copy-start.3
  133.3 0.9 copy-done.3
  134.3 0.9 copy-done.5
  135.2 0.9 copy-done.7
  136.2 17.1 %transform.1.transform_ref = bf16[1024,1024]{1,0:T(8,128)(2,1)S(1)} custom-call(s32[1]{0:T(128)} %bitcast.place_ref, s32[1,1]{1,0:T(1,128)S(6)} %copy.10.tally_ref, f32[1,1024]{1,0:T(1,128)S(1)} %bitcast.45, bf16[16,1024]{1,0:T(8,128)(2,1)S(1)} %get-tuple-element.28.innov_ref, bf16[128,1024]{1,0:T(8,128)(2,1)S(1)} %get-tuple-element.32.refs_0_, ...), custom_call_target="tpu_custom_call" | custom-call | bytes 1048576 | tf_op jit(solution)/shard_map/transform/pallas_call | solution.py:319
  153.2 5.2 %analysed_a.1 = bf16[8,128,1024]{2,1,0:T(8,128)(2,1)S(1)} custom-call(s32[1]{0:T(128)} %bitcast.place_ref, bf16[1024,1024]{1,0:T(8,128)(2,1)S(1)} %transform.1.transform_ref, bf16[1024,1024]{1,0:T(8,128)(2,1)} %bitcast.14.state_ref), custom_call_target="tpu_custom_call" | custom-call | bytes 1048576 | tf_op jit(solution)/shard_map/analysed_a/pallas_call | solution.py:361
  158.4 1.1 slice_bitcast_fusion
  159.6 3.3 %collective-permute-start.10 = (bf16[128,1024]{1,0:T(8,128)(2,1)S(1)}, bf16[128,1024]{1,0:T(8,128)(2,1)S(1)}, u32[]{:S(2)}, u32[]{:S(2)}) collective-permute-start(bf16[128,1024]{1,0:T(8,128)(2,1)S(1)} %get-tuple-element.53), channel_id=1, source_target_pairs={{0,20},{4,16},{8,28},{12,24},{16,4},{20,0},{24,12},{28,8},{1,21},{... | collective-permute-start | bytes 786440 | tf_op jit(solution)/shard_map/ppermute | solution.py:401
  162.8 0.6 collective-permute-start.9
  163.4 24.8 %all-to-all-done.1 = bf16[8,128,1024]{2,1,0:T(8,128)(2,1)} async-done(((bf16[8,128,1024]{2,1,0:T(8,128)(2,1)}), bf16[8,128,1024]{2,1,0:T(8,128)(2,1)}, u32[]{:S(2)}, u32[]{:S(2)}) %all-to-all-start.1) | async-done | bytes 2097184 | tf_op jit(solution)/shard_map/all_to_all | solution.py:398
  188.2 5.1 %analysed_b.1 = bf16[8,128,1024]{2,1,0:T(8,128)(2,1)S(1)} custom-call(s32[1]{0:T(128)} %bitcast.place_ref, bf16[1024,1024]{1,0:T(8,128)(2,1)S(1)} %transform.1.transform_ref, bf16[1024,1024]{1,0:T(8,128)(2,1)} %bitcast.15.state_ref), custom_call_target="tpu_custom_call" | custom-call | bytes 1048576 | tf_op jit(solution)/shard_map/analysed_b/pallas_call | solution.py:361
  193.3 0.0 copy-start.1
  193.3 1.4 copy-done.1
  194.6 0.0 collective-permute-done.10.refs_5_
  194.6 4.7 %collective-permute-done.9.refs_4_ = bf16[128,1024]{1,0:T(8,128)(2,1)S(1)} collective-permute-done((bf16[128,1024]{1,0:T(8,128)(2,1)S(1)}, bf16[128,1024]{1,0:T(8,128)(2,1)S(1)}, u32[]{:S(2)}, u32[]{:S(2)}) %collective-permute-start.9) | collective-permute-done | bytes 262176 | tf_op jit(solution)/shard_map/ppermute | solution.py:401
  199.3 6.1 %all-to-all-start.2 = ((bf16[8,128,1024]{2,1,0:T(8,128)(2,1)}), bf16[8,128,1024]{2,1,0:T(8,128)(2,1)S(1)}, u32[]{:S(2)}, u32[]{:S(2)}) async-start(bf16[8,128,1024]{2,1,0:T(8,128)(2,1)} %copy-done.1), calls=%async_computation.2 | async-start | bytes 4194304 | tf_op jit(solution)/shard_map/all_to_all | solution.py:398
  205.4 1.5 collective-permute-start.11
  206.9 0.6 collective-permute-start.12
  207.5 1.5 collective-permute-start.13
  208.9 0.0 copy-done.11
  208.9 1.5 collective-permute-start.14
  210.4 1.5 collective-permute-start.15
  211.9 6.2 %collective-permute-done.11.refs_1_ = bf16[128,1024]{1,0:T(8,128)(2,1)S(1)} collective-permute-done((bf16[128,1024]{1,0:T(8,128)(2,1)}, bf16[128,1024]{1,0:T(8,128)(2,1)S(1)}, u32[]{:S(2)}, u32[]{:S(2)}) %collective-permute-start.11) | collective-permute-done | bytes 262176 | tf_op jit(solution)/shard_map/ppermute | solution.py:401
  218.1 10.4 %collective-permute-done.12.refs_2_ = bf16[128,1024]{1,0:T(8,128)(2,1)S(1)} collective-permute-done((bf16[128,1024]{1,0:T(8,128)(2,1)}, bf16[128,1024]{1,0:T(8,128)(2,1)S(1)}, u32[]{:S(2)}, u32[]{:S(2)}) %collective-permute-start.12) | collective-permute-done | bytes 262176 | tf_op jit(solution)/shard_map/ppermute | solution.py:401
  228.4 3.8 %collective-permute-done.13.refs_3_ = bf16[128,1024]{1,0:T(8,128)(2,1)S(1)} collective-permute-done((bf16[128,1024]{1,0:T(8,128)(2,1)}, bf16[128,1024]{1,0:T(8,128)(2,1)S(1)}, u32[]{:S(2)}, u32[]{:S(2)}) %collective-permute-start.13) | collective-permute-done | bytes 262176 | tf_op jit(solution)/shard_map/ppermute | solution.py:401
  232.2 7.9 %collective-permute-done.14.refs_6_ = bf16[128,1024]{1,0:T(8,128)(2,1)S(1)} collective-permute-done((bf16[128,1024]{1,0:T(8,128)(2,1)S(1)}, bf16[128,1024]{1,0:T(8,128)(2,1)S(1)}, u32[]{:S(2)}, u32[]{:S(2)}) %collective-permute-start.14) | collective-permute-done | bytes 262176 | tf_op jit(solution)/shard_map/ppermute | solution.py:401
  240.1 3.2 %collective-permute-done.15.refs_7_ = bf16[128,1024]{1,0:T(8,128)(2,1)S(1)} collective-permute-done((bf16[128,1024]{1,0:T(8,128)(2,1)S(1)}, bf16[128,1024]{1,0:T(8,128)(2,1)S(1)}, u32[]{:S(2)}, u32[]{:S(2)}) %collective-permute-start.15) | collective-permute-done | bytes 262176 | tf_op jit(solution)/shard_map/ppermute | solution.py:401
  243.3 1.6 analysis_a.1.whole_ref
  244.9 0.0 all-to-all-done.2.part_ref
  244.9 1.5 analysis_b.1
  (11 shorter events, 0.0 us)
Async XLA Ops:
  3.0 124.9 %all-to-all-start = ((bf16[8,128,1024]{2,1,0:T(8,128)(2,1)}), bf16[8,128,1024]{2,1,0:T(8,128)(2,1)}, u32[]{:S(2)}, u32[]{:S(2)}) async-start(bf16[8,128,1024]{2,1,0:T(8,128)(2,1)} %state_a.1), calls=%async_computation | async-start | bytes 4194304 | tf_op jit(solution)/shard_map/all_to_all | solution.py:398
  9.3 36.1 %copy-start.8 = (s32[1,8,1024]{2,1,0:T(8,128)S(1)}, s32[1,8,1024]{2,1,0:T(8,128)}, u32[]{:S(2)}) copy-start(s32[1,8,1024]{2,1,0:T(8,128)} %param.9) | copy-start | bytes 98308
  13.1 30.4 %collective-permute-start = (bf16[8,144,1024]{2,1,0:T(8,128)(2,1)}, bf16[8,144,1024]{2,1,0:T(8,128)(2,1)S(1)}, u32[]{:S(2)}, u32[]{:S(2)}) collective-permute-start(bf16[8,144,1024]{2,1,0:T(8,128)(2,1)} %pool_rows.1.own_ref), channel_id=1, source_target_pairs={{0,1},{1,2},{2,3},{4,5},{5,6},{6,7},{8,9},{9,10},{10,11},{12,13},{... | collective-permute-start | bytes 7077896 | tf_op jit(solution)/shard_map/ppermute | solution.py:410
  15.1 30.3 %collective-permute-start.1 = (bf16[8,144,1024]{2,1,0:T(8,128)(2,1)}, bf16[8,144,1024]{2,1,0:T(8,128)(2,1)}, u32[]{:S(2)}, u32[]{:S(2)}) collective-permute-start(bf16[8,144,1024]{2,1,0:T(8,128)(2,1)} %pool_rows.1.own_ref), channel_id=1, source_target_pairs={{1,0},{2,1},{3,2},{5,4},{6,5},{7,6},{9,8},{10,9},{11,10},{13,12},{... | collective-permute-start | bytes 7077896 | tf_op jit(solution)/shard_map/ppermute | solution.py:411
  45.4 1.7 copy-start
  69.1 7.5 %collective-permute-start.2 = (bf16[128,1024]{1,0:T(8,128)(2,1)S(1)}, bf16[128,1024]{1,0:T(8,128)(2,1)S(1)}, u32[]{:S(2)}, u32[]{:S(2)}) collective-permute-start(bf16[128,1024]{1,0:T(8,128)(2,1)S(1)} %get-tuple-element.61), channel_id=1, source_target_pairs={{0,4},{4,0},{8,12},{12,8},{16,20},{20,16},{24,28},{28,24},{1,5},{5... | collective-permute-start | bytes 786440 | tf_op jit(solution)/shard_map/ppermute | solution.py:401
  70.6 7.5 %collective-permute-start.3 = (bf16[128,1024]{1,0:T(8,128)(2,1)S(1)}, bf16[128,1024]{1,0:T(8,128)(2,1)S(1)}, u32[]{:S(2)}, u32[]{:S(2)}) collective-permute-start(bf16[128,1024]{1,0:T(8,128)(2,1)S(1)} %get-tuple-element.60), channel_id=1, source_target_pairs={{0,8},{4,12},{8,0},{12,4},{16,24},{20,28},{24,16},{28,20},{1,9},{5... | collective-permute-start | bytes 786440 | tf_op jit(solution)/shard_map/ppermute | solution.py:401
  71.2 10.8 %collective-permute-start.4 = (bf16[128,1024]{1,0:T(8,128)(2,1)S(1)}, bf16[128,1024]{1,0:T(8,128)(2,1)S(1)}, u32[]{:S(2)}, u32[]{:S(2)}) collective-permute-start(bf16[128,1024]{1,0:T(8,128)(2,1)S(1)} %get-tuple-element.59), channel_id=1, source_target_pairs={{0,12},{4,8},{8,4},{12,0},{16,28},{20,24},{24,20},{28,16},{1,13},{... | collective-permute-start | bytes 786440 | tf_op jit(solution)/shard_map/ppermute | solution.py:401
  72.7 20.7 %collective-permute-start.5 = (bf16[128,1024]{1,0:T(8,128)(2,1)S(1)}, bf16[128,1024]{1,0:T(8,128)(2,1)S(1)}, u32[]{:S(2)}, u32[]{:S(2)}) collective-permute-start(bf16[128,1024]{1,0:T(8,128)(2,1)S(1)} %get-tuple-element.58), channel_id=1, source_target_pairs={{0,16},{4,20},{8,24},{12,28},{16,0},{20,4},{24,8},{28,12},{1,17},{... | collective-permute-start | bytes 786440 | tf_op jit(solution)/shard_map/ppermute | solution.py:401
  75.1 33.6 %collective-permute-start.6 = (bf16[128,1024]{1,0:T(8,128)(2,1)S(1)}, bf16[128,1024]{1,0:T(8,128)(2,1)S(1)}, u32[]{:S(2)}, u32[]{:S(2)}) collective-permute-start(bf16[128,1024]{1,0:T(8,128)(2,1)S(1)} %get-tuple-element.57), channel_id=1, source_target_pairs={{0,20},{4,16},{8,28},{12,24},{16,4},{20,0},{24,12},{28,8},{1,21},{... | collective-permute-start | bytes 786440 | tf_op jit(solution)/shard_map/ppermute | solution.py:401
  76.6 37.8 %collective-permute-start.7 = (bf16[128,1024]{1,0:T(8,128)(2,1)S(1)}, bf16[128,1024]{1,0:T(8,128)(2,1)S(1)}, u32[]{:S(2)}, u32[]{:S(2)}) collective-permute-start(bf16[128,1024]{1,0:T(8,128)(2,1)S(1)} %get-tuple-element.56), channel_id=1, source_target_pairs={{0,24},{4,28},{8,16},{12,20},{16,8},{20,12},{24,0},{28,4},{1,25},{... | collective-permute-start | bytes 786440 | tf_op jit(solution)/shard_map/ppermute | solution.py:401
  78.1 49.1 %collective-permute-start.8 = (bf16[128,1024]{1,0:T(8,128)(2,1)S(1)}, bf16[128,1024]{1,0:T(8,128)(2,1)S(1)}, u32[]{:S(2)}, u32[]{:S(2)}) collective-permute-start(bf16[128,1024]{1,0:T(8,128)(2,1)S(1)} %get-tuple-element.55), channel_id=1, source_target_pairs={{0,28},{4,24},{8,20},{12,16},{16,12},{20,8},{24,4},{28,0},{1,29},{... | collective-permute-start | bytes 786440 | tf_op jit(solution)/shard_map/ppermute | solution.py:401
  108.7 0.7 copy-start.2
  114.5 0.7 copy-start.4
  127.2 0.7 copy-start.6
  127.9 5.4 %copy-start.9 = (f32[1,1,1024]{2,1,0:T(1,128)S(1)}, f32[1,1,1024]{2,1,0:T(1,128)}, u32[]{:S(2)}) copy-start(f32[1,1,1024]{2,1,0:T(1,128)} %param.11) | copy-start | bytes 12292
  127.9 60.3 %all-to-all-start.1 = ((bf16[8,128,1024]{2,1,0:T(8,128)(2,1)}), bf16[8,128,1024]{2,1,0:T(8,128)(2,1)}, u32[]{:S(2)}, u32[]{:S(2)}) async-start(bf16[8,128,1024]{2,1,0:T(8,128)(2,1)} %state_b.1), calls=%async_computation.1 | async-start | bytes 4194304 | tf_op jit(solution)/shard_map/all_to_all | solution.py:398
  133.3 1.0 copy-start.3
  134.3 0.9 copy-start.5
  135.2 0.9 copy-start.7
  159.6 35.1 %collective-permute-start.10 = (bf16[128,1024]{1,0:T(8,128)(2,1)S(1)}, bf16[128,1024]{1,0:T(8,128)(2,1)S(1)}, u32[]{:S(2)}, u32[]{:S(2)}) collective-permute-start(bf16[128,1024]{1,0:T(8,128)(2,1)S(1)} %get-tuple-element.53), channel_id=1, source_target_pairs={{0,20},{4,16},{8,28},{12,24},{16,4},{20,0},{24,12},{28,8},{1,21},{... | collective-permute-start | bytes 786440 | tf_op jit(solution)/shard_map/ppermute | solution.py:401
  162.8 36.5 %collective-permute-start.9 = (bf16[128,1024]{1,0:T(8,128)(2,1)S(1)}, bf16[128,1024]{1,0:T(8,128)(2,1)S(1)}, u32[]{:S(2)}, u32[]{:S(2)}) collective-permute-start(bf16[128,1024]{1,0:T(8,128)(2,1)S(1)} %get-tuple-element.54), channel_id=1, source_target_pairs={{0,16},{4,20},{8,24},{12,28},{16,0},{20,4},{24,8},{28,12},{1,17},{... | collective-permute-start | bytes 786440 | tf_op jit(solution)/shard_map/ppermute | solution.py:401
  193.3 1.4 copy-start.1
  194.6 14.3 %copy-start.11 = (bf16[128,1024]{1,0:T(8,128)(2,1)S(1)}, bf16[128,1024]{1,0:T(8,128)(2,1)}, u32[]{:S(2)}) copy-start(bf16[128,1024]{1,0:T(8,128)(2,1)} %get-tuple-element.48) | copy-start | bytes 786436
  194.6 15.8 %copy-start.10 = (bf16[128,1024]{1,0:T(8,128)(2,1)S(1)}, bf16[128,1024]{1,0:T(8,128)(2,1)}, u32[]{:S(2)}) copy-start(bf16[128,1024]{1,0:T(8,128)(2,1)} %get-tuple-element.47) | copy-start | bytes 786436
  199.3 45.6 %all-to-all-start.2 = ((bf16[8,128,1024]{2,1,0:T(8,128)(2,1)}), bf16[8,128,1024]{2,1,0:T(8,128)(2,1)S(1)}, u32[]{:S(2)}, u32[]{:S(2)}) async-start(bf16[8,128,1024]{2,1,0:T(8,128)(2,1)} %copy-done.1), calls=%async_computation.2 | async-start | bytes 4194304 | tf_op jit(solution)/shard_map/all_to_all | solution.py:398
  205.4 12.6 %collective-permute-start.11 = (bf16[128,1024]{1,0:T(8,128)(2,1)}, bf16[128,1024]{1,0:T(8,128)(2,1)S(1)}, u32[]{:S(2)}, u32[]{:S(2)}) collective-permute-start(bf16[128,1024]{1,0:T(8,128)(2,1)} %get-tuple-element.51), channel_id=1, source_target_pairs={{0,4},{4,0},{8,12},{12,8},{16,20},{20,16},{24,28},{28,24},{1,5},{5... | collective-permute-start | bytes 786440 | tf_op jit(solution)/shard_map/ppermute | solution.py:401
  206.9 21.5 %collective-permute-start.12 = (bf16[128,1024]{1,0:T(8,128)(2,1)}, bf16[128,1024]{1,0:T(8,128)(2,1)S(1)}, u32[]{:S(2)}, u32[]{:S(2)}) collective-permute-start(bf16[128,1024]{1,0:T(8,128)(2,1)} %get-tuple-element.50), channel_id=1, source_target_pairs={{0,8},{4,12},{8,0},{12,4},{16,24},{20,28},{24,16},{28,20},{1,9},{5... | collective-permute-start | bytes 786440 | tf_op jit(solution)/shard_map/ppermute | solution.py:401
  207.5 24.8 %collective-permute-start.13 = (bf16[128,1024]{1,0:T(8,128)(2,1)}, bf16[128,1024]{1,0:T(8,128)(2,1)S(1)}, u32[]{:S(2)}, u32[]{:S(2)}) collective-permute-start(bf16[128,1024]{1,0:T(8,128)(2,1)} %get-tuple-element.49), channel_id=1, source_target_pairs={{0,12},{4,8},{8,4},{12,0},{16,28},{20,24},{24,20},{28,16},{1,13},{... | collective-permute-start | bytes 786440 | tf_op jit(solution)/shard_map/ppermute | solution.py:401
  208.9 31.2 %collective-permute-start.14 = (bf16[128,1024]{1,0:T(8,128)(2,1)S(1)}, bf16[128,1024]{1,0:T(8,128)(2,1)S(1)}, u32[]{:S(2)}, u32[]{:S(2)}) collective-permute-start(bf16[128,1024]{1,0:T(8,128)(2,1)S(1)} %copy-done.11), channel_id=1, source_target_pairs={{0,24},{4,28},{8,16},{12,20},{16,8},{20,12},{24,0},{28,4},{1,25},{... | collective-permute-start | bytes 786440 | tf_op jit(solution)/shard_map/ppermute | solution.py:401
  210.4 32.9 %collective-permute-start.15 = (bf16[128,1024]{1,0:T(8,128)(2,1)S(1)}, bf16[128,1024]{1,0:T(8,128)(2,1)S(1)}, u32[]{:S(2)}, u32[]{:S(2)}) collective-permute-start(bf16[128,1024]{1,0:T(8,128)(2,1)S(1)} %copy-done.10), channel_id=1, source_target_pairs={{0,28},{4,24},{8,20},{12,16},{16,12},{20,8},{24,4},{28,0},{1,29},{... | collective-permute-start | bytes 786440 | tf_op jit(solution)/shard_map/ppermute | solution.py:401

commit v8 on v7

--- a/solution.py
+++ b/solution.py
@@ -11,7 +11,7 @@
 SLOT_CHUNK = 256
 MEMBER_TILE = 32
 TRANSFORM_CHUNK = 256
-ANALYSIS_TILE = 256
+ANALYSIS_TILE = 128
 MIB = 1024 * 1024
 
 
@@ -88,66 +88,63 @@
     )(obs, innov)
 
 
-def gather_kernel(first, place_ref, own_ref, up_ref, down_ref, idx_ref, out_ref, *inn_refs):
-    block = (pl.program_id(0) + first) ^ place_ref[0]
+def gather_kernel(place_ref, own_ref, up_ref, down_ref, idx_ref, out_ref, inn_ref, stacked):
+    block = pl.program_id(0) ^ place_ref[0]
     blocks, rows, depth = own_ref.shape
     members = out_ref.shape[1]
     slots = out_ref.shape[2]
-    if not inn_refs:
-        rows = members
     west = jnp.maximum(block - 1, 0)
     east = jnp.minimum(block + 1, blocks - 1)
     sources = (
-        (own_ref, block, None),
-        (up_ref, block, None),
-        (down_ref, block, None),
-        (own_ref, west, block > 0),
-        (own_ref, east, block < blocks - 1),
+        own_ref[block, :rows],
+        up_ref[block, :rows],
+        down_ref[block, :rows],
+        jnp.where(block > 0, own_ref[west, :rows], 0.0),
+        jnp.where(block < blocks - 1, own_ref[east, :rows], 0.0),
     )
+    for number, source in enumerate(sources):
+        stacked[number * rows : (number + 1) * rows] = source.astype(jnp.bfloat16)
     columns = lax.broadcasted_iota(jnp.int32, (depth, SLOT_CHUNK), 0)
 
     @pl.loop(0, slots // SLOT_CHUNK)
     def _(chunk):
         where = pl.ds(pl.multiple_of(chunk * SLOT_CHUNK, SLOT_CHUNK), SLOT_CHUNK)
         picks = idx_ref[pl.ds(block, 1), where]
-        acc = jnp.zeros((rows, SLOT_CHUNK), jnp.float32)
-        for number, (ref, at, live) in enumerate(sources):
-            local = picks - number * depth
-            if live is not None:
-                local = jnp.where(live, local, -1)
-            one_hot = jnp.where(columns == local, 1.0, 0.0).astype(jnp.bfloat16)
-            acc += jnp.dot(ref[at, :rows], one_hot, preferred_element_type=jnp.float32)
-        out_ref[0, :, where] = acc[:members].astype(jnp.bfloat16)
-        for inn_ref in inn_refs:
-
-            @pl.when(pl.program_id(0) == 0)
-            def _():
-                inn_ref[:, where] = acc[members:].astype(jnp.bfloat16)
-
-
-def gather_chosen(place, own, up, down, picks, first, count, name):
+        source = sum((picks >= number * depth).astype(jnp.int32) for number in range(1, 5))
+        one_hot = jnp.where(columns == picks - source * depth, 1.0, 0.0).astype(jnp.bfloat16)
+        products = jnp.dot(stacked[...], one_hot, preferred_element_type=jnp.float32)
+        chosen = products[:rows]
+        for number in range(1, 5):
+            part = products[number * rows : (number + 1) * rows]
+            chosen = jnp.where(source == number, part, chosen)
+        out_ref[0, :, where] = chosen[:members].astype(jnp.bfloat16)
+
+        @pl.when(pl.program_id(0) == 0)
+        def _():
+            inn_ref[:, where] = chosen[members:].astype(jnp.bfloat16)
+
+
+def gather_chosen(place, own, up, down, picks):
     blocks, rows, depth = own.shape
     members = rows - INNOV_ROWS
     slots = picks.shape[1]
     vmem = pl.BlockSpec(memory_space=pltpu.VMEM)
-    out_specs = [pl.BlockSpec((1, members, slots), lambda k: (k, 0, 0))]
-    out_shape = [jax.ShapeDtypeStruct((count, members, slots), jnp.bfloat16)]
-    if first == 0:
-        out_specs.append(pl.BlockSpec((INNOV_ROWS, slots), lambda k: (0, 0)))
-        out_shape.append(jax.ShapeDtypeStruct((INNOV_ROWS, slots), jnp.bfloat16))
-    return pl.pallas_call(
-        functools.partial(gather_kernel, first),
-        grid=(count,),
+    return pl.pallas_call(
+        gather_kernel,
+        grid=(blocks,),
         in_specs=[pl.BlockSpec(memory_space=pltpu.SMEM)] + [vmem] * 4,
-        out_specs=out_specs,
-        out_shape=out_shape,
+        out_specs=[
+            pl.BlockSpec((1, members, slots), lambda k: (k, 0, 0)),
+            pl.BlockSpec((INNOV_ROWS, slots), lambda k: (0, 0)),
+        ],
+        out_shape=[
+            jax.ShapeDtypeStruct((blocks, members, slots), jnp.bfloat16),
+            jax.ShapeDtypeStruct((INNOV_ROWS, slots), jnp.bfloat16),
+        ],
+        scratch_shapes=[pltpu.VMEM((5 * rows, depth), jnp.bfloat16)],
         compiler_params=pltpu.CompilerParams(vmem_limit_bytes=40 * MIB),
-        cost_estimate=pl.CostEstimate(
-            flops=0,
-            bytes_accessed=rows * slots,
-            transcendentals=0,
-        ),
-        name=name,
+        cost_estimate=pl.CostEstimate(flops=0, bytes_accessed=rows * slots, transcendentals=0),
+        name="gather_chosen",
     )(place, own, up, down, picks)
 
 
@@ -166,12 +163,13 @@
         copy.wait()
 
 
-def to_members_kernel(start, part_ref, whole_ref, out_ref, stage, sent):
+def to_members_kernel(start, part_ref, out_ref, stage, sent):
     store_tiles(out_ref, start, stage, sent, lambda rows: jnp.swapaxes(part_ref[:, rows, :], 0, 1))
 
 
-def pairs_to_members_kernel(start, place_ref, *refs):
+def pairs_to_members_kernel(start, place_ref, whole_ref, *refs):
     *part_refs, out_ref, turned, stage, sent = refs
+    del whole_ref
 
     def make(rows):
         for number, ref in enumerate(part_refs):
@@ -181,47 +179,47 @@
     store_tiles(out_ref, start, stage, sent, make)
 
 
-def to_members(part, start, whole, name):
+def to_members(part, start, entries, name):
     blocks, members, width = part.shape
-    hbm = pl.BlockSpec(memory_space=pltpu.HBM)
     return pl.pallas_call(
         functools.partial(to_members_kernel, start),
-        in_specs=[pl.BlockSpec(memory_space=pltpu.VMEM), hbm],
-        out_specs=hbm,
-        out_shape=jax.ShapeDtypeStruct(whole.shape, part.dtype),
+        in_specs=[pl.BlockSpec(memory_space=pltpu.VMEM)],
+        out_specs=pl.BlockSpec(memory_space=pltpu.HBM),
+        out_shape=jax.ShapeDtypeStruct((members, blocks, entries), part.dtype),
         scratch_shapes=[
             pltpu.VMEM((members, blocks, width), part.dtype),
             pltpu.SemaphoreType.DMA((members // MEMBER_TILE,)),
         ],
+        compiler_params=pltpu.CompilerParams(vmem_limit_bytes=16 * MIB),
+        cost_estimate=pl.CostEstimate(
+            flops=0, bytes_accessed=4 * members * blocks * width, transcendentals=0
+        ),
+        name=name,
+    )(part)
+
+
+def pairs_to_members(place, parts, start, whole, name):
+    blocks = len(parts)
+    members, width = parts[0].shape
+    hbm = pl.BlockSpec(memory_space=pltpu.HBM)
+    return pl.pallas_call(
+        functools.partial(pairs_to_members_kernel, start),
+        in_specs=[pl.BlockSpec(memory_space=pltpu.SMEM), hbm]
+        + [pl.BlockSpec(memory_space=pltpu.VMEM)] * blocks,
+        out_specs=hbm,
+        out_shape=jax.ShapeDtypeStruct(whole.shape, whole.dtype),
+        scratch_shapes=[
+            pltpu.VMEM((blocks, MEMBER_TILE, width), whole.dtype),
+            pltpu.VMEM((members, blocks, width), whole.dtype),
+            pltpu.SemaphoreType.DMA((members // MEMBER_TILE,)),
+        ],
         input_output_aliases={1: 0},
         compiler_params=pltpu.CompilerParams(vmem_limit_bytes=16 * MIB),
         cost_estimate=pl.CostEstimate(
             flops=0, bytes_accessed=4 * members * blocks * width, transcendentals=0
         ),
         name=name,
-    )(part, whole)
-
-
-def pairs_to_members(place, parts, start, entries, name):
-    blocks = len(parts)
-    members, width = parts[0].shape
-    return pl.pallas_call(
-        functools.partial(pairs_to_members_kernel, start),
-        in_specs=[pl.BlockSpec(memory_space=pltpu.SMEM)]
-        + [pl.BlockSpec(memory_space=pltpu.VMEM)] * blocks,
-        out_specs=pl.BlockSpec(memory_space=pltpu.HBM),
-        out_shape=jax.ShapeDtypeStruct((members, blocks, entries), parts[0].dtype),
-        scratch_shapes=[
-            pltpu.VMEM((blocks, MEMBER_TILE, width), parts[0].dtype),
-            pltpu.VMEM((members, blocks, width), parts[0].dtype),
-            pltpu.SemaphoreType.DMA((members // MEMBER_TILE,)),
-        ],
-        compiler_params=pltpu.CompilerParams(vmem_limit_bytes=16 * MIB),
-        cost_estimate=pl.CostEstimate(
-            flops=0, bytes_accessed=4 * members * blocks * width, transcendentals=0
-        ),
-        name=name,
-    )(place, *parts)
+    )(place, whole, *parts)
 
 
 def transform_kernel(place_ref, tally_ref, weight_ref, innov_ref, *refs):
@@ -409,12 +407,9 @@
     pool = pool_rows(devs, measured_minus_predicted[0])
     up = lax.ppermute(pool, "reg", to_next)
     down = lax.ppermute(pool, "reg", to_last)
-    picks = measure_pool_indices[0]
-    far = gather_chosen(place, pool, up, down, picks, half, half, "gather_far")[0]
-    pool, far = lax.optimization_barrier((pool, far))
-    far = [swap(far[k], k + half) for k in range(half)]
-    near, innov = gather_chosen(place, pool, up, down, picks, 0, half, "gather_near")
-    near = [near[0]] + [swap(near[k], k) for k in range(1, half)]
+    chosen, innov = gather_chosen(place, pool, up, down, measure_pool_indices[0])
+    far = [swap(chosen[k], k) for k in range(half, devices)]
+    near = [chosen[0]] + [swap(chosen[k], k) for k in range(1, half)]
     state_b = to_blocks(state, width, entries - width, "state_b")
     near, far, state_a, state_b = lax.optimization_barrier((near, far, state_a, state_b))
     state_b = exchange(state_b)
@@ -429,8 +424,8 @@
         (done_b, *done_a[half : half + 2])
     )
     done_b = exchange(done_b)
-    whole = pairs_to_members(place, done_a, 0, entries, "analysis_a")
-    whole = to_members(done_b, width, whole, "analysis_b")
+    whole = to_members(done_b, width, entries, "analysis_b")
+    whole = pairs_to_members(place, done_a, 0, whole, "analysis_a")
     return whole[:, None]
 
 

time: 247 us -> 243 us (0.984)
  the two profiles are of different devices: /device:TPU:10 before, /device:TPU:9 now
where the time goes in v8:
time: 243 us; the launch traced here: 242 us
  waiting for transfers between devices  124 us (51%)
  Pallas kernels  70 us (29%)
  starting transfers between devices  36.9 us (15%)
  local copies, waits for them, and re-layouts  9.89 us (4%)
    ppermute x14, waiting for transfers between devices, swap(): return lax.ppermute(x, 'mem', [(i, i ^ number) for i in range(devices)])  61.3 us
    all_to_all x3, waiting for transfers between devices, exchange(): return lax.all_to_all(x, 'mem', split_axis=0, concat_axis=0, tiled=True)  34.1 us
    ppermute x1, waiting for transfers between devices, body(): up = lax.ppermute(pool, 'reg', to_next)  24.1 us
    pallas_call x1, Pallas kernels, gather_chosen(): pl.pallas_call(gather_kernel, grid=(blocks,), in_specs=[pl.BlockSpec(memo...  21.2 us
    pallas_call x1, Pallas kernels, ensemble_transform(): pl.pallas_call(transform_kernel, in_specs=[pl.BlockSpec(memory_space=pltp...  18.1 us
    pallas_call x2, Pallas kernels, analysed(): pl.pallas_call(functools.partial(analysis_kernel, in_pairs), grid=(width...  16.7 us
    all_to_all x3, starting transfers between devices, exchange(): return lax.all_to_all(x, 'mem', split_axis=0, concat_axis=0, tiled=True)  16 us
    ppermute x14, starting transfers between devices, swap(): return lax.ppermute(x, 'mem', [(i, i ^ number) for i in range(devices)])  14.7 us
  transfers between devices with their start and end apart: 19, of which 11 were waited for; matrix products, arithmetic and copies ran while one was open for 1% of the time, Pallas kernels for 27%

profile of v8, /device:TPU:9, one launch (start us, length us, event | category | flops | bytes accessed | tf_op | source)
XLA Modules:
  0.0 241.8 jit_solution(7736655810054315806)
XLA Ops:
  0.0 3.0 %state_a.1 = bf16[8,128,1024]{2,1,0:T(8,128)(2,1)} custom-call(bf16[128,8,2048]{2,1,0:T(8,128)(2,1)} %bitcast.46), custom_call_target="tpu_custom_call" | custom-call | bytes 4194304 | tf_op jit(solution)/shard_map/state_a/pallas_call | solution.py:42
  3.0 5.7 %all-to-all-start = ((bf16[8,128,1024]{2,1,0:T(8,128)(2,1)}), bf16[8,128,1024]{2,1,0:T(8,128)(2,1)S(1)}, u32[]{:S(2)}, u32[]{:S(2)}) async-start(bf16[8,128,1024]{2,1,0:T(8,128)(2,1)} %state_a.1), calls=%async_computation | async-start | bytes 4194304 | tf_op jit(solution)/shard_map/all_to_all | solution.py:396
  8.8 0.0 copy-start.8
  8.8 3.8 %pool_rows.1.own_ref = bf16[8,144,1024]{2,1,0:T(8,128)(2,1)} custom-call(bf16[128,8,1024]{2,1,0:T(8,128)(2,1)} %bitcast.48, bf16[8,1024]{1,0:T(8,128)(2,1)} %bitcast.49), custom_call_target="tpu_custom_call" | custom-call | bytes 4718592 | tf_op jit(solution)/shard_map/pool_rows/pallas_call | solution.py:74
  12.6 4.2 %collective-permute-start = (bf16[8,144,1024]{2,1,0:T(8,128)(2,1)}, bf16[8,144,1024]{2,1,0:T(8,128)(2,1)}, u32[]{:S(2)}, u32[]{:S(2)}) collective-permute-start(bf16[8,144,1024]{2,1,0:T(8,128)(2,1)} %pool_rows.1.own_ref), channel_id=1, source_target_pairs={{0,1},{1,2},{2,3},{4,5},{5,6},{6,7},{8,9},{9,10},{10,11},{12,13},{... | collective-permute-start | bytes 7077896 | tf_op jit(solution)/shard_map/ppermute | solution.py:408
  16.8 1.9 collective-permute-start.1
  18.8 24.1 %collective-permute-done.up_ref = bf16[8,144,1024]{2,1,0:T(8,128)(2,1)} collective-permute-done((bf16[8,144,1024]{2,1,0:T(8,128)(2,1)}, bf16[8,144,1024]{2,1,0:T(8,128)(2,1)}, u32[]{:S(2)}, u32[]{:S(2)}) %collective-permute-start) | collective-permute-done | bytes 2359328 | tf_op jit(solution)/shard_map/ppermute | solution.py:408
  42.9 4.6 %collective-permute-done.1.down_ref = bf16[8,144,1024]{2,1,0:T(8,128)(2,1)} collective-permute-done((bf16[8,144,1024]{2,1,0:T(8,128)(2,1)}, bf16[8,144,1024]{2,1,0:T(8,128)(2,1)}, u32[]{:S(2)}, u32[]{:S(2)}) %collective-permute-start.1) | collective-permute-done | bytes 2359328 | tf_op jit(solution)/shard_map/ppermute | solution.py:409
  47.5 0.0 copy-done.8
  47.5 0.0 copy-start
  47.5 1.7 copy-done
  49.2 21.2 %gather_chosen.1 = (bf16[8,128,1024]{2,1,0:T(8,128)(2,1)S(1)}, bf16[16,1024]{1,0:T(8,128)(2,1)S(1)}) custom-call(s32[1]{0:T(128)} %bitcast.place_ref, bf16[8,144,1024]{2,1,0:T(8,128)(2,1)S(1)} %copy-done, bf16[8,144,1024]{2,1,0:T(8,128)(2,1)} %collective-permute-done.up_ref, bf16[8,144,1024]{2,1,0:T(8,128)(2,1)} %collective-permute-done.1.down_ref, ...), custom_call_target="tpu_custom_call" | custom-call | bytes 147456 | tf_op jit(solution)/shard_map/gather_chosen/pallas_call | solution.py:132
  70.4 1.2 slice_bitcast_fusion.8
  71.6 1.0 collective-permute-start.2
  72.6 0.5 collective-permute-start.3
  73.1 1.2 collective-permute-start.4
  74.3 1.9 collective-permute-start.5
  76.2 1.2 collective-permute-start.6
  77.3 5.1 %collective-permute-done.2.refs_1_ = bf16[128,1024]{1,0:T(8,128)(2,1)S(1)} collective-permute-done((bf16[128,1024]{1,0:T(8,128)(2,1)S(1)}, bf16[128,1024]{1,0:T(8,128)(2,1)S(1)}, u32[]{:S(2)}, u32[]{:S(2)}) %collective-permute-start.2) | collective-permute-done | bytes 262176 | tf_op jit(solution)/shard_map/ppermute | solution.py:399
  82.5 1.2 collective-permute-start.7
  83.7 0.0 collective-permute-done.3.refs_2_
  83.7 1.0 collective-permute-start.8
  84.6 3.0 %state_b.1 = bf16[8,128,1024]{2,1,0:T(8,128)(2,1)} custom-call(bf16[128,8,2048]{2,1,0:T(8,128)(2,1)} %bitcast.47), custom_call_target="tpu_custom_call" | custom-call | bytes 4194304 | tf_op jit(solution)/shard_map/state_b/pallas_call | solution.py:42
  87.7 0.0 collective-permute-done.4.refs_3_
  87.7 0.0 collective-permute-done.5.refs_4_
  87.7 15.2 %collective-permute-done.6.refs_5_ = bf16[128,1024]{1,0:T(8,128)(2,1)S(1)} collective-permute-done((bf16[128,1024]{1,0:T(8,128)(2,1)}, bf16[128,1024]{1,0:T(8,128)(2,1)S(1)}, u32[]{:S(2)}, u32[]{:S(2)}) %collective-permute-start.6) | collective-permute-done | bytes 262176 | tf_op jit(solution)/shard_map/ppermute | solution.py:399
  102.9 0.0 copy-start.4
  102.9 0.7 copy-done.4
  103.6 11.0 %collective-permute-done.7.refs_6_ = bf16[128,1024]{1,0:T(8,128)(2,1)S(1)} collective-permute-done((bf16[128,1024]{1,0:T(8,128)(2,1)}, bf16[128,1024]{1,0:T(8,128)(2,1)S(1)}, u32[]{:S(2)}, u32[]{:S(2)}) %collective-permute-start.7) | collective-permute-done | bytes 262176 | tf_op jit(solution)/shard_map/ppermute | solution.py:399
  114.6 0.7 copy-done.6
  115.2 6.8 %collective-permute-done.8.refs_7_ = bf16[128,1024]{1,0:T(8,128)(2,1)} collective-permute-done((bf16[128,1024]{1,0:T(8,128)(2,1)}, bf16[128,1024]{1,0:T(8,128)(2,1)}, u32[]{:S(2)}, u32[]{:S(2)}) %collective-permute-start.8) | collective-permute-done | bytes 262176 | tf_op jit(solution)/shard_map/ppermute | solution.py:399
  122.1 0.0 all-to-all-done
  122.1 1.3 copy-done.1
  123.5 4.3 %all-to-all-start.1 = ((bf16[8,128,1024]{2,1,0:T(8,128)(2,1)}), bf16[8,128,1024]{2,1,0:T(8,128)(2,1)}, u32[]{:S(2)}, u32[]{:S(2)}) async-start(bf16[8,128,1024]{2,1,0:T(8,128)(2,1)} %state_b.1), calls=%async_computation.1 | async-start | bytes 4194304 | tf_op jit(solution)/shard_map/all_to_all | solution.py:396
  128.4 0.0 copy-done.9
  128.4 0.0 copy-start.5
  128.4 0.9 copy-done.5
  129.4 0.9 copy-done.7
  130.3 18.1 %transform.1.transform_ref = bf16[1024,1024]{1,0:T(8,128)(2,1)S(1)} custom-call(s32[1]{0:T(128)} %bitcast.place_ref, s32[1,1]{1,0:T(1,128)S(6)} %copy.10.tally_ref, f32[1,1024]{1,0:T(1,128)S(1)} %bitcast.45, bf16[16,1024]{1,0:T(8,128)(2,1)S(1)} %get-tuple-element.25.innov_ref, bf16[128,1024]{1,0:T(8,128)(2,1)S(1)} %get-tuple-element.28.refs_0_, ...), custom_call_target="tpu_custom_call" | custom-call | bytes 1048576 | tf_op jit(solution)/shard_map/transform/pallas_call | solution.py:317
  148.4 0.0 copy-done.2
  148.4 8.2 %analysed_a.1 = bf16[8,128,1024]{2,1,0:T(8,128)(2,1)S(1)} custom-call(s32[1]{0:T(128)} %bitcast.place_ref, bf16[1024,1024]{1,0:T(8,128)(2,1)S(1)} %transform.1.transform_ref, bf16[1024,1024]{1,0:T(8,128)(2,1)S(1)} %bitcast.43), custom_call_target="tpu_custom_call" | custom-call | bytes 1048576 | tf_op jit(solution)/shard_map/analysed_a/pallas_call | solution.py:359
  156.7 1.1 slice_bitcast_fusion
  157.8 1.6 collective-permute-start.10
  159.3 0.3 collective-permute-start.9
  159.6 0.0 all-to-all-done.1
  159.6 8.4 %analysed_b.1 = bf16[8,128,1024]{2,1,0:T(8,128)(2,1)S(1)} custom-call(s32[1]{0:T(128)} %bitcast.place_ref, bf16[1024,1024]{1,0:T(8,128)(2,1)S(1)} %transform.1.transform_ref, bf16[1024,1024]{1,0:T(8,128)(2,1)} %bitcast.15.state_ref), custom_call_target="tpu_custom_call" | custom-call | bytes 1048576 | tf_op jit(solution)/shard_map/analysed_b/pallas_call | solution.py:359
  168.0 0.0 copy-start.3
  168.0 1.3 copy-done.3
  169.4 6.5 %collective-permute-done.10.refs_5_ = bf16[128,1024]{1,0:T(8,128)(2,1)S(1)} collective-permute-done((bf16[128,1024]{1,0:T(8,128)(2,1)S(1)}, bf16[128,1024]{1,0:T(8,128)(2,1)S(1)}, u32[]{:S(2)}, u32[]{:S(2)}) %collective-permute-start.10) | collective-permute-done | bytes 262176 | tf_op jit(solution)/shard_map/ppermute | solution.py:399
  175.8 11.2 %collective-permute-done.9.refs_4_ = bf16[128,1024]{1,0:T(8,128)(2,1)S(1)} collective-permute-done((bf16[128,1024]{1,0:T(8,128)(2,1)S(1)}, bf16[128,1024]{1,0:T(8,128)(2,1)S(1)}, u32[]{:S(2)}, u32[]{:S(2)}) %collective-permute-start.9) | collective-permute-done | bytes 262176 | tf_op jit(solution)/shard_map/ppermute | solution.py:399
  187.1 6.0 %all-to-all-start.2 = ((bf16[8,128,1024]{2,1,0:T(8,128)(2,1)}), bf16[8,128,1024]{2,1,0:T(8,128)(2,1)S(1)}, u32[]{:S(2)}, u32[]{:S(2)}) async-start(bf16[8,128,1024]{2,1,0:T(8,128)(2,1)} %copy-done.3), calls=%async_computation.2 | async-start | bytes 4194304 | tf_op jit(solution)/shard_map/all_to_all | solution.py:396
  193.1 1.2 collective-permute-start.11
  194.3 0.3 collective-permute-start.12
  194.5 1.2 collective-permute-start.13
  195.7 1.2 collective-permute-start.14
  196.9 1.2 collective-permute-start.15
  198.1 34.1 %all-to-all-done.2.part_ref = bf16[8,128,1024]{2,1,0:T(8,128)(2,1)S(1)} async-done(((bf16[8,128,1024]{2,1,0:T(8,128)(2,1)}), bf16[8,128,1024]{2,1,0:T(8,128)(2,1)S(1)}, u32[]{:S(2)}, u32[]{:S(2)}) %all-to-all-start.2) | async-done | bytes 2097184 | tf_op jit(solution)/shard_map/all_to_all | solution.py:396
  232.2 1.5 analysis_b.1.whole_ref
  233.7 0.0 collective-permute-done.11.refs_1_
  233.7 0.0 collective-permute-done.12.refs_2_
  233.7 0.0 collective-permute-done.13.refs_3_
  233.7 1.9 collective-permute-done.14.refs_6_
  235.6 3.5 %collective-permute-done.15.refs_7_ = bf16[128,1024]{1,0:T(8,128)(2,1)} collective-permute-done((bf16[128,1024]{1,0:T(8,128)(2,1)}, bf16[128,1024]{1,0:T(8,128)(2,1)}, u32[]{:S(2)}, u32[]{:S(2)}) %collective-permute-start.15) | collective-permute-done | bytes 262176 | tf_op jit(solution)/shard_map/ppermute | solution.py:399
  239.1 2.7 %analysis_a.1 = bf16[128,8,2048]{2,1,0:T(8,128)(2,1)} custom-call(s32[1]{0:T(128)} %bitcast.place_ref, bf16[128,8,2048]{2,1,0:T(8,128)(2,1)} %analysis_b.1.whole_ref, bf16[128,1024]{1,0:T(8,128)(2,1)S(1)} %get-tuple-element.48.refs_0_, bf16[128,1024]{1,0:T(8,128)(2,1)S(1)} %collective-permute-done.11.refs_1_, ...), custom_call_target="tpu_custom_call", output_to_operand_aliasing={{}: (1, {})} | custom-call | bytes 4194304 | tf_op jit(solution)/shard_map/analysis_a/pallas_call | solution.py:205
  (5 shorter events, 0.0 us)
Async XLA Ops:
  3.0 119.1 %all-to-all-start = ((bf16[8,128,1024]{2,1,0:T(8,128)(2,1)}), bf16[8,128,1024]{2,1,0:T(8,128)(2,1)S(1)}, u32[]{:S(2)}, u32[]{:S(2)}) async-start(bf16[8,128,1024]{2,1,0:T(8,128)(2,1)} %state_a.1), calls=%async_computation | async-start | bytes 4194304 | tf_op jit(solution)/shard_map/all_to_all | solution.py:396
  8.8 38.7 %copy-start.8 = (s32[1,8,1024]{2,1,0:T(8,128)S(1)}, s32[1,8,1024]{2,1,0:T(8,128)}, u32[]{:S(2)}) copy-start(s32[1,8,1024]{2,1,0:T(8,128)} %param.9) | copy-start | bytes 98308
  12.6 30.3 %collective-permute-start = (bf16[8,144,1024]{2,1,0:T(8,128)(2,1)}, bf16[8,144,1024]{2,1,0:T(8,128)(2,1)}, u32[]{:S(2)}, u32[]{:S(2)}) collective-permute-start(bf16[8,144,1024]{2,1,0:T(8,128)(2,1)} %pool_rows.1.own_ref), channel_id=1, source_target_pairs={{0,1},{1,2},{2,3},{4,5},{5,6},{6,7},{8,9},{9,10},{10,11},{12,13},{... | collective-permute-start | bytes 7077896 | tf_op jit(solution)/shard_map/ppermute | solution.py:408
  16.8 30.7 %collective-permute-start.1 = (bf16[8,144,1024]{2,1,0:T(8,128)(2,1)}, bf16[8,144,1024]{2,1,0:T(8,128)(2,1)}, u32[]{:S(2)}, u32[]{:S(2)}) collective-permute-start(bf16[8,144,1024]{2,1,0:T(8,128)(2,1)} %pool_rows.1.own_ref), channel_id=1, source_target_pairs={{1,0},{2,1},{3,2},{5,4},{6,5},{7,6},{9,8},{10,9},{11,10},{13,12},{... | collective-permute-start | bytes 7077896 | tf_op jit(solution)/shard_map/ppermute | solution.py:409
  47.5 1.7 copy-start
  71.6 10.8 %collective-permute-start.2 = (bf16[128,1024]{1,0:T(8,128)(2,1)S(1)}, bf16[128,1024]{1,0:T(8,128)(2,1)S(1)}, u32[]{:S(2)}, u32[]{:S(2)}) collective-permute-start(bf16[128,1024]{1,0:T(8,128)(2,1)S(1)} %get-tuple-element.57), channel_id=1, source_target_pairs={{0,4},{4,0},{8,12},{12,8},{16,20},{20,16},{24,28},{28,24},{1,5},{5... | collective-permute-start | bytes 786440 | tf_op jit(solution)/shard_map/ppermute | solution.py:399
  72.6 11.0 %collective-permute-start.3 = (bf16[128,1024]{1,0:T(8,128)(2,1)S(1)}, bf16[128,1024]{1,0:T(8,128)(2,1)S(1)}, u32[]{:S(2)}, u32[]{:S(2)}) collective-permute-start(bf16[128,1024]{1,0:T(8,128)(2,1)S(1)} %get-tuple-element.56), channel_id=1, source_target_pairs={{0,8},{4,12},{8,0},{12,4},{16,24},{20,28},{24,16},{28,20},{1,9},{5... | collective-permute-start | bytes 786440 | tf_op jit(solution)/shard_map/ppermute | solution.py:399
  73.1 14.6 %collective-permute-start.4 = (bf16[128,1024]{1,0:T(8,128)(2,1)}, bf16[128,1024]{1,0:T(8,128)(2,1)S(1)}, u32[]{:S(2)}, u32[]{:S(2)}) collective-permute-start(bf16[128,1024]{1,0:T(8,128)(2,1)} %get-tuple-element.55), channel_id=1, source_target_pairs={{0,12},{4,8},{8,4},{12,0},{16,28},{20,24},{24,20},{28,16},{1,13},{... | collective-permute-start | bytes 786440 | tf_op jit(solution)/shard_map/ppermute | solution.py:399
  74.3 13.4 %collective-permute-start.5 = (bf16[128,1024]{1,0:T(8,128)(2,1)}, bf16[128,1024]{1,0:T(8,128)(2,1)S(1)}, u32[]{:S(2)}, u32[]{:S(2)}) collective-permute-start(bf16[128,1024]{1,0:T(8,128)(2,1)} %get-tuple-element.54), channel_id=1, source_target_pairs={{0,16},{4,20},{8,24},{12,28},{16,0},{20,4},{24,8},{28,12},{1,17},{... | collective-permute-start | bytes 786440 | tf_op jit(solution)/shard_map/ppermute | solution.py:399
  76.2 26.7 %collective-permute-start.6 = (bf16[128,1024]{1,0:T(8,128)(2,1)}, bf16[128,1024]{1,0:T(8,128)(2,1)S(1)}, u32[]{:S(2)}, u32[]{:S(2)}) collective-permute-start(bf16[128,1024]{1,0:T(8,128)(2,1)} %get-tuple-element.53), channel_id=1, source_target_pairs={{0,20},{4,16},{8,28},{12,24},{16,4},{20,0},{24,12},{28,8},{1,21},{... | collective-permute-start | bytes 786440 | tf_op jit(solution)/shard_map/ppermute | solution.py:399
  82.5 32.1 %collective-permute-start.7 = (bf16[128,1024]{1,0:T(8,128)(2,1)}, bf16[128,1024]{1,0:T(8,128)(2,1)S(1)}, u32[]{:S(2)}, u32[]{:S(2)}) collective-permute-start(bf16[128,1024]{1,0:T(8,128)(2,1)} %get-tuple-element.52), channel_id=1, source_target_pairs={{0,24},{4,28},{8,16},{12,20},{16,8},{20,12},{24,0},{28,4},{1,25},{... | collective-permute-start | bytes 786440 | tf_op jit(solution)/shard_map/ppermute | solution.py:399
  83.7 38.4 %collective-permute-start.8 = (bf16[128,1024]{1,0:T(8,128)(2,1)}, bf16[128,1024]{1,0:T(8,128)(2,1)}, u32[]{:S(2)}, u32[]{:S(2)}) collective-permute-start(bf16[128,1024]{1,0:T(8,128)(2,1)} %get-tuple-element.51), channel_id=1, source_target_pairs={{0,28},{4,24},{8,20},{12,16},{16,12},{20,8},{24,4},{28,0},{1,29},{... | collective-permute-start | bytes 786440 | tf_op jit(solution)/shard_map/ppermute | solution.py:399
  102.9 0.7 copy-start.4
  114.6 0.7 copy-start.6
  122.1 1.4 copy-start.1
  122.1 6.3 %copy-start.9 = (f32[1,1,1024]{2,1,0:T(1,128)S(1)}, f32[1,1,1024]{2,1,0:T(1,128)}, u32[]{:S(2)}) copy-start(f32[1,1,1024]{2,1,0:T(1,128)} %param.11) | copy-start | bytes 12292
  123.5 36.1 %all-to-all-start.1 = ((bf16[8,128,1024]{2,1,0:T(8,128)(2,1)}), bf16[8,128,1024]{2,1,0:T(8,128)(2,1)}, u32[]{:S(2)}, u32[]{:S(2)}) async-start(bf16[8,128,1024]{2,1,0:T(8,128)(2,1)} %state_b.1), calls=%async_computation.1 | async-start | bytes 4194304 | tf_op jit(solution)/shard_map/all_to_all | solution.py:396
  128.4 1.0 copy-start.5
  129.4 0.9 copy-start.7
  130.3 18.1 %copy-start.2 = (bf16[8,128,1024]{2,1,0:T(8,128)(2,1)S(1)}, bf16[8,128,1024]{2,1,0:T(8,128)(2,1)}, u32[]{:S(2)}) copy-start(bf16[8,128,1024]{2,1,0:T(8,128)(2,1)} %copy-done.1) | copy-start | bytes 6291460
  157.8 18.1 %collective-permute-start.10 = (bf16[128,1024]{1,0:T(8,128)(2,1)S(1)}, bf16[128,1024]{1,0:T(8,128)(2,1)S(1)}, u32[]{:S(2)}, u32[]{:S(2)}) collective-permute-start(bf16[128,1024]{1,0:T(8,128)(2,1)S(1)} %get-tuple-element.49), channel_id=1, source_target_pairs={{0,20},{4,16},{8,28},{12,24},{16,4},{20,0},{24,12},{28,8},{1,21},{... | collective-permute-start | bytes 786440 | tf_op jit(solution)/shard_map/ppermute | solution.py:399
  159.3 27.7 %collective-permute-start.9 = (bf16[128,1024]{1,0:T(8,128)(2,1)S(1)}, bf16[128,1024]{1,0:T(8,128)(2,1)S(1)}, u32[]{:S(2)}, u32[]{:S(2)}) collective-permute-start(bf16[128,1024]{1,0:T(8,128)(2,1)S(1)} %get-tuple-element.50), channel_id=1, source_target_pairs={{0,16},{4,20},{8,24},{12,28},{16,0},{20,4},{24,8},{28,12},{1,17},{... | collective-permute-start | bytes 786440 | tf_op jit(solution)/shard_map/ppermute | solution.py:399
  168.0 1.3 copy-start.3
  187.1 45.1 %all-to-all-start.2 = ((bf16[8,128,1024]{2,1,0:T(8,128)(2,1)}), bf16[8,128,1024]{2,1,0:T(8,128)(2,1)S(1)}, u32[]{:S(2)}, u32[]{:S(2)}) async-start(bf16[8,128,1024]{2,1,0:T(8,128)(2,1)} %copy-done.3), calls=%async_computation.2 | async-start | bytes 4194304 | tf_op jit(solution)/shard_map/all_to_all | solution.py:396
  193.1 40.6 %collective-permute-start.11 = (bf16[128,1024]{1,0:T(8,128)(2,1)}, bf16[128,1024]{1,0:T(8,128)(2,1)S(1)}, u32[]{:S(2)}, u32[]{:S(2)}) collective-permute-start(bf16[128,1024]{1,0:T(8,128)(2,1)} %get-tuple-element.47), channel_id=1, source_target_pairs={{0,4},{4,0},{8,12},{12,8},{16,20},{20,16},{24,28},{28,24},{1,5},{5... | collective-permute-start | bytes 786440 | tf_op jit(solution)/shard_map/ppermute | solution.py:399
  194.3 39.4 %collective-permute-start.12 = (bf16[128,1024]{1,0:T(8,128)(2,1)}, bf16[128,1024]{1,0:T(8,128)(2,1)S(1)}, u32[]{:S(2)}, u32[]{:S(2)}) collective-permute-start(bf16[128,1024]{1,0:T(8,128)(2,1)} %get-tuple-element.46), channel_id=1, source_target_pairs={{0,8},{4,12},{8,0},{12,4},{16,24},{20,28},{24,16},{28,20},{1,9},{5... | collective-permute-start | bytes 786440 | tf_op jit(solution)/shard_map/ppermute | solution.py:399
  194.5 39.2 %collective-permute-start.13 = (bf16[128,1024]{1,0:T(8,128)(2,1)}, bf16[128,1024]{1,0:T(8,128)(2,1)}, u32[]{:S(2)}, u32[]{:S(2)}) collective-permute-start(bf16[128,1024]{1,0:T(8,128)(2,1)} %get-tuple-element.45), channel_id=1, source_target_pairs={{0,12},{4,8},{8,4},{12,0},{16,28},{20,24},{24,20},{28,16},{1,13},{... | collective-permute-start | bytes 786440 | tf_op jit(solution)/shard_map/ppermute | solution.py:399
  195.7 39.9 %collective-permute-start.14 = (bf16[128,1024]{1,0:T(8,128)(2,1)}, bf16[128,1024]{1,0:T(8,128)(2,1)}, u32[]{:S(2)}, u32[]{:S(2)}) collective-permute-start(bf16[128,1024]{1,0:T(8,128)(2,1)} %get-tuple-element.44), channel_id=1, source_target_pairs={{0,24},{4,28},{8,16},{12,20},{16,8},{20,12},{24,0},{28,4},{1,25},{... | collective-permute-start | bytes 786440 | tf_op jit(solution)/shard_map/ppermute | solution.py:399
  196.9 42.2 %collective-permute-start.15 = (bf16[128,1024]{1,0:T(8,128)(2,1)}, bf16[128,1024]{1,0:T(8,128)(2,1)}, u32[]{:S(2)}, u32[]{:S(2)}) collective-permute-start(bf16[128,1024]{1,0:T(8,128)(2,1)} %get-tuple-element.43), channel_id=1, source_target_pairs={{0,28},{4,24},{8,20},{12,16},{16,12},{20,8},{24,4},{28,0},{1,29},{... | collective-permute-start | bytes 786440 | tf_op jit(solution)/shard_map/ppermute | solution.py:399

commit v9 on v8

--- a/solution.py
+++ b/solution.py
@@ -30,22 +30,34 @@
         use(rows)
 
 
-def to_blocks_kernel(start, state_ref, out_ref, stage, arrived):
+def to_blocks_kernel(start, state_ref, out_ref, stage, turned, arrived, sent):
+    stores = []
+
     def use(rows):
-        out_ref[:, rows, :] = jnp.swapaxes(stage[rows], 0, 1)
+        turned[:, rows, :] = jnp.swapaxes(stage[rows], 0, 1)
+        store = pltpu.make_async_copy(
+            turned.at[:, rows, :], out_ref.at[:, rows, :], sent.at[len(stores)]
+        )
+        store.start()
+        stores.append(store)
 
     fetch_tiles(state_ref, start, stage, arrived, use)
+    for store in stores:
+        store.wait()
 
 
 def to_blocks(state, start, width, name):
     members, blocks, _ = state.shape
+    hbm = pl.BlockSpec(memory_space=pltpu.HBM)
     return pl.pallas_call(
         functools.partial(to_blocks_kernel, start),
-        in_specs=[pl.BlockSpec(memory_space=pltpu.HBM)],
-        out_specs=pl.BlockSpec(memory_space=pltpu.VMEM),
+        in_specs=[hbm],
+        out_specs=hbm,
         out_shape=jax.ShapeDtypeStruct((blocks, members, width), state.dtype),
         scratch_shapes=[
             pltpu.VMEM((members, blocks, width), state.dtype),
+            pltpu.VMEM((blocks, members, width), state.dtype),
+            pltpu.SemaphoreType.DMA((members // MEMBER_TILE,)),
             pltpu.SemaphoreType.DMA((members // MEMBER_TILE,)),
         ],
         compiler_params=pltpu.CompilerParams(vmem_limit_bytes=60 * MIB),

time: 243 us -> 242 us (level)
  transfers between devices with their start and end apart: 19 -> 19, of which waited for: 11 -> 11; matrix products, arithmetic and copies ran while one was open for 1% -> 1% of each run, Pallas kernels for 27% -> 26%
where the time goes in v9:
time: 242 us; the launch traced here: 241 us
  waiting for transfers between devices  125 us (52%)
  Pallas kernels  69.1 us (29%)
  starting transfers between devices  36.9 us (15%)
  local copies, waits for them, and re-layouts  9.89 us (4%)
    ppermute x14, waiting for transfers between devices, swap(): return lax.ppermute(x, 'mem', [(i, i ^ number) for i in range(devices)])  61.7 us
    all_to_all x3, waiting for transfers between devices, exchange(): return lax.all_to_all(x, 'mem', split_axis=0, concat_axis=0, tiled=True)  34.1 us
    ppermute x1, waiting for transfers between devices, body(): up = lax.ppermute(pool, 'reg', to_next)  24.1 us
    pallas_call x1, Pallas kernels, gather_chosen(): pl.pallas_call(gather_kernel, grid=(blocks,), in_specs=[pl.BlockSpec(memo...  21.2 us
    pallas_call x1, Pallas kernels, ensemble_transform(): pl.pallas_call(transform_kernel, in_specs=[pl.BlockSpec(memory_space=pltp...  18.1 us
    pallas_call x2, Pallas kernels, analysed(): pl.pallas_call(functools.partial(analysis_kernel, in_pairs), grid=(width...  16.7 us
    all_to_all x3, starting transfers between devices, exchange(): return lax.all_to_all(x, 'mem', split_axis=0, concat_axis=0, tiled=True)  16 us
    ppermute x14, starting transfers between devices, swap(): return lax.ppermute(x, 'mem', [(i, i ^ number) for i in range(devices)])  14.8 us
  transfers between devices with their start and end apart: 19, of which 11 were waited for; matrix products, arithmetic and copies ran while one was open for 1% of the time, Pallas kernels for 26%

profile of v9, /device:TPU:9, one launch (start us, length us, event | category | flops | bytes accessed | tf_op | source)
XLA Modules:
  0.0 241.3 jit_solution(8159573870562756292)
XLA Ops:
  0.0 2.6 %state_a.1 = bf16[8,128,1024]{2,1,0:T(8,128)(2,1)} custom-call(bf16[128,8,2048]{2,1,0:T(8,128)(2,1)} %bitcast.46), custom_call_target="tpu_custom_call" | custom-call | bytes 4194304 | tf_op jit(solution)/shard_map/state_a/pallas_call | solution.py:52
  2.6 5.7 %all-to-all-start = ((bf16[8,128,1024]{2,1,0:T(8,128)(2,1)}), bf16[8,128,1024]{2,1,0:T(8,128)(2,1)S(1)}, u32[]{:S(2)}, u32[]{:S(2)}) async-start(bf16[8,128,1024]{2,1,0:T(8,128)(2,1)} %state_a.1), calls=%async_computation | async-start | bytes 4194304 | tf_op jit(solution)/shard_map/all_to_all | solution.py:408
  8.3 0.0 copy-start.8
  8.3 3.8 %pool_rows.1.own_ref = bf16[8,144,1024]{2,1,0:T(8,128)(2,1)} custom-call(bf16[128,8,1024]{2,1,0:T(8,128)(2,1)} %bitcast.48, bf16[8,1024]{1,0:T(8,128)(2,1)} %bitcast.49), custom_call_target="tpu_custom_call" | custom-call | bytes 4718592 | tf_op jit(solution)/shard_map/pool_rows/pallas_call | solution.py:86
  12.1 4.2 %collective-permute-start = (bf16[8,144,1024]{2,1,0:T(8,128)(2,1)}, bf16[8,144,1024]{2,1,0:T(8,128)(2,1)}, u32[]{:S(2)}, u32[]{:S(2)}) collective-permute-start(bf16[8,144,1024]{2,1,0:T(8,128)(2,1)} %pool_rows.1.own_ref), channel_id=1, source_target_pairs={{0,1},{1,2},{2,3},{4,5},{5,6},{6,7},{8,9},{9,10},{10,11},{12,13},{... | collective-permute-start | bytes 7077896 | tf_op jit(solution)/shard_map/ppermute | solution.py:420
  16.4 1.9 collective-permute-start.1
  18.3 24.1 %collective-permute-done.up_ref = bf16[8,144,1024]{2,1,0:T(8,128)(2,1)} collective-permute-done((bf16[8,144,1024]{2,1,0:T(8,128)(2,1)}, bf16[8,144,1024]{2,1,0:T(8,128)(2,1)}, u32[]{:S(2)}, u32[]{:S(2)}) %collective-permute-start) | collective-permute-done | bytes 2359328 | tf_op jit(solution)/shard_map/ppermute | solution.py:420
  42.5 4.6 %collective-permute-done.1.down_ref = bf16[8,144,1024]{2,1,0:T(8,128)(2,1)} collective-permute-done((bf16[8,144,1024]{2,1,0:T(8,128)(2,1)}, bf16[8,144,1024]{2,1,0:T(8,128)(2,1)}, u32[]{:S(2)}, u32[]{:S(2)}) %collective-permute-start.1) | collective-permute-done | bytes 2359328 | tf_op jit(solution)/shard_map/ppermute | solution.py:421
  47.1 0.0 copy-done.8
  47.1 0.0 copy-start
  47.1 1.7 copy-done
  48.7 21.2 %gather_chosen.1 = (bf16[8,128,1024]{2,1,0:T(8,128)(2,1)S(1)}, bf16[16,1024]{1,0:T(8,128)(2,1)S(1)}) custom-call(s32[1]{0:T(128)} %bitcast.place_ref, bf16[8,144,1024]{2,1,0:T(8,128)(2,1)S(1)} %copy-done, bf16[8,144,1024]{2,1,0:T(8,128)(2,1)} %collective-permute-done.up_ref, bf16[8,144,1024]{2,1,0:T(8,128)(2,1)} %collective-permute-done.1.down_ref, ...), custom_call_target="tpu_custom_call" | custom-call | bytes 147456 | tf_op jit(solution)/shard_map/gather_chosen/pallas_call | solution.py:144
  70.0 1.2 slice_bitcast_fusion.8
  71.2 1.0 collective-permute-start.2
  72.2 0.5 collective-permute-start.3
  72.6 1.2 collective-permute-start.4
  73.8 1.9 collective-permute-start.5
  75.7 1.2 collective-permute-start.6
  76.9 5.1 %collective-permute-done.2.refs_1_ = bf16[128,1024]{1,0:T(8,128)(2,1)S(1)} collective-permute-done((bf16[128,1024]{1,0:T(8,128)(2,1)S(1)}, bf16[128,1024]{1,0:T(8,128)(2,1)S(1)}, u32[]{:S(2)}, u32[]{:S(2)}) %collective-permute-start.2) | collective-permute-done | bytes 262176 | tf_op jit(solution)/shard_map/ppermute | solution.py:411
  82.0 1.2 collective-permute-start.7
  83.2 0.0 collective-permute-done.3.refs_2_
  83.2 1.0 collective-permute-start.8
  84.2 2.6 %state_b.1 = bf16[8,128,1024]{2,1,0:T(8,128)(2,1)} custom-call(bf16[128,8,2048]{2,1,0:T(8,128)(2,1)} %bitcast.47), custom_call_target="tpu_custom_call" | custom-call | bytes 4194304 | tf_op jit(solution)/shard_map/state_b/pallas_call | solution.py:52
  86.8 0.0 collective-permute-done.4.refs_3_
  86.8 0.0 collective-permute-done.5.refs_4_
  86.8 15.6 %collective-permute-done.6.refs_5_ = bf16[128,1024]{1,0:T(8,128)(2,1)S(1)} collective-permute-done((bf16[128,1024]{1,0:T(8,128)(2,1)}, bf16[128,1024]{1,0:T(8,128)(2,1)S(1)}, u32[]{:S(2)}, u32[]{:S(2)}) %collective-permute-start.6) | collective-permute-done | bytes 262176 | tf_op jit(solution)/shard_map/ppermute | solution.py:411
  102.4 0.0 copy-start.4
  102.4 0.7 copy-done.4
  103.1 11.0 %collective-permute-done.7.refs_6_ = bf16[128,1024]{1,0:T(8,128)(2,1)S(1)} collective-permute-done((bf16[128,1024]{1,0:T(8,128)(2,1)}, bf16[128,1024]{1,0:T(8,128)(2,1)S(1)}, u32[]{:S(2)}, u32[]{:S(2)}) %collective-permute-start.7) | collective-permute-done | bytes 262176 | tf_op jit(solution)/shard_map/ppermute | solution.py:411
  114.1 0.7 copy-done.6
  114.8 6.8 %collective-permute-done.8.refs_7_ = bf16[128,1024]{1,0:T(8,128)(2,1)} collective-permute-done((bf16[128,1024]{1,0:T(8,128)(2,1)}, bf16[128,1024]{1,0:T(8,128)(2,1)}, u32[]{:S(2)}, u32[]{:S(2)}) %collective-permute-start.8) | collective-permute-done | bytes 262176 | tf_op jit(solution)/shard_map/ppermute | solution.py:411
  121.6 0.0 all-to-all-done
  121.6 1.3 copy-done.1
  123.0 4.3 %all-to-all-start.1 = ((bf16[8,128,1024]{2,1,0:T(8,128)(2,1)}), bf16[8,128,1024]{2,1,0:T(8,128)(2,1)}, u32[]{:S(2)}, u32[]{:S(2)}) async-start(bf16[8,128,1024]{2,1,0:T(8,128)(2,1)} %state_b.1), calls=%async_computation.1 | async-start | bytes 4194304 | tf_op jit(solution)/shard_map/all_to_all | solution.py:408
  128.0 0.0 copy-done.9
  128.0 0.0 copy-start.5
  128.0 0.9 copy-done.5
  128.9 0.9 copy-done.7
  129.9 18.1 %transform.1.transform_ref = bf16[1024,1024]{1,0:T(8,128)(2,1)S(1)} custom-call(s32[1]{0:T(128)} %bitcast.place_ref, s32[1,1]{1,0:T(1,128)S(6)} %copy.10.tally_ref, f32[1,1024]{1,0:T(1,128)S(1)} %bitcast.45, bf16[16,1024]{1,0:T(8,128)(2,1)S(1)} %get-tuple-element.25.innov_ref, bf16[128,1024]{1,0:T(8,128)(2,1)S(1)} %get-tuple-element.28.refs_0_, ...), custom_call_target="tpu_custom_call" | custom-call | bytes 1048576 | tf_op jit(solution)/shard_map/transform/pallas_call | solution.py:329
  148.0 0.0 copy-done.2
  148.0 8.2 %analysed_a.1 = bf16[8,128,1024]{2,1,0:T(8,128)(2,1)S(1)} custom-call(s32[1]{0:T(128)} %bitcast.place_ref, bf16[1024,1024]{1,0:T(8,128)(2,1)S(1)} %transform.1.transform_ref, bf16[1024,1024]{1,0:T(8,128)(2,1)S(1)} %bitcast.43), custom_call_target="tpu_custom_call" | custom-call | bytes 1048576 | tf_op jit(solution)/shard_map/analysed_a/pallas_call | solution.py:371
  156.2 1.1 slice_bitcast_fusion
  157.3 1.6 collective-permute-start.10
  158.9 0.3 collective-permute-start.9
  159.2 0.0 all-to-all-done.1
  159.2 8.4 %analysed_b.1 = bf16[8,128,1024]{2,1,0:T(8,128)(2,1)S(1)} custom-call(s32[1]{0:T(128)} %bitcast.place_ref, bf16[1024,1024]{1,0:T(8,128)(2,1)S(1)} %transform.1.transform_ref, bf16[1024,1024]{1,0:T(8,128)(2,1)} %bitcast.15.state_ref), custom_call_target="tpu_custom_call" | custom-call | bytes 1048576 | tf_op jit(solution)/shard_map/analysed_b/pallas_call | solution.py:371
  167.6 0.0 copy-start.3
  167.6 1.3 copy-done.3
  168.9 6.5 %collective-permute-done.10.refs_5_ = bf16[128,1024]{1,0:T(8,128)(2,1)S(1)} collective-permute-done((bf16[128,1024]{1,0:T(8,128)(2,1)S(1)}, bf16[128,1024]{1,0:T(8,128)(2,1)S(1)}, u32[]{:S(2)}, u32[]{:S(2)}) %collective-permute-start.10) | collective-permute-done | bytes 262176 | tf_op jit(solution)/shard_map/ppermute | solution.py:411
  175.4 11.2 %collective-permute-done.9.refs_4_ = bf16[128,1024]{1,0:T(8,128)(2,1)S(1)} collective-permute-done((bf16[128,1024]{1,0:T(8,128)(2,1)S(1)}, bf16[128,1024]{1,0:T(8,128)(2,1)S(1)}, u32[]{:S(2)}, u32[]{:S(2)}) %collective-permute-start.9) | collective-permute-done | bytes 262176 | tf_op jit(solution)/shard_map/ppermute | solution.py:411
  186.6 6.0 %all-to-all-start.2 = ((bf16[8,128,1024]{2,1,0:T(8,128)(2,1)}), bf16[8,128,1024]{2,1,0:T(8,128)(2,1)S(1)}, u32[]{:S(2)}, u32[]{:S(2)}) async-start(bf16[8,128,1024]{2,1,0:T(8,128)(2,1)} %copy-done.3), calls=%async_computation.2 | async-start | bytes 4194304 | tf_op jit(solution)/shard_map/all_to_all | solution.py:408
  192.6 1.2 collective-permute-start.11
  193.8 0.3 collective-permute-start.12
  194.1 1.2 collective-permute-start.13
  195.2 1.2 collective-permute-start.14
  196.4 1.2 collective-permute-start.15
  197.6 34.1 %all-to-all-done.2.part_ref = bf16[8,128,1024]{2,1,0:T(8,128)(2,1)S(1)} async-done(((bf16[8,128,1024]{2,1,0:T(8,128)(2,1)}), bf16[8,128,1024]{2,1,0:T(8,128)(2,1)S(1)}, u32[]{:S(2)}, u32[]{:S(2)}) %all-to-all-start.2) | async-done | bytes 2097184 | tf_op jit(solution)/shard_map/all_to_all | solution.py:408
  231.7 1.5 analysis_b.1.whole_ref
  233.2 0.0 collective-permute-done.11.refs_1_
  233.2 0.0 collective-permute-done.12.refs_2_
  233.2 0.0 collective-permute-done.13.refs_3_
  233.3 1.9 collective-permute-done.14.refs_6_
  235.2 3.5 %collective-permute-done.15.refs_7_ = bf16[128,1024]{1,0:T(8,128)(2,1)} collective-permute-done((bf16[128,1024]{1,0:T(8,128)(2,1)}, bf16[128,1024]{1,0:T(8,128)(2,1)}, u32[]{:S(2)}, u32[]{:S(2)}) %collective-permute-start.15) | collective-permute-done | bytes 262176 | tf_op jit(solution)/shard_map/ppermute | solution.py:411
  238.6 2.7 %analysis_a.1 = bf16[128,8,2048]{2,1,0:T(8,128)(2,1)} custom-call(s32[1]{0:T(128)} %bitcast.place_ref, bf16[128,8,2048]{2,1,0:T(8,128)(2,1)} %analysis_b.1.whole_ref, bf16[128,1024]{1,0:T(8,128)(2,1)S(1)} %get-tuple-element.48.refs_0_, bf16[128,1024]{1,0:T(8,128)(2,1)S(1)} %collective-permute-done.11.refs_1_, ...), custom_call_target="tpu_custom_call", output_to_operand_aliasing={{}: (1, {})} | custom-call | bytes 4194304 | tf_op jit(solution)/shard_map/analysis_a/pallas_call | solution.py:217
  (5 shorter events, 0.0 us)
Async XLA Ops:
  2.6 119.1 %all-to-all-start = ((bf16[8,128,1024]{2,1,0:T(8,128)(2,1)}), bf16[8,128,1024]{2,1,0:T(8,128)(2,1)S(1)}, u32[]{:S(2)}, u32[]{:S(2)}) async-start(bf16[8,128,1024]{2,1,0:T(8,128)(2,1)} %state_a.1), calls=%async_computation | async-start | bytes 4194304 | tf_op jit(solution)/shard_map/all_to_all | solution.py:408
  8.3 38.7 %copy-start.8 = (s32[1,8,1024]{2,1,0:T(8,128)S(1)}, s32[1,8,1024]{2,1,0:T(8,128)}, u32[]{:S(2)}) copy-start(s32[1,8,1024]{2,1,0:T(8,128)} %param.9) | copy-start | bytes 98308
  12.1 30.3 %collective-permute-start = (bf16[8,144,1024]{2,1,0:T(8,128)(2,1)}, bf16[8,144,1024]{2,1,0:T(8,128)(2,1)}, u32[]{:S(2)}, u32[]{:S(2)}) collective-permute-start(bf16[8,144,1024]{2,1,0:T(8,128)(2,1)} %pool_rows.1.own_ref), channel_id=1, source_target_pairs={{0,1},{1,2},{2,3},{4,5},{5,6},{6,7},{8,9},{9,10},{10,11},{12,13},{... | collective-permute-start | bytes 7077896 | tf_op jit(solution)/shard_map/ppermute | solution.py:420
  16.4 30.7 %collective-permute-start.1 = (bf16[8,144,1024]{2,1,0:T(8,128)(2,1)}, bf16[8,144,1024]{2,1,0:T(8,128)(2,1)}, u32[]{:S(2)}, u32[]{:S(2)}) collective-permute-start(bf16[8,144,1024]{2,1,0:T(8,128)(2,1)} %pool_rows.1.own_ref), channel_id=1, source_target_pairs={{1,0},{2,1},{3,2},{5,4},{6,5},{7,6},{9,8},{10,9},{11,10},{13,12},{... | collective-permute-start | bytes 7077896 | tf_op jit(solution)/shard_map/ppermute | solution.py:421
  47.1 1.7 copy-start
  71.2 10.8 %collective-permute-start.2 = (bf16[128,1024]{1,0:T(8,128)(2,1)S(1)}, bf16[128,1024]{1,0:T(8,128)(2,1)S(1)}, u32[]{:S(2)}, u32[]{:S(2)}) collective-permute-start(bf16[128,1024]{1,0:T(8,128)(2,1)S(1)} %get-tuple-element.57), channel_id=1, source_target_pairs={{0,4},{4,0},{8,12},{12,8},{16,20},{20,16},{24,28},{28,24},{1,5},{5... | collective-permute-start | bytes 786440 | tf_op jit(solution)/shard_map/ppermute | solution.py:411
  72.2 11.0 %collective-permute-start.3 = (bf16[128,1024]{1,0:T(8,128)(2,1)S(1)}, bf16[128,1024]{1,0:T(8,128)(2,1)S(1)}, u32[]{:S(2)}, u32[]{:S(2)}) collective-permute-start(bf16[128,1024]{1,0:T(8,128)(2,1)S(1)} %get-tuple-element.56), channel_id=1, source_target_pairs={{0,8},{4,12},{8,0},{12,4},{16,24},{20,28},{24,16},{28,20},{1,9},{5... | collective-permute-start | bytes 786440 | tf_op jit(solution)/shard_map/ppermute | solution.py:411
  72.6 14.1 %collective-permute-start.4 = (bf16[128,1024]{1,0:T(8,128)(2,1)}, bf16[128,1024]{1,0:T(8,128)(2,1)S(1)}, u32[]{:S(2)}, u32[]{:S(2)}) collective-permute-start(bf16[128,1024]{1,0:T(8,128)(2,1)} %get-tuple-element.55), channel_id=1, source_target_pairs={{0,12},{4,8},{8,4},{12,0},{16,28},{20,24},{24,20},{28,16},{1,13},{... | collective-permute-start | bytes 786440 | tf_op jit(solution)/shard_map/ppermute | solution.py:411
  73.8 12.9 %collective-permute-start.5 = (bf16[128,1024]{1,0:T(8,128)(2,1)}, bf16[128,1024]{1,0:T(8,128)(2,1)S(1)}, u32[]{:S(2)}, u32[]{:S(2)}) collective-permute-start(bf16[128,1024]{1,0:T(8,128)(2,1)} %get-tuple-element.54), channel_id=1, source_target_pairs={{0,16},{4,20},{8,24},{12,28},{16,0},{20,4},{24,8},{28,12},{1,17},{... | collective-permute-start | bytes 786440 | tf_op jit(solution)/shard_map/ppermute | solution.py:411
  75.7 26.7 %collective-permute-start.6 = (bf16[128,1024]{1,0:T(8,128)(2,1)}, bf16[128,1024]{1,0:T(8,128)(2,1)S(1)}, u32[]{:S(2)}, u32[]{:S(2)}) collective-permute-start(bf16[128,1024]{1,0:T(8,128)(2,1)} %get-tuple-element.53), channel_id=1, source_target_pairs={{0,20},{4,16},{8,28},{12,24},{16,4},{20,0},{24,12},{28,8},{1,21},{... | collective-permute-start | bytes 786440 | tf_op jit(solution)/shard_map/ppermute | solution.py:411
  82.0 32.1 %collective-permute-start.7 = (bf16[128,1024]{1,0:T(8,128)(2,1)}, bf16[128,1024]{1,0:T(8,128)(2,1)S(1)}, u32[]{:S(2)}, u32[]{:S(2)}) collective-permute-start(bf16[128,1024]{1,0:T(8,128)(2,1)} %get-tuple-element.52), channel_id=1, source_target_pairs={{0,24},{4,28},{8,16},{12,20},{16,8},{20,12},{24,0},{28,4},{1,25},{... | collective-permute-start | bytes 786440 | tf_op jit(solution)/shard_map/ppermute | solution.py:411
  83.2 38.4 %collective-permute-start.8 = (bf16[128,1024]{1,0:T(8,128)(2,1)}, bf16[128,1024]{1,0:T(8,128)(2,1)}, u32[]{:S(2)}, u32[]{:S(2)}) collective-permute-start(bf16[128,1024]{1,0:T(8,128)(2,1)} %get-tuple-element.51), channel_id=1, source_target_pairs={{0,28},{4,24},{8,20},{12,16},{16,12},{20,8},{24,4},{28,0},{1,29},{... | collective-permute-start | bytes 786440 | tf_op jit(solution)/shard_map/ppermute | solution.py:411
  102.4 0.7 copy-start.4
  114.1 0.7 copy-start.6
  121.6 1.4 copy-start.1
  121.6 6.3 %copy-start.9 = (f32[1,1,1024]{2,1,0:T(1,128)S(1)}, f32[1,1,1024]{2,1,0:T(1,128)}, u32[]{:S(2)}) copy-start(f32[1,1,1024]{2,1,0:T(1,128)} %param.11) | copy-start | bytes 12292
  123.0 36.2 %all-to-all-start.1 = ((bf16[8,128,1024]{2,1,0:T(8,128)(2,1)}), bf16[8,128,1024]{2,1,0:T(8,128)(2,1)}, u32[]{:S(2)}, u32[]{:S(2)}) async-start(bf16[8,128,1024]{2,1,0:T(8,128)(2,1)} %state_b.1), calls=%async_computation.1 | async-start | bytes 4194304 | tf_op jit(solution)/shard_map/all_to_all | solution.py:408
  128.0 1.0 copy-start.5
  128.9 0.9 copy-start.7
  129.9 18.1 %copy-start.2 = (bf16[8,128,1024]{2,1,0:T(8,128)(2,1)S(1)}, bf16[8,128,1024]{2,1,0:T(8,128)(2,1)}, u32[]{:S(2)}) copy-start(bf16[8,128,1024]{2,1,0:T(8,128)(2,1)} %copy-done.1) | copy-start | bytes 6291460
  157.3 18.1 %collective-permute-start.10 = (bf16[128,1024]{1,0:T(8,128)(2,1)S(1)}, bf16[128,1024]{1,0:T(8,128)(2,1)S(1)}, u32[]{:S(2)}, u32[]{:S(2)}) collective-permute-start(bf16[128,1024]{1,0:T(8,128)(2,1)S(1)} %get-tuple-element.49), channel_id=1, source_target_pairs={{0,20},{4,16},{8,28},{12,24},{16,4},{20,0},{24,12},{28,8},{1,21},{... | collective-permute-start | bytes 786440 | tf_op jit(solution)/shard_map/ppermute | solution.py:411
  158.9 27.7 %collective-permute-start.9 = (bf16[128,1024]{1,0:T(8,128)(2,1)S(1)}, bf16[128,1024]{1,0:T(8,128)(2,1)S(1)}, u32[]{:S(2)}, u32[]{:S(2)}) collective-permute-start(bf16[128,1024]{1,0:T(8,128)(2,1)S(1)} %get-tuple-element.50), channel_id=1, source_target_pairs={{0,16},{4,20},{8,24},{12,28},{16,0},{20,4},{24,8},{28,12},{1,17},{... | collective-permute-start | bytes 786440 | tf_op jit(solution)/shard_map/ppermute | solution.py:411
  167.6 1.3 copy-start.3
  186.6 45.1 %all-to-all-start.2 = ((bf16[8,128,1024]{2,1,0:T(8,128)(2,1)}), bf16[8,128,1024]{2,1,0:T(8,128)(2,1)S(1)}, u32[]{:S(2)}, u32[]{:S(2)}) async-start(bf16[8,128,1024]{2,1,0:T(8,128)(2,1)} %copy-done.3), calls=%async_computation.2 | async-start | bytes 4194304 | tf_op jit(solution)/shard_map/all_to_all | solution.py:408
  192.6 40.6 %collective-permute-start.11 = (bf16[128,1024]{1,0:T(8,128)(2,1)}, bf16[128,1024]{1,0:T(8,128)(2,1)S(1)}, u32[]{:S(2)}, u32[]{:S(2)}) collective-permute-start(bf16[128,1024]{1,0:T(8,128)(2,1)} %get-tuple-element.47), channel_id=1, source_target_pairs={{0,4},{4,0},{8,12},{12,8},{16,20},{20,16},{24,28},{28,24},{1,5},{5... | collective-permute-start | bytes 786440 | tf_op jit(solution)/shard_map/ppermute | solution.py:411
  193.8 39.5 %collective-permute-start.12 = (bf16[128,1024]{1,0:T(8,128)(2,1)}, bf16[128,1024]{1,0:T(8,128)(2,1)S(1)}, u32[]{:S(2)}, u32[]{:S(2)}) collective-permute-start(bf16[128,1024]{1,0:T(8,128)(2,1)} %get-tuple-element.46), channel_id=1, source_target_pairs={{0,8},{4,12},{8,0},{12,4},{16,24},{20,28},{24,16},{28,20},{1,9},{5... | collective-permute-start | bytes 786440 | tf_op jit(solution)/shard_map/ppermute | solution.py:411
  194.1 39.2 %collective-permute-start.13 = (bf16[128,1024]{1,0:T(8,128)(2,1)}, bf16[128,1024]{1,0:T(8,128)(2,1)}, u32[]{:S(2)}, u32[]{:S(2)}) collective-permute-start(bf16[128,1024]{1,0:T(8,128)(2,1)} %get-tuple-element.45), channel_id=1, source_target_pairs={{0,12},{4,8},{8,4},{12,0},{16,28},{20,24},{24,20},{28,16},{1,13},{... | collective-permute-start | bytes 786440 | tf_op jit(solution)/shard_map/ppermute | solution.py:411
  195.2 39.9 %collective-permute-start.14 = (bf16[128,1024]{1,0:T(8,128)(2,1)}, bf16[128,1024]{1,0:T(8,128)(2,1)}, u32[]{:S(2)}, u32[]{:S(2)}) collective-permute-start(bf16[128,1024]{1,0:T(8,128)(2,1)} %get-tuple-element.44), channel_id=1, source_target_pairs={{0,24},{4,28},{8,16},{12,20},{16,8},{20,12},{24,0},{28,4},{1,25},{... | collective-permute-start | bytes 786440 | tf_op jit(solution)/shard_map/ppermute | solution.py:411
  196.4 42.2 %collective-permute-start.15 = (bf16[128,1024]{1,0:T(8,128)(2,1)}, bf16[128,1024]{1,0:T(8,128)(2,1)}, u32[]{:S(2)}, u32[]{:S(2)}) collective-permute-start(bf16[128,1024]{1,0:T(8,128)(2,1)} %get-tuple-element.43), channel_id=1, source_target_pairs={{0,28},{4,24},{8,20},{12,16},{16,12},{20,8},{24,4},{28,0},{1,29},{... | collective-permute-start | bytes 786440 | tf_op jit(solution)/shard_map/ppermute | solution.py:411

commit v10 on v9

--- a/solution.py
+++ b/solution.py
@@ -9,9 +9,10 @@
 
 INNOV_ROWS = 16
 SLOT_CHUNK = 256
-MEMBER_TILE = 32
+MEMBER_TILE = 16
 TRANSFORM_CHUNK = 256
-ANALYSIS_TILE = 128
+TILE_A = 128
+TILE_B = 512
 MIB = 1024 * 1024
 
 
@@ -365,20 +366,20 @@
         out_ref[...] = result
 
 
-def analysed(place, transform, part, in_pairs, name):
+def analysed(place, transform, part, in_pairs, tile, name):
     blocks, members, width = part.shape
     count_k = blocks * members
     return pl.pallas_call(
         functools.partial(analysis_kernel, in_pairs),
-        grid=(width // ANALYSIS_TILE,),
+        grid=(width // tile,),
         in_specs=[
             pl.BlockSpec(memory_space=pltpu.SMEM),
             pl.BlockSpec(memory_space=pltpu.VMEM),
-            pl.BlockSpec((count_k, ANALYSIS_TILE), lambda i: (0, i)),
-        ],
-        out_specs=pl.BlockSpec((blocks, members, ANALYSIS_TILE), lambda i: (0, 0, i)),
+            pl.BlockSpec((count_k, tile), lambda i: (0, i)),
+        ],
+        out_specs=pl.BlockSpec((blocks, members, tile), lambda i: (0, 0, i)),
         out_shape=jax.ShapeDtypeStruct(part.shape, jnp.bfloat16),
-        scratch_shapes=[pltpu.VMEM((blocks, members, ANALYSIS_TILE), jnp.bfloat16)],
+        scratch_shapes=[pltpu.VMEM((blocks, members, tile), jnp.bfloat16)],
         compiler_params=pltpu.CompilerParams(vmem_limit_bytes=32 * MIB),
         cost_estimate=pl.CostEstimate(
             flops=0,
@@ -428,10 +429,10 @@
     transform = ensemble_transform(
         place, active_measure_tally, tapered_error_weight[0], innov, near + far
     )
-    done_a = analysed(place, transform, state_a, True, "analysed_a")
+    done_a = analysed(place, transform, state_a, True, TILE_A, "analysed_a")
     transform, done_a = lax.optimization_barrier((transform, done_a))
     done_a = [done_a[0]] + [swap(done_a[k], k) for k in range(1, devices)]
-    done_b = analysed(place, transform, state_b, False, "analysed_b")
+    done_b = analysed(place, transform, state_b, False, TILE_B, "analysed_b")
     done_b, *done_a[half : half + 2] = lax.optimization_barrier(
         (done_b, *done_a[half : half + 2])
     )

time: 242 us -> 242 us (level)
  Pallas kernels: 69.1 us -> 64.7 us
    pallas_call x2, Pallas kernels: 16.7 us -> 12.6 us  [analysed(): pl.pallas_call(functools.partial(analysis_kernel, in_pairs), grid=(width...]
    ppermute x14, waiting for transfers between devices: 61.7 us -> 64.8 us  [swap(): return lax.ppermute(x, 'mem', [(i, i ^ number) for i in range(devices)])]
  transfers between devices with their start and end apart: 19 -> 19, of which waited for: 11 -> 11; matrix products, arithmetic and copies ran while one was open for 1% -> 1% of each run, Pallas kernels for 26% -> 25%
where the time goes in v10:
time: 242 us; the launch traced here: 241 us
  waiting for transfers between devices  127 us (52%)
  Pallas kernels  64.7 us (27%)
  starting transfers between devices  38.5 us (16%)
  local copies, waits for them, and re-layouts  9.89 us (4%)
    ppermute x14, waiting for transfers between devices, swap(): return lax.ppermute(x, 'mem', [(i, i ^ number) for i in range(devices)])  64.8 us
    all_to_all x3, waiting for transfers between devices, exchange(): return lax.all_to_all(x, 'mem', split_axis=0, concat_axis=0, tiled=True)  33.7 us
    ppermute x1, waiting for transfers between devices, body(): up = lax.ppermute(pool, 'reg', to_next)  24.1 us
    pallas_call x1, Pallas kernels, gather_chosen(): pl.pallas_call(gather_kernel, grid=(blocks,), in_specs=[pl.BlockSpec(memo...  21.2 us
    pallas_call x1, Pallas kernels, ensemble_transform(): pl.pallas_call(transform_kernel, in_specs=[pl.BlockSpec(memory_space=pltp...  18.1 us
    all_to_all x3, starting transfers between devices, exchange(): return lax.all_to_all(x, 'mem', split_axis=0, concat_axis=0, tiled=True)  16.4 us
    ppermute x14, starting transfers between devices, swap(): return lax.ppermute(x, 'mem', [(i, i ^ number) for i in range(devices)])  15.9 us
    pallas_call x2, Pallas kernels, analysed(): pl.pallas_call(functools.partial(analysis_kernel, in_pairs), grid=(width...  12.6 us
  transfers between devices with their start and end apart: 19, of which 11 were waited for; matrix products, arithmetic and copies ran while one was open for 1% of the time, Pallas kernels for 25%

profile of v10, /device:TPU:9, one launch (start us, length us, event | category | flops | bytes accessed | tf_op | source)
XLA Modules:
  0.0 241.1 jit_solution(13828653003227364181)
XLA Ops:
  0.0 2.5 %state_a.1 = bf16[8,128,1024]{2,1,0:T(8,128)(2,1)} custom-call(bf16[128,8,2048]{2,1,0:T(8,128)(2,1)} %bitcast.46), custom_call_target="tpu_custom_call" | custom-call | bytes 4194304 | tf_op jit(solution)/shard_map/state_a/pallas_call | solution.py:53
  2.5 5.7 %all-to-all-start = ((bf16[8,128,1024]{2,1,0:T(8,128)(2,1)}), bf16[8,128,1024]{2,1,0:T(8,128)(2,1)S(1)}, u32[]{:S(2)}, u32[]{:S(2)}) async-start(bf16[8,128,1024]{2,1,0:T(8,128)(2,1)} %state_a.1), calls=%async_computation | async-start | bytes 4194304 | tf_op jit(solution)/shard_map/all_to_all | solution.py:409
  8.2 0.0 copy-start.8
  8.2 3.8 %pool_rows.1.own_ref = bf16[8,144,1024]{2,1,0:T(8,128)(2,1)} custom-call(bf16[128,8,1024]{2,1,0:T(8,128)(2,1)} %bitcast.48, bf16[8,1024]{1,0:T(8,128)(2,1)} %bitcast.49), custom_call_target="tpu_custom_call" | custom-call | bytes 4718592 | tf_op jit(solution)/shard_map/pool_rows/pallas_call | solution.py:87
  12.0 4.2 %collective-permute-start = (bf16[8,144,1024]{2,1,0:T(8,128)(2,1)}, bf16[8,144,1024]{2,1,0:T(8,128)(2,1)}, u32[]{:S(2)}, u32[]{:S(2)}) collective-permute-start(bf16[8,144,1024]{2,1,0:T(8,128)(2,1)} %pool_rows.1.own_ref), channel_id=1, source_target_pairs={{0,1},{1,2},{2,3},{4,5},{5,6},{6,7},{8,9},{9,10},{10,11},{12,13},{... | collective-permute-start | bytes 7077896 | tf_op jit(solution)/shard_map/ppermute | solution.py:421
  16.2 1.9 collective-permute-start.1
  18.2 24.1 %collective-permute-done.up_ref = bf16[8,144,1024]{2,1,0:T(8,128)(2,1)} collective-permute-done((bf16[8,144,1024]{2,1,0:T(8,128)(2,1)}, bf16[8,144,1024]{2,1,0:T(8,128)(2,1)}, u32[]{:S(2)}, u32[]{:S(2)}) %collective-permute-start) | collective-permute-done | bytes 2359328 | tf_op jit(solution)/shard_map/ppermute | solution.py:421
  42.3 4.6 %collective-permute-done.1.down_ref = bf16[8,144,1024]{2,1,0:T(8,128)(2,1)} collective-permute-done((bf16[8,144,1024]{2,1,0:T(8,128)(2,1)}, bf16[8,144,1024]{2,1,0:T(8,128)(2,1)}, u32[]{:S(2)}, u32[]{:S(2)}) %collective-permute-start.1) | collective-permute-done | bytes 2359328 | tf_op jit(solution)/shard_map/ppermute | solution.py:422
  46.9 0.0 copy-done.8
  46.9 0.0 copy-start
  46.9 1.7 copy-done
  48.6 21.2 %gather_chosen.1 = (bf16[8,128,1024]{2,1,0:T(8,128)(2,1)S(1)}, bf16[16,1024]{1,0:T(8,128)(2,1)S(1)}) custom-call(s32[1]{0:T(128)} %bitcast.place_ref, bf16[8,144,1024]{2,1,0:T(8,128)(2,1)S(1)} %copy-done, bf16[8,144,1024]{2,1,0:T(8,128)(2,1)} %collective-permute-done.up_ref, bf16[8,144,1024]{2,1,0:T(8,128)(2,1)} %collective-permute-done.1.down_ref, ...), custom_call_target="tpu_custom_call" | custom-call | bytes 147456 | tf_op jit(solution)/shard_map/gather_chosen/pallas_call | solution.py:145
  69.8 1.2 slice_bitcast_fusion.8
  71.0 1.0 collective-permute-start.2
  72.0 0.3 collective-permute-start.3
  72.3 1.4 collective-permute-start.4
  73.7 1.9 collective-permute-start.5
  75.6 1.2 collective-permute-start.6
  76.7 4.2 %collective-permute-done.2.refs_1_ = bf16[128,1024]{1,0:T(8,128)(2,1)S(1)} collective-permute-done((bf16[128,1024]{1,0:T(8,128)(2,1)S(1)}, bf16[128,1024]{1,0:T(8,128)(2,1)S(1)}, u32[]{:S(2)}, u32[]{:S(2)}) %collective-permute-start.2) | collective-permute-done | bytes 262176 | tf_op jit(solution)/shard_map/ppermute | solution.py:412
  81.0 2.1 collective-permute-start.7
  83.0 0.0 collective-permute-done.3.refs_2_
  83.0 1.0 collective-permute-start.8
  84.0 2.5 %state_b.1 = bf16[8,128,1024]{2,1,0:T(8,128)(2,1)} custom-call(bf16[128,8,2048]{2,1,0:T(8,128)(2,1)} %bitcast.47), custom_call_target="tpu_custom_call" | custom-call | bytes 4194304 | tf_op jit(solution)/shard_map/state_b/pallas_call | solution.py:53
  86.5 0.0 collective-permute-done.4.refs_3_
  86.5 0.0 collective-permute-done.5.refs_4_
  86.5 15.8 %collective-permute-done.6.refs_5_ = bf16[128,1024]{1,0:T(8,128)(2,1)S(1)} collective-permute-done((bf16[128,1024]{1,0:T(8,128)(2,1)}, bf16[128,1024]{1,0:T(8,128)(2,1)S(1)}, u32[]{:S(2)}, u32[]{:S(2)}) %collective-permute-start.6) | collective-permute-done | bytes 262176 | tf_op jit(solution)/shard_map/ppermute | solution.py:412
  102.3 0.0 copy-start.4
  102.3 0.7 copy-done.4
  103.0 11.0 %collective-permute-done.7.refs_6_ = bf16[128,1024]{1,0:T(8,128)(2,1)S(1)} collective-permute-done((bf16[128,1024]{1,0:T(8,128)(2,1)}, bf16[128,1024]{1,0:T(8,128)(2,1)S(1)}, u32[]{:S(2)}, u32[]{:S(2)}) %collective-permute-start.7) | collective-permute-done | bytes 262176 | tf_op jit(solution)/shard_map/ppermute | solution.py:412
  114.0 0.7 copy-done.6
  114.7 6.7 %collective-permute-done.8.refs_7_ = bf16[128,1024]{1,0:T(8,128)(2,1)} collective-permute-done((bf16[128,1024]{1,0:T(8,128)(2,1)}, bf16[128,1024]{1,0:T(8,128)(2,1)}, u32[]{:S(2)}, u32[]{:S(2)}) %collective-permute-start.8) | collective-permute-done | bytes 262176 | tf_op jit(solution)/shard_map/ppermute | solution.py:412
  121.4 0.0 all-to-all-done
  121.4 1.3 copy-done.1
  122.7 4.3 %all-to-all-start.1 = ((bf16[8,128,1024]{2,1,0:T(8,128)(2,1)}), bf16[8,128,1024]{2,1,0:T(8,128)(2,1)}, u32[]{:S(2)}, u32[]{:S(2)}) async-start(bf16[8,128,1024]{2,1,0:T(8,128)(2,1)} %state_b.1), calls=%async_computation.1 | async-start | bytes 4194304 | tf_op jit(solution)/shard_map/all_to_all | solution.py:409
  127.7 0.0 copy-done.9
  127.7 0.0 copy-start.5
  127.7 0.9 copy-done.5
  128.6 0.9 copy-done.7
  129.6 18.1 %transform.1.transform_ref = bf16[1024,1024]{1,0:T(8,128)(2,1)S(1)} custom-call(s32[1]{0:T(128)} %bitcast.place_ref, s32[1,1]{1,0:T(1,128)S(6)} %copy.10.tally_ref, f32[1,1024]{1,0:T(1,128)S(1)} %bitcast.45, bf16[16,1024]{1,0:T(8,128)(2,1)S(1)} %get-tuple-element.25.innov_ref, bf16[128,1024]{1,0:T(8,128)(2,1)S(1)} %get-tuple-element.28.refs_0_, ...), custom_call_target="tpu_custom_call" | custom-call | bytes 1048576 | tf_op jit(solution)/shard_map/transform/pallas_call | solution.py:330
  147.7 0.0 copy-done.2
  147.7 8.2 %analysed_a.1 = bf16[8,128,1024]{2,1,0:T(8,128)(2,1)S(1)} custom-call(s32[1]{0:T(128)} %bitcast.place_ref, bf16[1024,1024]{1,0:T(8,128)(2,1)S(1)} %transform.1.transform_ref, bf16[1024,1024]{1,0:T(8,128)(2,1)S(1)} %bitcast.43), custom_call_target="tpu_custom_call" | custom-call | bytes 1048576 | tf_op jit(solution)/shard_map/analysed_a/pallas_call | solution.py:372
  156.0 1.1 slice_bitcast_fusion
  157.0 1.8 collective-permute-start.10
  158.8 0.3 collective-permute-start.9
  159.1 0.0 all-to-all-done.1
  159.1 4.3 %analysed_b.1 = bf16[8,128,1024]{2,1,0:T(8,128)(2,1)S(1)} custom-call(s32[1]{0:T(128)} %bitcast.place_ref, bf16[1024,1024]{1,0:T(8,128)(2,1)S(1)} %transform.1.transform_ref, bf16[1024,1024]{1,0:T(8,128)(2,1)} %bitcast.15.state_ref), custom_call_target="tpu_custom_call" | custom-call | bytes 1048576 | tf_op jit(solution)/shard_map/analysed_b/pallas_call | solution.py:372
  163.4 0.0 copy-start.3
  163.4 1.3 copy-done.3
  164.7 10.5 %collective-permute-done.10.refs_5_ = bf16[128,1024]{1,0:T(8,128)(2,1)S(1)} collective-permute-done((bf16[128,1024]{1,0:T(8,128)(2,1)S(1)}, bf16[128,1024]{1,0:T(8,128)(2,1)S(1)}, u32[]{:S(2)}, u32[]{:S(2)}) %collective-permute-start.10) | collective-permute-done | bytes 262176 | tf_op jit(solution)/shard_map/ppermute | solution.py:412
  175.2 11.2 %collective-permute-done.9.refs_4_ = bf16[128,1024]{1,0:T(8,128)(2,1)S(1)} collective-permute-done((bf16[128,1024]{1,0:T(8,128)(2,1)S(1)}, bf16[128,1024]{1,0:T(8,128)(2,1)S(1)}, u32[]{:S(2)}, u32[]{:S(2)}) %collective-permute-start.9) | collective-permute-done | bytes 262176 | tf_op jit(solution)/shard_map/ppermute | solution.py:412
  186.5 6.4 %all-to-all-start.2 = ((bf16[8,128,1024]{2,1,0:T(8,128)(2,1)}), bf16[8,128,1024]{2,1,0:T(8,128)(2,1)S(1)}, u32[]{:S(2)}, u32[]{:S(2)}) async-start(bf16[8,128,1024]{2,1,0:T(8,128)(2,1)} %copy-done.3), calls=%async_computation.2 | async-start | bytes 4194304 | tf_op jit(solution)/shard_map/all_to_all | solution.py:409
  192.9 1.2 collective-permute-start.11
  194.1 0.3 collective-permute-start.12
  194.4 1.2 collective-permute-start.13
  195.5 1.2 collective-permute-start.14
  196.7 1.2 collective-permute-start.15
  197.9 33.7 %all-to-all-done.2.part_ref = bf16[8,128,1024]{2,1,0:T(8,128)(2,1)S(1)} async-done(((bf16[8,128,1024]{2,1,0:T(8,128)(2,1)}), bf16[8,128,1024]{2,1,0:T(8,128)(2,1)S(1)}, u32[]{:S(2)}, u32[]{:S(2)}) %all-to-all-start.2) | async-done | bytes 2097184 | tf_op jit(solution)/shard_map/all_to_all | solution.py:409
  231.6 1.4 analysis_b.1.whole_ref
  233.0 0.0 collective-permute-done.11.refs_1_
  233.0 0.0 collective-permute-done.12.refs_2_
  233.0 0.0 collective-permute-done.13.refs_3_
  233.1 2.1 collective-permute-done.14.refs_6_
  235.1 3.4 %collective-permute-done.15.refs_7_ = bf16[128,1024]{1,0:T(8,128)(2,1)} collective-permute-done((bf16[128,1024]{1,0:T(8,128)(2,1)}, bf16[128,1024]{1,0:T(8,128)(2,1)}, u32[]{:S(2)}, u32[]{:S(2)}) %collective-permute-start.15) | collective-permute-done | bytes 262176 | tf_op jit(solution)/shard_map/ppermute | solution.py:412
  238.5 2.6 %analysis_a.1 = bf16[128,8,2048]{2,1,0:T(8,128)(2,1)} custom-call(s32[1]{0:T(128)} %bitcast.place_ref, bf16[128,8,2048]{2,1,0:T(8,128)(2,1)} %analysis_b.1.whole_ref, bf16[128,1024]{1,0:T(8,128)(2,1)S(1)} %get-tuple-element.48.refs_0_, bf16[128,1024]{1,0:T(8,128)(2,1)S(1)} %collective-permute-done.11.refs_1_, ...), custom_call_target="tpu_custom_call", output_to_operand_aliasing={{}: (1, {})} | custom-call | bytes 4194304 | tf_op jit(solution)/shard_map/analysis_a/pallas_call | solution.py:218
  (5 shorter events, 0.0 us)
Async XLA Ops:
  2.5 118.9 %all-to-all-start = ((bf16[8,128,1024]{2,1,0:T(8,128)(2,1)}), bf16[8,128,1024]{2,1,0:T(8,128)(2,1)S(1)}, u32[]{:S(2)}, u32[]{:S(2)}) async-start(bf16[8,128,1024]{2,1,0:T(8,128)(2,1)} %state_a.1), calls=%async_computation | async-start | bytes 4194304 | tf_op jit(solution)/shard_map/all_to_all | solution.py:409
  8.2 38.7 %copy-start.8 = (s32[1,8,1024]{2,1,0:T(8,128)S(1)}, s32[1,8,1024]{2,1,0:T(8,128)}, u32[]{:S(2)}) copy-start(s32[1,8,1024]{2,1,0:T(8,128)} %param.9) | copy-start | bytes 98308
  12.0 30.3 %collective-permute-start = (bf16[8,144,1024]{2,1,0:T(8,128)(2,1)}, bf16[8,144,1024]{2,1,0:T(8,128)(2,1)}, u32[]{:S(2)}, u32[]{:S(2)}) collective-permute-start(bf16[8,144,1024]{2,1,0:T(8,128)(2,1)} %pool_rows.1.own_ref), channel_id=1, source_target_pairs={{0,1},{1,2},{2,3},{4,5},{5,6},{6,7},{8,9},{9,10},{10,11},{12,13},{... | collective-permute-start | bytes 7077896 | tf_op jit(solution)/shard_map/ppermute | solution.py:421
  16.2 30.7 %collective-permute-start.1 = (bf16[8,144,1024]{2,1,0:T(8,128)(2,1)}, bf16[8,144,1024]{2,1,0:T(8,128)(2,1)}, u32[]{:S(2)}, u32[]{:S(2)}) collective-permute-start(bf16[8,144,1024]{2,1,0:T(8,128)(2,1)} %pool_rows.1.own_ref), channel_id=1, source_target_pairs={{1,0},{2,1},{3,2},{5,4},{6,5},{7,6},{9,8},{10,9},{11,10},{13,12},{... | collective-permute-start | bytes 7077896 | tf_op jit(solution)/shard_map/ppermute | solution.py:422
  46.9 1.7 copy-start
  71.0 9.9 %collective-permute-start.2 = (bf16[128,1024]{1,0:T(8,128)(2,1)S(1)}, bf16[128,1024]{1,0:T(8,128)(2,1)S(1)}, u32[]{:S(2)}, u32[]{:S(2)}) collective-permute-start(bf16[128,1024]{1,0:T(8,128)(2,1)S(1)} %get-tuple-element.57), channel_id=1, source_target_pairs={{0,4},{4,0},{8,12},{12,8},{16,20},{20,16},{24,28},{28,24},{1,5},{5... | collective-permute-start | bytes 786440 | tf_op jit(solution)/shard_map/ppermute | solution.py:412
  72.0 11.0 %collective-permute-start.3 = (bf16[128,1024]{1,0:T(8,128)(2,1)S(1)}, bf16[128,1024]{1,0:T(8,128)(2,1)S(1)}, u32[]{:S(2)}, u32[]{:S(2)}) collective-permute-start(bf16[128,1024]{1,0:T(8,128)(2,1)S(1)} %get-tuple-element.56), channel_id=1, source_target_pairs={{0,8},{4,12},{8,0},{12,4},{16,24},{20,28},{24,16},{28,20},{1,9},{5... | collective-permute-start | bytes 786440 | tf_op jit(solution)/shard_map/ppermute | solution.py:412
  72.3 14.2 %collective-permute-start.4 = (bf16[128,1024]{1,0:T(8,128)(2,1)}, bf16[128,1024]{1,0:T(8,128)(2,1)S(1)}, u32[]{:S(2)}, u32[]{:S(2)}) collective-permute-start(bf16[128,1024]{1,0:T(8,128)(2,1)} %get-tuple-element.55), channel_id=1, source_target_pairs={{0,12},{4,8},{8,4},{12,0},{16,28},{20,24},{24,20},{28,16},{1,13},{... | collective-permute-start | bytes 786440 | tf_op jit(solution)/shard_map/ppermute | solution.py:412
  73.7 12.9 %collective-permute-start.5 = (bf16[128,1024]{1,0:T(8,128)(2,1)}, bf16[128,1024]{1,0:T(8,128)(2,1)S(1)}, u32[]{:S(2)}, u32[]{:S(2)}) collective-permute-start(bf16[128,1024]{1,0:T(8,128)(2,1)} %get-tuple-element.54), channel_id=1, source_target_pairs={{0,16},{4,20},{8,24},{12,28},{16,0},{20,4},{24,8},{28,12},{1,17},{... | collective-permute-start | bytes 786440 | tf_op jit(solution)/shard_map/ppermute | solution.py:412
  75.6 26.8 %collective-permute-start.6 = (bf16[128,1024]{1,0:T(8,128)(2,1)}, bf16[128,1024]{1,0:T(8,128)(2,1)S(1)}, u32[]{:S(2)}, u32[]{:S(2)}) collective-permute-start(bf16[128,1024]{1,0:T(8,128)(2,1)} %get-tuple-element.53), channel_id=1, source_target_pairs={{0,20},{4,16},{8,28},{12,24},{16,4},{20,0},{24,12},{28,8},{1,21},{... | collective-permute-start | bytes 786440 | tf_op jit(solution)/shard_map/ppermute | solution.py:412
  81.0 33.1 %collective-permute-start.7 = (bf16[128,1024]{1,0:T(8,128)(2,1)}, bf16[128,1024]{1,0:T(8,128)(2,1)S(1)}, u32[]{:S(2)}, u32[]{:S(2)}) collective-permute-start(bf16[128,1024]{1,0:T(8,128)(2,1)} %get-tuple-element.52), channel_id=1, source_target_pairs={{0,24},{4,28},{8,16},{12,20},{16,8},{20,12},{24,0},{28,4},{1,25},{... | collective-permute-start | bytes 786440 | tf_op jit(solution)/shard_map/ppermute | solution.py:412
  83.0 38.3 %collective-permute-start.8 = (bf16[128,1024]{1,0:T(8,128)(2,1)}, bf16[128,1024]{1,0:T(8,128)(2,1)}, u32[]{:S(2)}, u32[]{:S(2)}) collective-permute-start(bf16[128,1024]{1,0:T(8,128)(2,1)} %get-tuple-element.51), channel_id=1, source_target_pairs={{0,28},{4,24},{8,20},{12,16},{16,12},{20,8},{24,4},{28,0},{1,29},{... | collective-permute-start | bytes 786440 | tf_op jit(solution)/shard_map/ppermute | solution.py:412
  102.3 0.7 copy-start.4
  114.0 0.7 copy-start.6
  121.4 1.4 copy-start.1
  121.4 6.3 %copy-start.9 = (f32[1,1,1024]{2,1,0:T(1,128)S(1)}, f32[1,1,1024]{2,1,0:T(1,128)}, u32[]{:S(2)}) copy-start(f32[1,1,1024]{2,1,0:T(1,128)} %param.11) | copy-start | bytes 12292
  122.7 36.3 %all-to-all-start.1 = ((bf16[8,128,1024]{2,1,0:T(8,128)(2,1)}), bf16[8,128,1024]{2,1,0:T(8,128)(2,1)}, u32[]{:S(2)}, u32[]{:S(2)}) async-start(bf16[8,128,1024]{2,1,0:T(8,128)(2,1)} %state_b.1), calls=%async_computation.1 | async-start | bytes 4194304 | tf_op jit(solution)/shard_map/all_to_all | solution.py:409
  127.7 1.0 copy-start.5
  128.6 0.9 copy-start.7
  129.6 18.1 %copy-start.2 = (bf16[8,128,1024]{2,1,0:T(8,128)(2,1)S(1)}, bf16[8,128,1024]{2,1,0:T(8,128)(2,1)}, u32[]{:S(2)}) copy-start(bf16[8,128,1024]{2,1,0:T(8,128)(2,1)} %copy-done.1) | copy-start | bytes 6291460
  157.0 18.2 %collective-permute-start.10 = (bf16[128,1024]{1,0:T(8,128)(2,1)S(1)}, bf16[128,1024]{1,0:T(8,128)(2,1)S(1)}, u32[]{:S(2)}, u32[]{:S(2)}) collective-permute-start(bf16[128,1024]{1,0:T(8,128)(2,1)S(1)} %get-tuple-element.49), channel_id=1, source_target_pairs={{0,20},{4,16},{8,28},{12,24},{16,4},{20,0},{24,12},{28,8},{1,21},{... | collective-permute-start | bytes 786440 | tf_op jit(solution)/shard_map/ppermute | solution.py:412
  158.8 27.7 %collective-permute-start.9 = (bf16[128,1024]{1,0:T(8,128)(2,1)S(1)}, bf16[128,1024]{1,0:T(8,128)(2,1)S(1)}, u32[]{:S(2)}, u32[]{:S(2)}) collective-permute-start(bf16[128,1024]{1,0:T(8,128)(2,1)S(1)} %get-tuple-element.50), channel_id=1, source_target_pairs={{0,16},{4,20},{8,24},{12,28},{16,0},{20,4},{24,8},{28,12},{1,17},{... | collective-permute-start | bytes 786440 | tf_op jit(solution)/shard_map/ppermute | solution.py:412
  163.4 1.3 copy-start.3
  186.5 45.1 %all-to-all-start.2 = ((bf16[8,128,1024]{2,1,0:T(8,128)(2,1)}), bf16[8,128,1024]{2,1,0:T(8,128)(2,1)S(1)}, u32[]{:S(2)}, u32[]{:S(2)}) async-start(bf16[8,128,1024]{2,1,0:T(8,128)(2,1)} %copy-done.3), calls=%async_computation.2 | async-start | bytes 4194304 | tf_op jit(solution)/shard_map/all_to_all | solution.py:409
  192.9 40.1 %collective-permute-start.11 = (bf16[128,1024]{1,0:T(8,128)(2,1)}, bf16[128,1024]{1,0:T(8,128)(2,1)S(1)}, u32[]{:S(2)}, u32[]{:S(2)}) collective-permute-start(bf16[128,1024]{1,0:T(8,128)(2,1)} %get-tuple-element.47), channel_id=1, source_target_pairs={{0,4},{4,0},{8,12},{12,8},{16,20},{20,16},{24,28},{28,24},{1,5},{5... | collective-permute-start | bytes 786440 | tf_op jit(solution)/shard_map/ppermute | solution.py:412
  194.1 39.0 %collective-permute-start.12 = (bf16[128,1024]{1,0:T(8,128)(2,1)}, bf16[128,1024]{1,0:T(8,128)(2,1)S(1)}, u32[]{:S(2)}, u32[]{:S(2)}) collective-permute-start(bf16[128,1024]{1,0:T(8,128)(2,1)} %get-tuple-element.46), channel_id=1, source_target_pairs={{0,8},{4,12},{8,0},{12,4},{16,24},{20,28},{24,16},{28,20},{1,9},{5... | collective-permute-start | bytes 786440 | tf_op jit(solution)/shard_map/ppermute | solution.py:412
  194.4 38.7 %collective-permute-start.13 = (bf16[128,1024]{1,0:T(8,128)(2,1)}, bf16[128,1024]{1,0:T(8,128)(2,1)}, u32[]{:S(2)}, u32[]{:S(2)}) collective-permute-start(bf16[128,1024]{1,0:T(8,128)(2,1)} %get-tuple-element.45), channel_id=1, source_target_pairs={{0,12},{4,8},{8,4},{12,0},{16,28},{20,24},{24,20},{28,16},{1,13},{... | collective-permute-start | bytes 786440 | tf_op jit(solution)/shard_map/ppermute | solution.py:412
  195.5 39.6 %collective-permute-start.14 = (bf16[128,1024]{1,0:T(8,128)(2,1)}, bf16[128,1024]{1,0:T(8,128)(2,1)}, u32[]{:S(2)}, u32[]{:S(2)}) collective-permute-start(bf16[128,1024]{1,0:T(8,128)(2,1)} %get-tuple-element.44), channel_id=1, source_target_pairs={{0,24},{4,28},{8,16},{12,20},{16,8},{20,12},{24,0},{28,4},{1,25},{... | collective-permute-start | bytes 786440 | tf_op jit(solution)/shard_map/ppermute | solution.py:412
  196.7 41.8 %collective-permute-start.15 = (bf16[128,1024]{1,0:T(8,128)(2,1)}, bf16[128,1024]{1,0:T(8,128)(2,1)}, u32[]{:S(2)}, u32[]{:S(2)}) collective-permute-start(bf16[128,1024]{1,0:T(8,128)(2,1)} %get-tuple-element.43), channel_id=1, source_target_pairs={{0,28},{4,24},{8,20},{12,16},{16,12},{20,8},{24,4},{28,0},{1,29},{... | collective-permute-start | bytes 786440 | tf_op jit(solution)/shard_map/ppermute | solution.py:412
